TPU v7x, 32 devices: a whole 2x2x4 slice. The times are simulated.
32 devices in a mesh: fsdp: 32 (over z, y, x, core).
Axes of the slice: x: 2, y: 2, z: 4, core: 2. Of those that a mesh axis runs over, the one named last changes fastest.
Arguments:
- tokens: bfloat16 [65536, 768], P('fsdp'), may hold values from -6 to 6
- qkv_weight: bfloat16 [1769472], P('fsdp'), may hold values from -0.21875 to 0.21875
- out_weight: bfloat16 [589824], P('fsdp'), may hold values from -1.75 to 1.75
- in_weight: bfloat16 [1769472], P('fsdp'), may hold values from -0.21875 to 0.21875
- mlp_weight: bfloat16 [884736], P('fsdp'), may hold values from -0.375 to 0.375
- norm_gains: bfloat16 [1536], P('fsdp'), may hold values from 0.5 to 1.5
- cotangent: bfloat16 [65536, 768], P('fsdp'), may hold values from -6 to 6
Outputs:
- mixed_output: bfloat16 [65536, 768], P('fsdp')
- tokens_grad: float32 [65536, 768], P('fsdp')
- qkv_weight_grad: float32 [1769472], P('fsdp')
- out_weight_grad: float32 [589824], P('fsdp')
- in_weight_grad: float32 [1769472], P('fsdp')
- mlp_weight_grad: float32 [884736], P('fsdp')
- norm_gains_grad: float32 [1536], P('fsdp')
All inputs are finite; a program needn't handle non-finite values.
Results may differ from a plain program's by a relative error of at most 0.014.
Values may be sent and summed in bfloat16 or wider, within the bound.
No kernel may reach another device: no remote copies, remote signals or barrier semaphores. Data moves between devices by JAX's collectives and lax.ppermute only.
A program may use at most 256 MiB of HBM per device.

v0:
```python
import jax
import jax.numpy as jnp
from jax import lax
from jax.sharding import PartitionSpec as P

D = 768
HEADS = 12
HEAD = 64
FF = 1152
WIN = 128
LEN = 512


def layer_norm(values, gain):
    centered = values - jnp.mean(values, axis=-1, keepdims=True)
    spread = jnp.mean(centered * centered, axis=-1, keepdims=True)
    return centered * lax.rsqrt(spread + 1e-05) * gain


def rope_tables(length, head_size):
    inverse = 10000.0 ** (-jnp.arange(0, head_size, 2, dtype=jnp.float32) / head_size)
    angles = jnp.arange(length, dtype=jnp.float32)[:, None] * inverse[None, :]
    angles = jnp.concatenate([angles, angles], axis=-1)
    return (jnp.cos(angles)[:, None, :], jnp.sin(angles)[:, None, :])


def rotate(values, cosine_table, sine_table):
    midpoint = values.shape[-1] // 2
    turned = jnp.concatenate([-values[..., midpoint:], values[..., :midpoint]], axis=-1)
    return values * cosine_table + turned * sine_table


def gated_unit(joined):
    return jax.nn.gelu(joined[..., :FF], approximate=False) * joined[..., FF:]


def contract_rows(left_side, right_side):
    return lax.dot_general(
        left_side, right_side, (((0,), (0,)), ((), ())), preferred_element_type=jnp.float32
    )


def times_transposed(left_side, right_side):
    return lax.dot_general(
        left_side, right_side, (((1,), (1,)), ((), ())), preferred_element_type=jnp.float32
    )


def unpack(gathered):
    flat_qkv, flat_out, flat_in, flat_mlp, gains = gathered
    gains = gains.astype(jnp.float32)
    return (
        flat_qkv.reshape(D, 3 * D),
        flat_out.reshape(D, D),
        flat_in.reshape(D, 2 * FF),
        flat_mlp.reshape(FF, D),
        gains[:D],
        gains[D:],
    )


def masked_scores(queries, key_rows):
    scores = jnp.einsum(
        "qhc,khc->hqk", queries, key_rows, preferred_element_type=jnp.float32
    ) * HEAD ** (-0.5)
    places = jnp.arange(LEN)
    band_mask = jnp.abs(places[:, None] - places[None, :]) <= WIN // 2
    return jnp.where(band_mask, scores, -1e30)


def attend(members):
    queries, key_rows, value_rows = members
    scores = masked_scores(queries, key_rows)
    highest = jnp.max(scores, axis=-1, keepdims=True)
    summed = jnp.sum(jnp.exp(scores - highest), axis=-1, keepdims=True)
    log_total = highest + jnp.log(summed)
    attention_probs = jnp.exp(scores - log_total).astype(jnp.bfloat16)
    mixed_rows = jnp.einsum(
        "hqk,khc->qhc", attention_probs, value_rows, preferred_element_type=jnp.float32
    )
    return (mixed_rows.reshape(LEN, D), log_total[..., 0])


def attend_back(members):
    queries, key_rows, value_rows, log_total, grad_mix = members
    scores = masked_scores(queries, key_rows)
    soft = jnp.exp(scores - log_total[..., None])
    grad_soft = jnp.einsum("qhc,khc->hqk", grad_mix, value_rows, preferred_element_type=jnp.float32)
    inner_sum = jnp.sum(soft * grad_soft, axis=-1, keepdims=True)
    grad_scores = (soft * (grad_soft - inner_sum)).astype(jnp.bfloat16)
    grad_values = jnp.einsum(
        "hqk,qhc->khc", soft.astype(jnp.bfloat16), grad_mix, preferred_element_type=jnp.float32
    )
    grad_queries = jnp.einsum(
        "hqk,khc->qhc", grad_scores, key_rows, preferred_element_type=jnp.float32
    ) * HEAD ** (-0.5)
    grad_keys = jnp.einsum(
        "hqk,qhc->khc", grad_scores, queries, preferred_element_type=jnp.float32
    ) * HEAD ** (-0.5)
    return (grad_queries, grad_keys, grad_values)


def shards(tokens, qkv_weight, out_weight, in_weight, mlp_weight, norm_gains, cotangent):
    gathered = (
        lax.all_gather(qkv_weight, "fsdp", axis=0, tiled=True),
        lax.all_gather(out_weight, "fsdp", axis=0, tiled=True),
        lax.all_gather(in_weight, "fsdp", axis=0, tiled=True),
        lax.all_gather(mlp_weight, "fsdp", axis=0, tiled=True),
        lax.all_gather(norm_gains, "fsdp", axis=0, tiled=True),
    )
    w_qkv, w_out, w_in, w_mlp, gain_attn, gain_mlp = unpack(gathered)
    sequences = tokens.shape[0] // LEN
    inputs = tokens.astype(jnp.float32)
    normed_attn = layer_norm(inputs, gain_attn).astype(jnp.bfloat16)
    projected = jnp.dot(normed_attn, w_qkv, preferred_element_type=jnp.float32)
    projected = projected.reshape(sequences, LEN, 3, HEADS, HEAD)
    cosine_table, sine_table = rope_tables(LEN, HEAD)
    queries = rotate(projected[:, :, 0], cosine_table, sine_table).astype(jnp.bfloat16)
    key_rows = rotate(projected[:, :, 1], cosine_table, sine_table).astype(jnp.bfloat16)
    value_rows = projected[:, :, 2].astype(jnp.bfloat16)
    mixed_rows, log_totals = lax.map(attend, (queries, key_rows, value_rows))
    mixed_rows = mixed_rows.reshape(-1, D).astype(jnp.bfloat16)
    hidden = inputs + jnp.dot(mixed_rows, w_out, preferred_element_type=jnp.float32)
    normed_mlp = layer_norm(hidden, gain_mlp).astype(jnp.bfloat16)
    joined = jnp.dot(normed_mlp, w_in, preferred_element_type=jnp.float32)
    gated_rows = gated_unit(joined).astype(jnp.bfloat16)
    output = hidden + jnp.dot(gated_rows, w_mlp, preferred_element_type=jnp.float32)
    w_qkv, w_out, w_in, w_mlp, gain_attn, gain_mlp = unpack(
        (
            lax.all_gather(qkv_weight, "fsdp", axis=0, tiled=True),
            lax.all_gather(out_weight, "fsdp", axis=0, tiled=True),
            lax.all_gather(in_weight, "fsdp", axis=0, tiled=True),
            lax.all_gather(mlp_weight, "fsdp", axis=0, tiled=True),
            lax.all_gather(norm_gains, "fsdp", axis=0, tiled=True),
        )
    )
    grad_output = cotangent.astype(jnp.float32)
    mlp_weight_grad = contract_rows(gated_rows, cotangent)
    grad_gated = times_transposed(cotangent, w_mlp)
    _, pull_gate = jax.vjp(gated_unit, joined)
    grad_joined = pull_gate(grad_gated)[0].astype(jnp.bfloat16)
    in_weight_grad = contract_rows(normed_mlp, grad_joined)
    grad_normed_mlp = times_transposed(grad_joined, w_in)
    _, pull_second = jax.vjp(layer_norm, hidden, gain_mlp)
    grad_from_norm, gain_mlp_grad = pull_second(grad_normed_mlp)
    grad_hidden = grad_output + grad_from_norm
    grad_mix_out = grad_hidden.astype(jnp.bfloat16)
    out_weight_grad = contract_rows(mixed_rows, grad_mix_out)
    grad_mix = times_transposed(grad_mix_out, w_out).astype(jnp.bfloat16)
    grad_mix = grad_mix.reshape(sequences, LEN, HEADS, HEAD)
    grad_queries, grad_keys, grad_values = lax.map(
        attend_back, (queries, key_rows, value_rows, log_totals, grad_mix)
    )
    grad_queries = rotate(grad_queries, cosine_table, -sine_table)
    grad_keys = rotate(grad_keys, cosine_table, -sine_table)
    grad_projected = (
        jnp.stack([grad_queries, grad_keys, grad_values], axis=2)
        .reshape(-1, 3 * D)
        .astype(jnp.bfloat16)
    )
    qkv_weight_grad = contract_rows(normed_attn, grad_projected)
    grad_normed_attn = times_transposed(grad_projected, w_qkv)
    _, pull_first = jax.vjp(layer_norm, inputs, gain_attn)
    grad_from_first, gain_attn_grad = pull_first(grad_normed_attn)
    tokens_grad = grad_hidden + grad_from_first
    gains_grad = jnp.concatenate([gain_attn_grad, gain_mlp_grad], axis=0)
    qkv_share, out_share, in_share, mlp_share, gains_share = (
        lax.psum_scatter(qkv_weight_grad.reshape(-1), "fsdp", scatter_dimension=0, tiled=True),
        lax.psum_scatter(out_weight_grad.reshape(-1), "fsdp", scatter_dimension=0, tiled=True),
        lax.psum_scatter(in_weight_grad.reshape(-1), "fsdp", scatter_dimension=0, tiled=True),
        lax.psum_scatter(mlp_weight_grad.reshape(-1), "fsdp", scatter_dimension=0, tiled=True),
        lax.psum_scatter(gains_grad, "fsdp", scatter_dimension=0, tiled=True),
    )
    return (
        output.astype(jnp.bfloat16),
        tokens_grad,
        qkv_share,
        out_share,
        in_share,
        mlp_share,
        gains_share,
    )


def solution(mesh):
    placed = (
        P("fsdp", None),
        P("fsdp"),
        P("fsdp"),
        P("fsdp"),
        P("fsdp"),
        P("fsdp"),
        P("fsdp", None),
    )
    return jax.shard_map(
        shards,
        mesh=mesh,
        in_specs=placed,
        out_specs=(
            P("fsdp", None),
            P("fsdp", None),
            P("fsdp"),
            P("fsdp"),
            P("fsdp"),
            P("fsdp"),
            P("fsdp"),
        ),
        check_vma=False,
    )
```

profile of v0, /device:TPU:0, one launch (start us, length us, event | category | flops | bytes accessed | tf_op | source)
XLA Modules:
  0.0 993.8 jit_solution(14518751320647151101)
XLA Ops:
  11.0 42.0 %all-reduce.2 = bf16[1536]{0:T(1024)(128)(2,1)S(1)} all-reduce(bf16[1536]{0:T(1024)(128)(2,1)S(1)} %dynamic-update-slice), channel_id=1, replica_groups=mesh['fsdp'=32] {'fsdp'}, use_global_device_ids=true, to_apply=%add.2 | all-reduce | flops 1536 | bytes 6144
  59.8 4.8 copy.52
  75.4 49.8 %all-gather.11.cloned.1.call-done = bf16[884736]{0:T(1024)(128)(2,1)} async-done(((bf16[27648]{0:T(1024)(128)(2,1)}), bf16[884736]{0:T(1024)(128)(2,1)}) %all-gather.11.cloned.1.call-update) | async-done | bytes 1769488 | tf_op jit(solution)/shard_map/all_gather | solution.py:108
  129.3 57.7 %all-gather.5.cloned.1.call-done = bf16[1769472]{0:T(1024)(128)(2,1)} async-done(((bf16[55296]{0:T(1024)(128)(2,1)}), bf16[1769472]{0:T(1024)(128)(2,1)}) %all-gather.5.cloned.1.call-update) | async-done | bytes 3538960 | tf_op jit(solution)/shard_map/all_gather | solution.py:105
  187.0 7.6 reshape.208
  194.6 5.9 copy.47
  200.6 10.8 %fusion.86 = f32[4,512,3,12,64]{1,4,3,2,0:T(8,128)S(1)} fusion(bf16[4,512,768,1,1]{2,1,4,3,0:T(8,128)(2,1)} %bitcast.157, bf16[3,12,64,768,1]{3,2,1,0,4:T(8,128)(2,1)} %bitcast.155), kind=kOutput, calls=%fused_computation.147 | convolution fusion | flops 7247757312 | bytes 25559040 | tf_op jit(solution)/shard_map/dot_general | solution.py:115
  211.4 6.4 copy-done.4
  220.0 12.2 %slice_bitcast_fusion = (f32[4,512,12,64]{1,3,2,0:T(8,128)}, f32[4,512,12,64]{1,3,2,0:T(8,128)}) fusion(f32[4,512,3,12,64]{1,4,3,2,0:T(8,128)} %copy-done.4), kind=kLoop, calls=%fused_computation.91 | loop fusion | bytes 25165824 | tf_op jit(solution)/shard_map/squeeze | solution.py:119
  232.2 9.7 slice_negate_fusion
  241.9 12.3 %fusion.63 = (bf16[4,512,12,64]{1,3,2,0:T(8,128)(2,1)}, bf16[4,512,12,64]{1,3,2,0:T(8,128)(2,1)}) fusion(f32[4,512,12,32]{1,3,2,0:T(8,128)} %get-tuple-element.201, f32[4,512,12,32]{1,3,2,0:T(8,128)S(1)} %get-tuple-element.200, f32[512,64]{0,1:T(8,128)S(1)} %get-tuple-element.207, f32[512,64]{0,1:T(8,128)S(1)} %get-tuple-element.208, ...), kind=kLoop, calls=%fused_computation.99 | loop fusion | flops 15728640 | bytes 31719424 | tf_op jit(solution)/shard_map/convert_element_type | solution.py:119
  254.2 65.3 %while.26 = (s32[]{:T(128)}, bf16[4,512,768]{2,1,0:T(8,128)(2,1)}, f32[4,12,512]{2,1,0:T(8,128)}, bf16[4,512,12,64]{1,3,2,0:T(8,128)(2,1)}, bf16[4,512,12,64]{1,...) while((s32[]{:T(128)}, bf16[4,512,768]{2,1,0:T(8,128)(2,1)}, f32[4,12,512]{2,1,0:T(8,128)}, ...), condition=%wide.region_5.6_spmd, body=%wide.region_2.5_spmd.sunk | while | flops 840689664 | bytes 45294688 | solution.py:121
  261.4 5.1 fusion.126
  277.6 5.1 fusion.126
  293.8 5.1 fusion.126
  310.0 5.1 fusion.126
  319.5 5.2 fusion.85
  328.7 6.3 reshape.210
  335.1 10.5 %fusion.81 = f32[2048,2304]{1,0:T(8,128)S(1)} fusion(bf16[768,2304]{1,0:T(8,128)(2,1)S(1)} %reshape.210, f32[2048,768]{0,1:T(8,128)} %copy-done.7, f32[768]{0:T(1024)} %get-tuple-element.209, f32[2048]{0:T(1024)S(1)} %fusion.77, f32[2048]{0:T(1024)S(1)} %broadcast_multiply_fusion), kind=kOutput, calls=%fused_computation.143 | convolution fusion | flops 7254048768 | bytes 28724224 | tf_op jit(solution)/shard_map/dot_general | solution.py:125
  345.5 27.2 %fusion.70 = (f32[2048,1152]{1,0:T(8,128)}, f32[2048,1152]{1,0:T(8,128)}, f32[2048,1152]{1,0:T(8,128)}) fusion(f32[2048,2304]{1,0:T(8,128)S(1)} %fusion.81, bf16[2048,768]{1,0:T(8,128)(2,1)S(1)} %copy-done.13, bf16[1152,768]{1,0:T(8,128)(2,1)} %reshape.211), kind=kOutput, calls=%fused_computation.120 | convolution fusion | flops 3777232896 | bytes 42663936 | tf_op jit(solution)/shard_map/dot_general | solution.py:44
  372.8 14.6 %multiply_add_fusion = (f32[2048,1152]{1,0:T(8,128)}, bf16[2048,1152]{1,0:T(8,128)(2,1)}) fusion(f32[2048,1152]{1,0:T(8,128)} %get-tuple-element.185, f32[2048,1152]{1,0:T(8,128)} %get-tuple-element.213, f32[2048,2304]{1,0:T(8,128)S(1)} %fusion.81), kind=kLoop, calls=%fused_computation.68 | loop fusion | flops 40108032 | bytes 51904512 | tf_op jit(solution)/shard_map/transpose(jvp())/add_any | solution.py:34
  387.4 15.4 %multiply_reduce_fusion.1 = (f32[768]{0:T(1024)}, f32[2048]{0:T(1024)}, f32[2048,768]{0,1:T(8,128)}) fusion(f32[2048,768]{0,1:T(8,128)} %copy-done.7, f32[2048]{0:T(1024)S(1)} %fusion.77, f32[2048]{0:T(1024)S(1)} %broadcast_multiply_fusion, f32[768]{0:T(1024)S(1)} %copy-done.31, bf16[768,2304]{1,0:T(8,128)(2,1)S(1)} %reshape.210, ...), kind=kOutput, calls=%fused_computation.106 | convolution fusion | flops 7268201472 | bytes 35026944 | tf_op jit(solution)/shard_map/dot_general | solution.py:44
  402.8 18.6 %fusion.71 = f32[768,2304]{1,0:T(8,128)} fusion(f32[2048,1152]{1,0:T(8,128)} %get-tuple-element.190, f32[2048,1152]{1,0:T(8,128)} %get-tuple-element.184, f32[2048,768]{0,1:T(8,128)} %copy-done.7, f32[768]{0:T(1024)} %get-tuple-element.209, f32[2048]{0:T(1024)S(1)} %fusion.77, f32[2048]{0:T(1024)S(1)} %broadcast_multiply_fusion), kind=kOutput, calls=%fused_computation.121 | convolution fusion | flops 7263485952 | bytes 32263168 | tf_op jit(solution)/shard_map/dot_general | solution.py:38
  421.4 6.2 fusion.82
  445.9 7.9 reshape.215
  468.6 117.7 %while.27 = (s32[]{:T(128)}, f32[4,512,12,64]{1,3,2,0:T(8,128)}, f32[4,512,12,64]{1,3,2,0:T(8,128)}, bf16[4,512,12,64]{1,3,2,0:T(8,128)(2,1)}, bf16[4,512,12,64]...) while((s32[]{:T(128)}, f32[4,512,12,64]{1,3,2,0:T(8,128)}, ...), condition=%wide.region_12.13_spmd, body=%wide.region_10.12_spmd.sunk | while | flops 2062018560 | bytes 143586496 | solution.py:151
  476.0 8.5 multiply_reduce_fusion.5
  484.5 7.0 multiply_convert_fusion.6
  505.4 8.5 multiply_reduce_fusion.5
  514.0 7.0 multiply_convert_fusion.6
  534.8 8.5 multiply_reduce_fusion.5
  543.3 7.0 multiply_convert_fusion.6
  564.1 8.5 multiply_reduce_fusion.5
  572.6 7.0 multiply_convert_fusion.6
  586.3 7.1 slice_negate_fusion.3
  596.9 8.5 fusion.65
  605.4 8.4 maximum_convert_fusion
  613.8 12.2 %copy.55 = bf16[4,512,3,12,64]{1,0,4,3,2:T(4,128)(2,1)} copy(bf16[4,512,3,12,64]{1,4,3,0,2:T(8,128)(2,1)} %maximum_convert_fusion) | data formatting | bytes 18874368 | tf_op jit(solution)/shard_map/convert_element_type | solution.py:159
  626.0 11.6 %copy.80 = bf16[288,8,4,512]{3,1,2,0:T(8,128)(2,1)} copy(bf16[288,8,4,512]{3,2,1,0:T(4,128)(2,1)} %bitcast.146) | data formatting | bytes 18874368
  637.6 12.7 %fusion.87 = f32[768,2304]{1,0:T(8,128)} fusion(bf16[2048,768]{0,1:T(8,128)(2,1)S(1)} %copy-done.10, bf16[2048,2304]{0,1:T(8,128)(2,1)} %bitcast.151), kind=kOutput, calls=%fused_computation.148 | convolution fusion | flops 7247757312 | bytes 19660800 | tf_op jit(solution)/shard_map/dot_general | solution.py:38
  650.3 8.2 reshape.213
  658.5 10.7 %add_convert_fusion.1 = bf16[2048,768]{0,1:T(8,128)(2,1)} fusion(f32[2048,768]{0,1:T(8,128)} %copy-done.7, bf16[2048,1152]{1,0:T(8,128)(2,1)} %get-tuple-element.191, bf16[1152,768]{1,0:T(8,128)(2,1)} %reshape.211), kind=kOutput, calls=%fused_computation.110 | convolution fusion | flops 3627024384 | bytes 15925248 | tf_op jit(solution)/shard_map/dot_general | solution.py:127
  669.3 4.7 copy.56
  674.0 11.4 %fusion.59 = (f32[2048]{0:T(1024)S(1)}, f32[2048,768]{0,1:T(8,128)S(1)}) fusion(bf16[2048,768]{0,1:T(8,128)(2,1)S(1)} %copy-done.1, f32[768]{0:T(1024)S(1)} %copy-done.30, f32[2048]{0:T(1024)S(1)} %copy-done.20, bf16[768,2304]{1,0:T(8,128)(2,1)} %reshape.208, bf16[2048,2304]{0,1:T(8,128)(2,1)} %bitcast.152), kind=kOutput, calls=%fused_computation.90 | convolution fusion | flops 7255619584 | bytes 22432768 | tf_op jit(solution)/shard_map/dot_general | solution.py:44
  688.6 6.7 add_add_fusion.2
  695.3 6.6 copy.57
  701.9 40.5 %all-reduce.7 = f32[1536]{0:T(1024)S(1)} all-reduce(f32[1536]{0:T(1024)S(1)} %pad_maximum_fusion.1), channel_id=6, replica_groups=mesh['fsdp'=32] {'fsdp'}, use_global_device_ids=true, to_apply=%region_21.22.clone | all-reduce | flops 1536 | bytes 12288
  743.0 237.4 %all-reduce.11.cloned.1.call-done = (f32[1769472]{0:T(1024)}, f32[589824]{0:T(1024)}, f32[1769472]{0:T(1024)}, f32[884736]{0:T(1024)}) async-done(((f32[1769472]{0:T(1024)}, f32[589824]{0:T(1024)}, f32[1769472]{0:T(1024)}, f32[884736]{0:T(1024)}), (f32[1769472]{0:T(1024)}, f32[589824]{0:T(1024)}, f32[1769472]{0:T(1024)}, f32[884736]{0:T(1024)})) %all-reduce.11.cloned.1.call-update) | async-done | bytes 20054032
  (204 shorter events, 177.9 us)
Async XLA Ops:
  7.2 64.8 %all-gather.7.cloned.1.call-start = ((), (), s32[]{:S(2)}) async-start(), calls=%async_computation.1 | async-start | bytes 1216512 | tf_op jit(solution)/shard_map/all_gather | solution.py:106
  7.9 117.2 %all-gather.11.cloned.1.call-start = ((), (), s32[]{:S(2)}) async-start(), calls=%async_computation.3 | async-start | bytes 1824768 | tf_op jit(solution)/shard_map/all_gather | solution.py:108
  8.6 178.3 %all-gather.5.cloned.1.call-start = ((), (), s32[]{:S(2)}) async-start(), calls=%async_computation | async-start | bytes 3649536 | tf_op jit(solution)/shard_map/all_gather | solution.py:105
  9.4 319.3 %all-gather.9.cloned.1.call-start = ((), (), s32[]{:S(2)}) async-start(), calls=%async_computation.2 | async-start | bytes 3649536 | tf_op jit(solution)/shard_map/all_gather | solution.py:107
  10.0 970.5 %all-reduce.11.cloned.1.call-start = ((), (), s32[]{:S(2)}) async-start(), calls=%async_computation.4 | async-start | bytes 40108032
  53.6 11.0 %copy-start.29 = (f32[768]{0:T(1024)}, f32[768]{0:T(1024)S(1)}, u32[]{:S(2)}) copy-start(f32[768]{0:T(1024)S(1)} %get-tuple-element.210) | copy-start | bytes 9220
  54.6 187.3 %copy-start.15 = (f32[512,64]{0,1:T(8,128)}, f32[512,64]{0,1:T(8,128)S(1)}, u32[]{:S(2)}) copy-start(f32[512,64]{0,1:T(8,128)S(1)} %get-tuple-element.208) | copy-start | bytes 393220
  57.8 261.7 %copy-start = (bf16[2048,768]{0,1:T(8,128)(2,1)}, bf16[2048,768]{0,1:T(8,128)(2,1)S(1)}, u32[]{:S(2)}) copy-start(bf16[2048,768]{0,1:T(8,128)(2,1)S(1)} %copy.46) | copy-start | bytes 9437188
  58.3 9.0 copy-start.19
  59.8 7.5 copy-start.21
  211.4 6.4 copy-start.4
  335.1 10.5 %copy-start.13 = (bf16[2048,768]{1,0:T(8,128)(2,1)S(1)}, bf16[2048,768]{1,0:T(8,128)(2,1)}, u32[]{:S(2)}) copy-start(bf16[2048,768]{1,0:T(8,128)(2,1)} %param.17) | copy-start | bytes 9437188
  372.8 14.6 %copy-start.31 = (f32[768]{0:T(1024)S(1)}, f32[768]{0:T(1024)}, u32[]{:S(2)}) copy-start(f32[768]{0:T(1024)} %get-tuple-element.209) | copy-start | bytes 9220
  402.8 18.6 %copy-start.28 = (f32[2048]{0:T(1024)S(1)}, f32[2048]{0:T(1024)}, u32[]{:S(2)}) copy-start(f32[2048]{0:T(1024)} %copy-done.27) | copy-start | bytes 24580
  402.8 18.6 %copy-start.33 = (f32[2048]{0:T(1024)S(1)}, f32[2048]{0:T(1024)}, u32[]{:S(2)}) copy-start(f32[2048]{0:T(1024)} %get-tuple-element.143) | copy-start | bytes 24580
  402.8 18.6 %copy-start.32 = (f32[768]{0:T(1024)S(1)}, f32[768]{0:T(1024)}, u32[]{:S(2)}) copy-start(f32[768]{0:T(1024)} %get-tuple-element.209) | copy-start | bytes 9220
  421.4 6.2 copy-start.5
  427.6 3.2 copy-start.3
  427.6 3.2 copy-start.23
  427.6 4.1 copy-start.35
  431.8 4.1 copy-start.17
  431.8 8.2 slice-start.2
  435.9 4.1 slice-start.3
  435.9 4.1 copy-start.14
  460.9 7.6 copy-start.2
  469.7 3.1 copy-start.9
  469.7 3.1 copy-start.11
  476.0 8.6 copy-start.12
  499.1 3.1 copy-start.9
  499.1 3.1 copy-start.11
  505.4 8.6 copy-start.12
  528.4 3.1 copy-start.9
  534.7 8.6 copy-start.12
  564.1 8.6 copy-start.12
  586.3 7.1 copy-start.8
  586.3 10.6 %slice-start = ((s8[6291456]{0:T(1024)(128)(4,1)}), s8[4194304]{0:T(1024)(128)(4,1)S(1)}, s32[]{:S(2)}) async-start(s8[6291456]{0:T(1024)(128)(4,1)} %bitcast.147), calls=%async_computation.5 | async-start | bytes 8388608
  593.4 3.5 slice-start.1
  593.4 3.5 copy-start.16
  593.4 3.5 copy-start.18
  626.0 11.6 %copy-start.10 = (bf16[2048,768]{0,1:T(8,128)(2,1)S(1)}, bf16[2048,768]{0,1:T(8,128)(2,1)}, u32[]{:S(2)}) copy-start(bf16[2048,768]{0,1:T(8,128)(2,1)} %fusion.56) | copy-start | bytes 9437188
  658.5 15.5 %copy-start.1 = (bf16[2048,768]{0,1:T(8,128)(2,1)S(1)}, bf16[2048,768]{0,1:T(8,128)(2,1)}, u32[]{:S(2)}) copy-start(bf16[2048,768]{0,1:T(8,128)(2,1)} %copy-done) | copy-start | bytes 9437188
  658.5 15.4 %copy-start.20 = (f32[2048]{0:T(1024)S(1)}, f32[2048]{0:T(1024)}, u32[]{:S(2)}) copy-start(f32[2048]{0:T(1024)} %copy-done.19) | copy-start | bytes 24580
  658.5 15.4 %copy-start.30 = (f32[768]{0:T(1024)S(1)}, f32[768]{0:T(1024)}, u32[]{:S(2)}) copy-start(f32[768]{0:T(1024)} %copy-done.29) | copy-start | bytes 9220
  674.0 11.4 %copy-start.26 = (f32[2048]{0:T(1024)S(1)}, f32[2048]{0:T(1024)}, u32[]{:S(2)}) copy-start(f32[2048]{0:T(1024)} %copy-done.25) | copy-start | bytes 24580
  674.0 11.4 %copy-start.22 = (f32[2048]{0:T(1024)S(1)}, f32[2048]{0:T(1024)}, u32[]{:S(2)}) copy-start(f32[2048]{0:T(1024)} %copy-done.21) | copy-start | bytes 24580
  685.4 3.2 copy-start.6
  685.4 3.2 copy-start.24
  695.3 6.6 copy-start.34
  (6 other events, 13.3 us)
Sparse Core Ops, SparseCore 0:
  10.9 56.7 all-gather.6
  70.5 54.5 all-gather.10
  128.0 58.9 all-gather.4
  189.7 58.8 all-gather.8
  658.6 321.7 all-reduce.10
where the time goes:
time: 1000 us; the launch traced here: 994 us
  waiting for transfers between devices  347 us (35%)
  matrix products  254 us (25%)
  local copies, waits for them, and re-layouts  165 us (16%)
  other arithmetic  129 us (13%)
  blocking collectives  82.6 us (8%)
  between operations  14.7 us (1%)
    unnamed x6, waiting for transfers between devices  240 us
    unnamed x2, blocking collectives  82.6 us
    dot_general x4, matrix products, times_transposed(): lax.dot_general(left_side, right_side, (((1,), (1,)), ((), ())), preferre...  58.1 us
    all_gather x1, waiting for transfers between devices, shards(): lax.all_gather(qkv_weight, 'fsdp', axis=0, tiled=True)  57.7 us
    unnamed x86, local copies, waits for them, and re-layouts  51.9 us
    all_gather x1, waiting for transfers between devices, shards(): lax.all_gather(mlp_weight, 'fsdp', axis=0, tiled=True)  49.8 us
    dot_general x4, matrix products, contract_rows(): lax.dot_general(left_side, right_side, (((0,), (0,)), ((), ())), preferre...  39.3 us
    dot_general x4, matrix products, attend_back(): jnp.einsum('qhc,khc->hqk', grad_mix, value_rows, preferred_element_type=j...  34.2 us
  transfers between devices with their start and end apart: 5, of which 3 were waited for; matrix products, arithmetic and copies ran while one was open for 20% of the time, Pallas kernels for 0%

commit v1 on v0

v1 whole, which is shorter than its diff:
```python
import functools

import jax
import jax.numpy as jnp
import numpy as np
from jax import lax
from jax.experimental import pallas as pl
from jax.experimental.pallas import tpu as pltpu
from jax.sharding import PartitionSpec as P

D = 768
HEADS = 12
HEAD = 64
FF = 1152
WIN = 128
LEN = 512
PAIR = 2 * HEAD
PAIRS = HEADS // 2
BLOCK = 128
SPAN = 2 * BLOCK
BLOCKS = LEN // BLOCK
STARTS = tuple(min(max(BLOCK * i - WIN // 2, 0), LEN - SPAN) for i in range(BLOCKS))
GROUPS = ((0, 2), (2, 4))
CORE, ALONG_X, ALONG_Y, ALONG_Z = 1, 2, 4, 8
VMEM_LIMIT = 60 * 1024 * 1024
f32 = jnp.float32
bf16 = jnp.bfloat16


def dot_nn(left, right):
    return lax.dot_general(left, right, (((1,), (0,)), ((), ())), preferred_element_type=f32)


def dot_nt(left, right):
    return lax.dot_general(left, right, (((1,), (1,)), ((), ())), preferred_element_type=f32)


def dot_tn(left, right):
    return lax.dot_general(left, right, (((0,), (0,)), ((), ())), preferred_element_type=f32)


def swap(values, bits):
    return lax.ppermute(values, "fsdp", [(i, i ^ bits) for i in range(32)])


def bit_of(bits):
    return (lax.axis_index("fsdp") & bits) != 0


def ordered(bits, mine, other, axis):
    return jnp.where(
        bit_of(bits), jnp.concatenate([other, mine], axis), jnp.concatenate([mine, other], axis)
    )


def table(entries):
    return jnp.stack([jnp.stack([jnp.int32(a), jnp.int32(b)]) for a, b in entries]).astype(jnp.int32)


def split_columns(shard):
    half = shard.shape[1] // 2
    low, high = shard[:, :half], shard[:, half:]
    other = swap(jnp.where(bit_of(CORE), low, high), CORE)
    return ordered(CORE, jnp.where(bit_of(CORE), high, low), other, 0)


def gather_rows(shard, first, second):
    own = split_columns(shard)
    rows, half = own.shape
    line = jnp.stack([own] + [swap(own, ALONG_Z * j) for j in (1, 2, 3)])
    plane = jnp.concatenate([line, swap(line, first)])
    far = swap(plane, second)
    pieces = [plane, far, swap(plane, CORE), swap(far, CORE)]
    return pieces, places(rows, half, first, second, (0, 1))


def places(rows, half, first, second, sides):
    core = lax.axis_index("fsdp") & 1
    entries = []
    for side in sides:
        for beyond in (0, 1):
            for near in (0, 1):
                for j in range(4):
                    flips = (ALONG_Z * j) | (first * near) | (second * beyond)
                    chip = (lax.axis_index("fsdp") ^ flips) // 2
                    entries.append((chip * rows, (core ^ side) * half))
    return table(entries)


def gather_tall(shard):
    own = split_columns(shard)
    own = ordered(ALONG_X, own, swap(own, ALONG_X), 0)
    rows, half = own.shape
    line = jnp.stack([own] + [swap(own, ALONG_Z * j) for j in (1, 2, 3)])
    far = swap(line, ALONG_Y)
    pieces = [line, far, swap(line, CORE), swap(far, CORE)]
    return pieces, tall_places(rows, half, (0, 1))


def tall_places(rows, half, sides):
    me = lax.axis_index("fsdp")
    entries = []
    for side in sides:
        for beyond in (0, 1):
            for j in range(4):
                spot = (me ^ (ALONG_Z * j) ^ (ALONG_Y * beyond)) // 4
                entries.append((spot * rows, ((me & 1) ^ side) * half))
    return table(entries)


def gather_vector(values):
    for bits in (CORE, ALONG_X, ALONG_Y, ALONG_Z, 2 * ALONG_Z):
        values = ordered(bits, values, swap(values, bits), 0)
    return values


def scatter_vector(values):
    for bits in (2 * ALONG_Z, ALONG_Z, ALONG_Y, ALONG_X, CORE):
        half = values.shape[0] // 2
        low, high = values[:half], values[half:]
        other = swap(jnp.where(bit_of(bits), low, high), bits)
        values = jnp.where(bit_of(bits), high, low) + other
    return values


def joined_sum(kept, received):
    return (kept.astype(f32) + received.astype(f32)).astype(bf16)


def halved(kept, received):
    half = kept.shape[0] // 2
    return (
        joined_sum(kept[:half], received[:half]),
        joined_sum(kept[half:], received[half:]),
    )


def summed_line(kept, received):
    line = joined_sum(kept, received)
    total = line[0].astype(f32)
    for j in (1, 2, 3):
        total = total + swap(line[j], ALONG_Z * j).astype(f32)
    return total


def join_columns(total):
    rows = total.shape[0] // 2
    low, high = total[:rows], total[rows:]
    other = swap(jnp.where(bit_of(CORE), low, high), CORE)
    return ordered(CORE, jnp.where(bit_of(CORE), high, low), other, 1)


def scatter_rows(kept, sent, first, second):
    keep, send = halved(kept, swap(sent, CORE))
    keep, send = halved(keep, swap(send, second))
    return join_columns(summed_line(keep, swap(send, first)))


def scatter_tall(kept, sent):
    keep, send = halved(kept, swap(sent, CORE))
    total = summed_line(keep, swap(send, ALONG_Y))
    rows = total.shape[0] // 2
    low, high = total[:rows], total[rows:]
    other = swap(jnp.where(bit_of(ALONG_X), low, high).astype(bf16), ALONG_X)
    total = jnp.where(bit_of(ALONG_X), high, low) + other.astype(f32)
    return join_columns(total)


def load_pieces(places_ref, pieces, weight, sem):
    copies = []
    at = 0
    for piece in pieces:
        blocks, rows, columns = piece.shape
        for block in range(blocks):
            row = pl.multiple_of(places_ref[2 * at], 16)
            column = pl.multiple_of(places_ref[2 * at + 1], 128)
            copy = pltpu.make_async_copy(
                piece.at[block], weight.at[pl.ds(row, rows), pl.ds(column, columns)], sem
            )
            copy.start()
            copies.append(copy)
            at += 1
    return copies


def store_blocks(places_ref, total, outs):
    at = 0
    for out in outs:
        blocks, rows, columns = out.shape
        for block in range(blocks):
            row = pl.multiple_of(places_ref[2 * at], 16)
            column = pl.multiple_of(places_ref[2 * at + 1], 128)
            out[block] = total[pl.ds(row, rows), pl.ds(column, columns)].astype(bf16)
            at += 1


def turn(values, tables, sign):
    cosine, sine_up, sine_down = tables
    up = pltpu.roll(values, HEAD // 2, 1)
    down = pltpu.roll(values, PAIR - HEAD // 2, 1)
    if sign > 0:
        return values * cosine + (up * sine_up + down * sine_down)
    return values * cosine - (up * sine_up + down * sine_down)


def norm_of(values):
    centered = values - jnp.mean(values, axis=-1, keepdims=True)
    spread = jnp.mean(centered * centered, axis=-1, keepdims=True)
    scale = lax.rsqrt(spread + 1e-05)
    return centered * scale, scale


def norm_back(grad, normed, scale):
    return scale * (
        grad
        - jnp.mean(grad, axis=-1, keepdims=True)
        - normed * jnp.mean(grad * normed, axis=-1, keepdims=True)
    )


def band(block):
    key = lax.broadcasted_iota(jnp.int32, (SPAN, SPAN), 0) + STARTS[block]
    query = lax.broadcasted_iota(jnp.int32, (SPAN, SPAN), 1) % BLOCK + block * BLOCK
    return jnp.abs(key - query) <= WIN // 2


def both_heads(values, masks_ref):
    return jnp.concatenate([values * masks_ref[0:1, :], values * masks_ref[1:2, :]], axis=0)


def one_of_each(stacked):
    own = jnp.concatenate([stacked[:HEAD, :BLOCK], stacked[HEAD:, BLOCK:]], axis=0)
    return own.T


def forward_kernel(
    pairs, pieces_n, places_ref, tokens_ref, gain_ref, tables_ref, masks_ref, *refs
):
    pieces = refs[:pieces_n]
    normed_ref, qkv_ref, probs_ref, mix_ref, weight, bias, sem = refs[pieces_n:]
    first = pl.program_id(0) == 0

    @pl.when(first)
    def _():
        copies = load_pieces(places_ref, pieces, weight, sem)
        for block in range(3):
            bias[block] = jnp.where(band(block if block < 2 else BLOCKS - 1), 0.0, -1e30)
        for copy in copies:
            copy.wait()

    normed, _ = norm_of(tokens_ref[...].astype(f32))
    normed_ref[...] = (normed * gain_ref[...]).astype(bf16)
    tables = (tables_ref[0], tables_ref[1], tables_ref[2])

    def project(pair, carry):
        column = pl.multiple_of(pair * 3 * PAIR, 128)
        projected = dot_nn(normed_ref[...], weight[:, pl.ds(column, 3 * PAIR)])
        queries = turn(projected[:, :PAIR], tables, 1)
        key_rows = turn(projected[:, PAIR : 2 * PAIR], tables, 1)
        qkv_ref[:, pl.ds(column, PAIR)] = queries.astype(bf16)
        qkv_ref[:, pl.ds(column + PAIR, PAIR)] = key_rows.astype(bf16)
        qkv_ref[:, pl.ds(column + 2 * PAIR, PAIR)] = projected[:, 2 * PAIR :].astype(bf16)
        return carry

    lax.fori_loop(0, pairs, project, 0)

    def attend(pair, carry):
        column = pl.multiple_of(pair * 3 * PAIR, 128)
        out_column = pl.multiple_of(pair * PAIR, 128)
        for block in range(BLOCKS):
            rows = slice(block * BLOCK, (block + 1) * BLOCK)
            window = slice(STARTS[block], STARTS[block] + SPAN)
            queries = both_heads(qkv_ref[rows, pl.ds(column, PAIR)], masks_ref) * bf16(HEAD**-0.5)
            scores = dot_nt(qkv_ref[window, pl.ds(column + PAIR, PAIR)], queries)
            scores = scores + bias[0 if block == 0 else (2 if block == BLOCKS - 1 else 1)]
            raised = jnp.exp(scores - jnp.max(scores, axis=0, keepdims=True))
            probs = raised * (1.0 / jnp.sum(raised, axis=0, keepdims=True))
            probs = probs.astype(bf16)
            probs_ref[0, pair, block] = probs
            mixed = dot_tn(qkv_ref[window, pl.ds(column + 2 * PAIR, PAIR)], probs)
            mix_ref[rows, pl.ds(out_column, PAIR)] = one_of_each(mixed).astype(bf16)
        return carry

    lax.fori_loop(0, pairs, attend, 0)


def feed_kernel(
    groups_n,
    counts,
    *refs,
):
    refs = list(refs)
    take = lambda n: [refs.pop(0) for _ in range(n)]
    out_places, in_places, mlp_places = take(3)
    out_back, in_back, mlp_back = take(3)
    tokens_ref, cot_ref, gain_ref = take(3)
    mix_refs = take(groups_n)
    out_pieces, in_pieces, mlp_pieces = (take(n) for n in counts)
    hidden_ref, gated_ref, grad_hidden_ref = take(3)
    grad_mix_refs = take(groups_n)
    (gain_grad_ref,) = take(1)
    out_grads, in_grads, mlp_grads = (take(2 if n > 1 else 1) for n in counts)
    w_out, w_in, w_mlp, t_out, t_in, t_mlp, sems = refs
    step = pl.program_id(0)

    @pl.when(step == 0)
    def _():
        copies = load_pieces(out_places, out_pieces, w_out, sems.at[0])
        copies += load_pieces(in_places, in_pieces, w_in, sems.at[1])
        copies += load_pieces(mlp_places, mlp_pieces, w_mlp, sems.at[2])
        t_out[...] = jnp.zeros_like(t_out)
        t_in[...] = jnp.zeros_like(t_in)
        t_mlp[...] = jnp.zeros_like(t_mlp)
        gain_grad_ref[...] = jnp.zeros_like(gain_grad_ref)
        for copy in copies:
            copy.wait()

    mixed = jnp.concatenate([ref[...] for ref in mix_refs], axis=1)
    cot = cot_ref[...]
    hidden = tokens_ref[...].astype(f32) + dot_nn(mixed, w_out[...])
    hidden_ref[...] = hidden
    normed, scale = norm_of(hidden)
    gain = gain_ref[...]
    normed_mlp = (normed * gain).astype(bf16)
    grad_gated = dot_nt(cot, w_mlp[...])
    entry = dot_nn(normed_mlp, w_in[:, :FF])
    gate = dot_nn(normed_mlp, w_in[:, FF:])
    below = 0.5 * (1.0 + lax.erf(entry * 0.7071067811865476))
    density = jnp.exp(-0.5 * entry * entry) * 0.3989422804014327
    unit = entry * below
    gated = (unit * gate).astype(bf16)
    gated_ref[...] = gated
    grad_entry = ((below + entry * density) * (gate * grad_gated)).astype(bf16)
    grad_gate = (unit * grad_gated).astype(bf16)
    t_mlp[...] += dot_tn(gated, cot)
    turned = normed_mlp.T
    t_in[:, :FF] += dot_nn(turned, grad_entry)
    t_in[:, FF:] += dot_nn(turned, grad_gate)
    grad_normed = dot_nt(grad_entry, w_in[:, :FF]) + dot_nt(grad_gate, w_in[:, FF:])
    gain_grad_ref[...] += jnp.sum(grad_normed * normed, axis=0, keepdims=True)
    grad_hidden = cot.astype(f32) + norm_back(grad_normed * gain, normed, scale)
    grad_hidden_ref[...] = grad_hidden
    grad_out = grad_hidden.astype(bf16)
    t_out[...] += dot_tn(mixed, grad_out)
    column = 0
    for ref in grad_mix_refs:
        width = ref.shape[1]
        ref[...] = dot_nt(grad_out, w_out[column : column + width, :]).astype(bf16)
        column += width

    @pl.when(step == pl.num_programs(0) - 1)
    def _():
        store_blocks(out_back, t_out, out_grads)
        store_blocks(in_back, t_in, in_grads)
        store_blocks(mlp_back, t_mlp, mlp_grads)


def backward_kernel(pairs, outs_n, back_ref, normed_ref, qkv_ref, probs_ref, grad_mix_ref, tables_ref, masks_ref, *refs):
    grad_ref = refs[0]
    outs = refs[1 : 1 + outs_n]
    total, grad_keys, grad_values, grad_queries = refs[1 + outs_n :]
    step = pl.program_id(0)

    @pl.when(step == 0)
    def _():
        total[...] = jnp.zeros_like(total)

    tables = (tables_ref[0], tables_ref[1], tables_ref[2])

    def back(pair, carry):
        column = pl.multiple_of(pair * 3 * PAIR, 128)
        out_column = pl.multiple_of(pair * PAIR, 128)
        grad_keys[...] = jnp.zeros_like(grad_keys)
        grad_values[...] = jnp.zeros_like(grad_values)
        for block in range(BLOCKS):
            rows = slice(block * BLOCK, (block + 1) * BLOCK)
            window = slice(STARTS[block], STARTS[block] + SPAN)
            queries = both_heads(qkv_ref[rows, pl.ds(column, PAIR)], masks_ref) * bf16(HEAD**-0.5)
            grad_mix = both_heads(grad_mix_ref[rows, pl.ds(out_column, PAIR)], masks_ref)
            probs = probs_ref[0, pair, block]
            grad_soft = dot_nt(qkv_ref[window, pl.ds(column + 2 * PAIR, PAIR)], grad_mix)
            soft = probs.astype(f32)
            inner = jnp.sum(soft * grad_soft, axis=0, keepdims=True)
            grad_scores = (soft * (grad_soft - inner)).astype(bf16)
            grad_values[window, :] += dot_nn(probs, grad_mix)
            grad_keys[window, :] += dot_nn(grad_scores, queries)
            grad_turned = dot_tn(qkv_ref[window, pl.ds(column + PAIR, PAIR)], grad_scores)
            grad_queries[rows, :] = one_of_each(grad_turned) * HEAD**-0.5
        grad_ref[:, pl.ds(column, PAIR)] = turn(grad_queries[...], tables, -1).astype(bf16)
        grad_ref[:, pl.ds(column + PAIR, PAIR)] = turn(grad_keys[...], tables, -1).astype(bf16)
        grad_ref[:, pl.ds(column + 2 * PAIR, PAIR)] = grad_values[...].astype(bf16)
        return carry

    lax.fori_loop(0, pairs, back, 0)
    total[...] += dot_tn(normed_ref[...], grad_ref[...])

    @pl.when(step == pl.num_programs(0) - 1)
    def _():
        store_blocks(back_ref, total, outs)


def final_kernel(groups_n, counts, *refs):
    refs = list(refs)
    take = lambda n: [refs.pop(0) for _ in range(n)]
    qkv_places = take(groups_n)
    (mlp_places,) = take(1)
    tokens_ref, gain_ref, hidden_ref, gated_ref, grad_hidden_ref = take(5)
    grad_refs = take(groups_n)
    qkv_pieces = [take(n) for n in counts[:-1]]
    mlp_pieces = take(counts[-1])
    output_ref, tokens_grad_ref, gain_grad_ref = take(3)
    weights = take(groups_n)
    w_mlp, sems = refs
    step = pl.program_id(0)

    @pl.when(step == 0)
    def _():
        copies = []
        for at in range(groups_n):
            copies += load_pieces(qkv_places[at], qkv_pieces[at], weights[at], sems.at[at])
        copies += load_pieces(mlp_places, mlp_pieces, w_mlp, sems.at[groups_n])
        gain_grad_ref[...] = jnp.zeros_like(gain_grad_ref)
        for copy in copies:
            copy.wait()

    grad_normed = dot_nt(grad_refs[0][...], weights[0][...])
    for grad_ref, weight in zip(grad_refs[1:], weights[1:]):
        grad_normed = grad_normed + dot_nt(grad_ref[...], weight[...])
    normed, scale = norm_of(tokens_ref[...].astype(f32))
    gain_grad_ref[...] += jnp.sum(grad_normed * normed, axis=0, keepdims=True)
    tokens_grad_ref[...] = grad_hidden_ref[...] + norm_back(grad_normed * gain_ref[...], normed, scale)
    output_ref[...] = (hidden_ref[...] + dot_nn(gated_ref[...], w_mlp[...])).astype(bf16)


SMEM = pl.BlockSpec(memory_space=pltpu.SMEM)
ANYWHERE = pl.BlockSpec(memory_space=pl.ANY)


def rows_spec(rows, columns):
    return pl.BlockSpec((rows, columns), lambda i: (i, 0))


def whole_spec(*shape):
    return pl.BlockSpec(shape, lambda i: (0,) * len(shape))


def call(kernel, steps, inputs, outputs, scratch, flops, nbytes):
    return pl.pallas_call(
        kernel,
        grid=(steps,),
        in_specs=[spec for _, spec in inputs],
        out_specs=[spec for _, _, spec in outputs],
        out_shape=[jax.ShapeDtypeStruct(shape, dtype) for shape, dtype, _ in outputs],
        scratch_shapes=scratch,
        compiler_params=pltpu.CompilerParams(
            dimension_semantics=("arbitrary",), vmem_limit_bytes=VMEM_LIMIT
        ),
        cost_estimate=pl.CostEstimate(flops=int(flops), bytes_accessed=int(nbytes), transcendentals=0),
    )(*[array for array, _ in inputs])


def rope_constants():
    inverse = 10000.0 ** (-np.arange(0, HEAD, 2, dtype=np.float64) / HEAD)
    angles = np.arange(LEN, dtype=np.float64)[:, None] * inverse[None, :]
    angles = np.concatenate([angles] * 4, axis=-1)
    upper = (np.arange(PAIR) % HEAD >= HEAD // 2)[None, :]
    sine = np.sin(angles)
    return np.stack([np.cos(angles), np.where(upper, sine, 0.0), np.where(upper, 0.0, -sine)]).astype(
        np.float32
    )


def shards(devices, tokens, qkv_weight, out_weight, in_weight, mlp_weight, norm_gains, cotangent):
    count = tokens.shape[0]
    sequences = count // LEN
    fast = devices == 32
    orders = ((ALONG_Y, ALONG_X), (ALONG_X, ALONG_Y))

    if fast:
        gains = gather_vector(norm_gains)
        by_pair = qkv_weight.reshape(24, 3, PAIRS, PAIR).transpose(0, 2, 1, 3)
        gathered_qkv = [
            gather_rows(by_pair[:, start : start + pairs].reshape(24, pairs * 3 * PAIR), *orders[at % 2])
            for at, (start, pairs) in enumerate(GROUPS)
        ]
        gathered_in = gather_rows(in_weight.reshape(24, 2 * FF), ALONG_X, ALONG_Y)
        gathered_out = gather_rows(out_weight.reshape(24, D), ALONG_Y, ALONG_X)
        gathered_mlp = gather_tall(mlp_weight.reshape(36, D))
    else:
        whole = lambda w: lax.all_gather(w, "fsdp", axis=0, tiled=True)
        nowhere = table([(0, 0)])
        gains = whole(norm_gains)
        by_pair = whole(qkv_weight).reshape(D, 3, PAIRS, PAIR).transpose(0, 2, 1, 3)
        gathered_qkv = [
            ([by_pair[:, start : start + pairs].reshape(1, D, pairs * 3 * PAIR)], nowhere)
            for start, pairs in GROUPS
        ]
        gathered_in = ([whole(in_weight).reshape(1, D, 2 * FF)], nowhere)
        gathered_out = ([whole(out_weight).reshape(1, D, D)], nowhere)
        gathered_mlp = ([whole(mlp_weight).reshape(1, FF, D)], nowhere)
    gains = gains.astype(f32)
    gain_attn, gain_mlp = gains[:D].reshape(1, D), gains[D:].reshape(1, D)

    def back_places(rows, columns, first, second):
        if not fast:
            return table([(0, 0)]), [(1, rows, columns)]
        if first is None:
            rows, half = rows // 8, columns // 2
            return tall_places(rows, half, (0, 1)), [(8, rows, half)] * 2
        rows, half = rows // 16, columns // 2
        return places(rows, half, first, second, (0, 1)), [(16, rows, half)] * 2

    tables = jnp.asarray(rope_constants())
    masks = np.arange(PAIR)[None, :] // HEAD == np.arange(2)[:, None]
    masks = jnp.asarray(masks.astype(np.float32)).astype(bf16)
    flat = lambda spots: spots.reshape(-1)

    qkv, probs, mixes = [], [], []
    normed = None
    for at, (start, pairs) in enumerate(GROUPS):
        pieces, spots = gathered_qkv[at]
        width = pairs * 3 * PAIR
        normed, qkv_rows, group_probs, mix = call(
            functools.partial(forward_kernel, pairs, len(pieces)),
            sequences,
            [
                (flat(spots), SMEM),
                (tokens, rows_spec(LEN, D)),
                (gain_attn, whole_spec(1, D)),
                (tables, whole_spec(3, LEN, PAIR)),
                (masks, whole_spec(2, PAIR)),
            ]
            + [(piece, ANYWHERE) for piece in pieces],
            [
                ((count, D), bf16, rows_spec(LEN, D)),
                ((count, width), bf16, rows_spec(LEN, width)),
                (
                    (sequences, pairs, BLOCKS, SPAN, SPAN),
                    bf16,
                    pl.BlockSpec((1, pairs, BLOCKS, SPAN, SPAN), lambda i: (i, 0, 0, 0, 0)),
                ),
                ((count, pairs * PAIR), bf16, rows_spec(LEN, pairs * PAIR)),
            ],
            [
                pltpu.VMEM((D, width), bf16),
                pltpu.VMEM((3, SPAN, SPAN), f32),
                pltpu.SemaphoreType.DMA,
            ],
            2 * count * D * width * 2,
            count * width * 4,
        )
        qkv.append(qkv_rows)
        probs.append(group_probs)
        mixes.append(mix)

    step_rows = 256
    gathered = (gathered_out, gathered_in, gathered_mlp)
    backs = (
        back_places(D, D, ALONG_Y, ALONG_X),
        back_places(D, 2 * FF, ALONG_X, ALONG_Y),
        back_places(FF, D, None, None),
    )
    counts = tuple(len(pieces) for pieces, _ in gathered)
    grads_out = [(shape, bf16, whole_spec(*shape)) for _, shapes in backs for shape in shapes]
    results = call(
        functools.partial(feed_kernel, len(GROUPS), counts),
        count // step_rows,
        [(flat(spots), SMEM) for _, spots in gathered]
        + [(flat(spots), SMEM) for spots, _ in backs]
        + [
            (tokens, rows_spec(step_rows, D)),
            (cotangent, rows_spec(step_rows, D)),
            (gain_mlp, whole_spec(1, D)),
        ]
        + [(mix, rows_spec(step_rows, mix.shape[1])) for mix in mixes]
        + [(piece, ANYWHERE) for pieces, _ in gathered for piece in pieces],
        [
            ((count, D), f32, rows_spec(step_rows, D)),
            ((count, FF), bf16, rows_spec(step_rows, FF)),
            ((count, D), f32, rows_spec(step_rows, D)),
        ]
        + [((count, mix.shape[1]), bf16, rows_spec(step_rows, mix.shape[1])) for mix in mixes]
        + [((1, D), f32, whole_spec(1, D))]
        + grads_out,
        [
            pltpu.VMEM((D, D), bf16),
            pltpu.VMEM((D, 2 * FF), bf16),
            pltpu.VMEM((FF, D), bf16),
            pltpu.VMEM((D, D), f32),
            pltpu.VMEM((D, 2 * FF), f32),
            pltpu.VMEM((FF, D), f32),
            pltpu.SemaphoreType.DMA((3,)),
        ],
        2 * count * (3 * D * D + 6 * D * FF + 2 * D * FF),
        count * D * 16,
    )
    hidden, gated, grad_hidden = results[:3]
    grad_mixes = results[3 : 3 + len(GROUPS)]
    gain_mlp_grad = results[3 + len(GROUPS)]
    weight_grads = results[4 + len(GROUPS) :]

    def scatter(blocks, first, second):
        if not fast:
            return lax.psum_scatter(
                blocks[0].astype(f32).reshape(-1), "fsdp", scatter_dimension=0, tiled=True
            )
        if first is None:
            return scatter_tall(*blocks).reshape(-1)
        return scatter_rows(*blocks, first, second).reshape(-1)

    each = 2 if fast else 1
    mlp_share = scatter(weight_grads[2 * each :], None, None)
    in_share = scatter(weight_grads[each : 2 * each], ALONG_X, ALONG_Y)
    out_share = scatter(weight_grads[:each], ALONG_Y, ALONG_X)

    grads = [None] * len(GROUPS)
    qkv_shares = [None] * len(GROUPS)
    for at in reversed(range(len(GROUPS))):
        start, pairs = GROUPS[at]
        width = pairs * 3 * PAIR
        spots, shapes = back_places(D, width, *orders[at % 2])
        results = call(
            functools.partial(backward_kernel, pairs, len(shapes)),
            sequences,
            [
                (flat(spots), SMEM),
                (normed, rows_spec(LEN, D)),
                (qkv[at], rows_spec(LEN, width)),
                (
                    probs[at],
                    pl.BlockSpec((1, pairs, BLOCKS, SPAN, SPAN), lambda i: (i, 0, 0, 0, 0)),
                ),
                (grad_mixes[at], rows_spec(LEN, pairs * PAIR)),
                (tables, whole_spec(3, LEN, PAIR)),
                (masks, whole_spec(2, PAIR)),
            ],
            [((count, width), bf16, rows_spec(LEN, width))]
            + [(shape, bf16, whole_spec(*shape)) for shape in shapes],
            [
                pltpu.VMEM((D, width), f32),
                pltpu.VMEM((LEN, PAIR), f32),
                pltpu.VMEM((LEN, PAIR), f32),
                pltpu.VMEM((LEN, PAIR), f32),
            ],
            2 * count * D * width * 2,
            count * width * 4,
        )
        grads[at] = results[0]
        qkv_shares[at] = scatter(results[1:], *orders[at % 2]) if fast else results[1:]

    if fast:
        qkv_share = jnp.concatenate(
            [share.reshape(24, pairs, 3, PAIR) for share, (_, pairs) in zip(qkv_shares, GROUPS)], axis=1
        )
        qkv_share = qkv_share.transpose(0, 2, 1, 3).reshape(-1)
    else:
        qkv_share = jnp.concatenate(
            [blocks[0].reshape(D, pairs, 3, PAIR) for blocks, (_, pairs) in zip(qkv_shares, GROUPS)], axis=1
        )
        qkv_share = scatter([qkv_share.transpose(0, 2, 1, 3)], None, None)

    counts = tuple(len(pieces) for pieces, _ in gathered_qkv) + (len(gathered_mlp[0]),)
    output, tokens_grad, gain_attn_grad = call(
        functools.partial(final_kernel, len(GROUPS), counts),
        count // step_rows,
        [(flat(spots), SMEM) for _, spots in gathered_qkv]
        + [(flat(gathered_mlp[1]), SMEM)]
        + [
            (tokens, rows_spec(step_rows, D)),
            (gain_attn, whole_spec(1, D)),
            (hidden, rows_spec(step_rows, D)),
            (gated, rows_spec(step_rows, FF)),
            (grad_hidden, rows_spec(step_rows, D)),
        ]
        + [(grad, rows_spec(step_rows, grad.shape[1])) for grad in grads]
        + [(piece, ANYWHERE) for pieces, _ in gathered_qkv for piece in pieces]
        + [(piece, ANYWHERE) for piece in gathered_mlp[0]],
        [
            ((count, D), bf16, rows_spec(step_rows, D)),
            ((count, D), f32, rows_spec(step_rows, D)),
            ((1, D), f32, whole_spec(1, D)),
        ],
        [pltpu.VMEM((D, pairs * 3 * PAIR), bf16) for _, pairs in GROUPS]
        + [pltpu.VMEM((FF, D), bf16), pltpu.SemaphoreType.DMA((len(GROUPS) + 1,))],
        2 * count * (3 * D * D + FF * D),
        count * D * 20,
    )
    gains_grad = jnp.concatenate([gain_attn_grad.reshape(-1), gain_mlp_grad.reshape(-1)])
    if fast:
        gains_share = scatter_vector(gains_grad)
    else:
        gains_share = lax.psum_scatter(gains_grad, "fsdp", scatter_dimension=0, tiled=True)
    return (output, tokens_grad, qkv_share, out_share, in_share, mlp_share, gains_share)


def solution(mesh):
    placed = (P("fsdp", None),) + (P("fsdp"),) * 5 + (P("fsdp", None),)
    return jax.shard_map(
        functools.partial(shards, mesh.shape["fsdp"]),
        mesh=mesh,
        in_specs=placed,
        out_specs=(P("fsdp", None),) * 2 + (P("fsdp"),) * 5,
        check_vma=False,
    )
```

time: 1000 us -> 411 us (0.41)
  waiting for transfers between devices: 347 us -> 88 us
  matrix products: 254 us -> 0 us
  Pallas kernels: 0 us -> 208 us
  local copies, waits for them, and re-layouts: 165 us -> 13.6 us
  other arithmetic: 129 us -> 14.2 us
  starting transfers between devices: 0.19 us -> 84.4 us
  blocking collectives: 82.6 us -> 0 us
  between operations: 14.7 us -> 1.62 us
    dot_general x40 -> x0, matrix products: 254 us -> none  [the longest x4 58.1 us: times_transposed(): lax.dot_general(left_side, right_side, (((1,), (1,)), ((), ())), preferre...]
    unnamed x6 -> x0, waiting for transfers between devices: 240 us -> none
    pallas_call x0 -> x6, Pallas kernels: none -> 208 us  [call(): pl.pallas_call(kernel, grid=(steps,), in_specs=[spec for _, spec in input...]
    all_gather x4 -> x0, waiting for transfers between devices: 107 us -> none  [the longest x1 57.7 us: shards(): lax.all_gather(qkv_weight, 'fsdp', axis=0, tiled=True)]
    ppermute x0 -> x85, waiting for transfers between devices: none -> 88 us  [swap(): return lax.ppermute(values, 'fsdp', [(i, i ^ bits) for i in range(32)])]
    ppermute x0 -> x85, starting transfers between devices: none -> 84.4 us  [swap(): return lax.ppermute(values, 'fsdp', [(i, i ^ bits) for i in range(32)])]
    unnamed x2 -> x0, blocking collectives: 82.6 us -> none
    unnamed x86 -> x62, local copies, waits for them, and re-layouts: 51.9 us -> 2.04 us
  transfers between devices with their start and end apart: 5 -> 85, of which waited for: 3 -> 32; matrix products, arithmetic and copies ran while one was open for 20% -> 6% of each run, Pallas kernels for 0% -> 17%
where the time goes in v1:
time: 411 us; the launch traced here: 410 us
  Pallas kernels  208 us (51%)
  waiting for transfers between devices  88 us (21%)
  starting transfers between devices  84.4 us (21%)
  other arithmetic  14.2 us (3%)
  local copies, waits for them, and re-layouts  13.6 us (3%)
    pallas_call x6, Pallas kernels, call(): pl.pallas_call(kernel, grid=(steps,), in_specs=[spec for _, spec in input...  208 us
    ppermute x85, waiting for transfers between devices, swap(): return lax.ppermute(values, 'fsdp', [(i, i ^ bits) for i in range(32)])  88 us
    ppermute x85, starting transfers between devices, swap(): return lax.ppermute(values, 'fsdp', [(i, i ^ bits) for i in range(32)])  84.4 us
  transfers between devices with their start and end apart: 85, of which 32 were waited for; matrix products, arithmetic and copies ran while one was open for 6% of the time, Pallas kernels for 17%

profile of v1, /device:TPU:0, one launch (start us, length us, event | category | flops | bytes accessed | tf_op | source)
XLA Modules:
  0.0 410.2 jit_solution(9837131479120875504)
XLA Ops:
  10.0 2.7 collective-permute-start.1
  14.4 2.0 collective-permute-start.2
  18.0 2.1 collective-permute-start.3
  21.6 3.1 collective-permute-start.4
  26.3 2.0 collective-permute-start.6
  28.3 2.7 collective-permute-start.7
  32.2 3.6 collective-permute-start.23
  38.1 3.9 collective-permute-start.15
  42.8 3.9 collective-permute-start.31
  47.1 1.6 collective-permute-start.9
  50.7 2.2 collective-permute-start.41
  52.9 5.7 %collective-permute-done.31 = bf16[48,1152]{1,0:T(8,128)(2,1)S(1)} collective-permute-done((bf16[48,1152]{1,0:T(8,128)(2,1)S(1)}, bf16[48,1152]{1,0:T(8,128)(2,1)S(1)}, u32[]{:S(2)}, u32[]{:S(2)}) %collective-permute-start.31) | collective-permute-done | bytes 110624 | tf_op jit(solution)/shard_map/ppermute | solution.py:43
  59.1 1.6 collective-permute-start.33
  60.8 7.7 %collective-permute-done.17 = bf16[4,48,768]{2,1,0:T(8,128)(2,1)S(1)} collective-permute-done((bf16[4,48,768]{2,1,0:T(8,128)(2,1)S(1)}, bf16[4,48,768]{2,1,0:T(8,128)(2,1)S(1)}, u32[]{:S(2)}, u32[]{:S(2)}) %collective-permute-start.17) | collective-permute-done | bytes 294944 | tf_op jit(solution)/shard_map/ppermute | solution.py:43
  68.6 1.6 collective-permute-start.18
  70.8 2.2 collective-permute-start.39
  73.0 3.3 collective-permute-done.33
  77.2 2.2 collective-permute-done.10.refs_1_.refs_11_
  82.8 3.0 collective-permute-done.26.refs_12_
  88.1 25.6 %shard_map.144 = (bf16[2048,768]{1,0:T(8,128)(2,1)}, bf16[2048,768]{1,0:T(8,128)(2,1)}, bf16[4,2,4,256,256]{4,3,2,1,0:T(8,128)(2,1)}, bf16[2048,256]{1,0:T(8,128)(2,1)}) custom-call(s32[64]{0:T(128)} %reshape.424.places_ref.refs_0_.refs_3_.back_ref, bf16[2048,768]{1,0:T(8,128)(2,1)} %refs_3_.1, f32[1,768]{1,0:T(1,128)} %reshape.427.gain_ref.refs_4_, ...), custom_call_target="tpu_custom_call" | custom-call | flops 4831838208 | bytes 6291456 | tf_op jit(solution)/shard_map/pallas_call | solution.py:448
  115.4 45.8 %shard_map.145 = (bf16[2048,768]{1,0:T(8,128)(2,1)}, bf16[2048,1536]{1,0:T(8,128)(2,1)}, bf16[4,4,4,256,256]{4,3,2,1,0:T(8,128)(2,1)}, bf16[2048,512]{1,0:T(8,128)(2,1)}) custom-call(s32[64]{0:T(128)} %reshape.425.places_ref.back_ref.refs_1_, bf16[2048,768]{1,0:T(8,128)(2,1)} %refs_3_.1, f32[1,768]{1,0:T(1,128)} %reshape.427.gain_ref.refs_4_, ...), custom_call_target="tpu_custom_call" | custom-call | flops 9663676416 | bytes 12582912 | tf_op jit(solution)/shard_map/pallas_call | solution.py:448
  162.4 57.4 %shard_map.146 = (f32[2048,768]{1,0:T(8,128)}, bf16[2048,1152]{1,0:T(8,128)(2,1)}, f32[2048,768]{1,0:T(8,128)}, bf16[2048,256]{1,0:T(8,128)(2,1)}, bf16[2048,512...) custom-call(s32[64]{0:T(128)} %reshape.424.places_ref.refs_0_.refs_3, ...), custom_call_target="tpu_custom_call" | custom-call | flops 36238786560 | bytes 25165824 | tf_op jit(solution)/shard_map/pallas_call | solution.py:448
  219.8 20.2 %shard_map.147 = (bf16[2048,768]{1,0:T(8,128)(2,1)}, bf16[16,48,384]{2,1,0:T(8,128)(2,1)}, bf16[16,48,384]{2,1,0:T(8,128)(2,1)}) custom-call(s32[64]{0:T(128)} %reshape.424.places_ref.refs_0_.refs_3_.back_ref, bf16[2048,768]{1,0:T(8,128)(2,1)} %get-tuple-element.40.normed_ref, bf16[2048,768]{1,0:T(8,128)(2,1)} %get-tuple-element.41.qkv_ref, ...), custom_call_target="tpu_custom_call" | custom-call | flops 4831838208 | bytes 6291456 | tf_op jit(solution)/shard_map/pallas_call | solution.py:448
  240.0 37.1 %shard_map.148 = (bf16[2048,1536]{1,0:T(8,128)(2,1)}, bf16[16,48,768]{2,1,0:T(8,128)(2,1)}, bf16[16,48,768]{2,1,0:T(8,128)(2,1)}) custom-call(s32[64]{0:T(128)} %reshape.425.places_ref.back_ref.refs_1_, bf16[2048,768]{1,0:T(8,128)(2,1)} %get-tuple-element.40.normed_ref, bf16[2048,1536]{1,0:T(8,128)(2,1)} %get-tuple-element.45.qkv_ref, ...), custom_call_target="tpu_custom_call" | custom-call | flops 9663676416 | bytes 12582912 | tf_op jit(solution)/shard_map/pallas_call | solution.py:448
  277.2 22.3 %shard_map.149 = (bf16[2048,768]{1,0:T(8,128)(2,1)}, f32[2048,768]{1,0:T(8,128)}, f32[1,768]{1,0:T(1,128)}) custom-call(s32[64]{0:T(128)} %reshape.424.places_ref.refs_0_.refs_3_.back_ref, s32[64]{0:T(128)} %reshape.425.places_ref.back_ref.refs_1_, s32[32]{0:T(128)} %reshape.426.refs_2_.refs_5_, bf16[2048,768]{1,0:T(8,128)(2,1)} %refs_3_.1, ...), custom_call_target="tpu_custom_call" | custom-call | flops 10871635968 | bytes 31457280 | tf_op jit(solution)/shard_map/pallas_call | solution.py:448
  301.5 3.3 collective-permute-done.80
  305.2 3.3 collective-permute-done.81
  309.3 2.9 collective-permute-done.82
  313.6 2.2 collective-permute-done.83
  320.4 6.7 %collective-permute-done.46 = bf16[8,48,384]{2,1,0:T(8,128)(2,1)S(1)} collective-permute-done((bf16[8,48,384]{2,1,0:T(8,128)(2,1)S(1)}, bf16[8,48,384]{2,1,0:T(8,128)(2,1)S(1)}, u32[]{:S(2)}, u32[]{:S(2)}) %collective-permute-start.46) | collective-permute-done | bytes 294944 | tf_op jit(solution)/shard_map/ppermute | solution.py:43
  327.9 4.9 %collective-permute-done.60 = bf16[8,48,384]{2,1,0:T(8,128)(2,1)S(1)} collective-permute-done((bf16[8,48,384]{2,1,0:T(8,128)(2,1)S(1)}, bf16[8,48,384]{2,1,0:T(8,128)(2,1)S(1)}, u32[]{:S(2)}, u32[]{:S(2)}) %collective-permute-start.60) | collective-permute-done | bytes 294944 | tf_op jit(solution)/shard_map/ppermute | solution.py:43
  333.9 2.5 collective-permute-start.50
  336.4 1.9 collective-permute-done.61
  339.7 2.7 collective-permute-start.64
  342.5 1.6 collective-permute-start.62
  350.2 8.0 %collective-permute-done.74 = bf16[4,144,384]{2,1,0:T(8,128)(2,1)S(1)} collective-permute-done((bf16[4,144,384]{2,1,0:T(8,128)(2,1)S(1)}, bf16[4,144,384]{2,1,0:T(8,128)(2,1)S(1)}, u32[]{:S(2)}, u32[]{:S(2)}) %collective-permute-start.74) | collective-permute-done | bytes 442400 | tf_op jit(solution)/shard_map/ppermute | solution.py:43
  359.0 1.8 collective-permute-start.77
  360.8 2.6 collective-permute-start.75
  365.9 2.2 collective-permute-done.76
  372.3 1.9 add_convert_fusion.1
  375.4 2.3 collective-permute-done.54
  378.8 2.5 collective-permute-start.57
  383.3 7.1 %collective-permute-done.67 = bf16[8,48,1152]{2,1,0:T(8,128)(2,1)S(1)} collective-permute-done((bf16[8,48,1152]{2,1,0:T(8,128)(2,1)S(1)}, bf16[8,48,1152]{2,1,0:T(8,128)(2,1)S(1)}, u32[]{:S(2)}, u32[]{:S(2)}) %collective-permute-start.67) | collective-permute-done | bytes 884768 | tf_op jit(solution)/shard_map/ppermute | solution.py:43
  392.8 6.0 %collective-permute-done.68 = bf16[4,48,1152]{2,1,0:T(8,128)(2,1)S(1)} collective-permute-done((bf16[4,48,1152]{2,1,0:T(8,128)(2,1)S(1)}, bf16[4,48,1152]{2,1,0:T(8,128)(2,1)S(1)}, u32[]{:S(2)}, u32[]{:S(2)}) %collective-permute-start.68) | collective-permute-done | bytes 442400 | tf_op jit(solution)/shard_map/ppermute | solution.py:43
  399.1 2.2 collective-permute-start.71
  401.5 2.1 collective-permute-start.69
  403.6 2.2 collective-permute-done.71
  405.7 2.3 collective-permute-done.70
  (352 shorter events, 67.9 us)
Async XLA Ops:
  0.7 9.3 %collective-permute-start = (bf16[48]{0:T(256)(128)(2,1)}, bf16[48]{0:T(256)(128)(2,1)S(1)}, u32[]{:S(2)}, u32[]{:S(2)}) collective-permute-start(bf16[48]{0:T(256)(128)(2,1)} %param.14), channel_id=1, source_target_pairs={{0,1},{1,0},{2,3},{3,2},{4,5},{5,4},{6,7},{7,6},{8,9},{9,8},{10,11... | collective-permute-start | bytes 296 | tf_op jit(solution)/shard_map/ppermute | solution.py:43
  2.2 24.1 %collective-permute-start.5 = (bf16[24,384]{1,0:T(8,128)(2,1)S(1)}, bf16[24,384]{1,0:T(8,128)(2,1)S(1)}, u32[]{:S(2)}, u32[]{:S(2)}) collective-permute-start(bf16[24,384]{1,0:T(8,128)(2,1)S(1)} %get-tuple-element.115), channel_id=1, source_target_pairs={{0,1},{1,0},{2,3},{3,2},{4,5},{5,4},{6,7},{7,6},{8,9},{9,8},{10,11... | collective-permute-start | bytes 55304 | tf_op jit(solution)/shard_map/ppermute | solution.py:43
  2.5 28.9 %collective-permute-start.13 = (bf16[24,768]{1,0:T(8,128)(2,1)S(1)}, bf16[24,768]{1,0:T(8,128)(2,1)S(1)}, u32[]{:S(2)}, u32[]{:S(2)}) collective-permute-start(bf16[24,768]{1,0:T(8,128)(2,1)S(1)} %get-tuple-element.109), channel_id=1, source_target_pairs={{0,1},{1,0},{2,3},{3,2},{4,5},{5,4},{6,7},{7,6},{8,9},{9,8},{10,11... | collective-permute-start | bytes 110600 | tf_op jit(solution)/shard_map/ppermute | solution.py:43
  3.9 24.4 %collective-permute-start.21 = (bf16[24,384]{1,0:T(8,128)(2,1)S(1)}, bf16[24,384]{1,0:T(8,128)(2,1)S(1)}, u32[]{:S(2)}, u32[]{:S(2)}) collective-permute-start(bf16[24,384]{1,0:T(8,128)(2,1)S(1)} %get-tuple-element.113), channel_id=1, source_target_pairs={{0,1},{1,0},{2,3},{3,2},{4,5},{5,4},{6,7},{7,6},{8,9},{9,8},{10,11... | collective-permute-start | bytes 55304 | tf_op jit(solution)/shard_map/ppermute | solution.py:43
  5.1 27.1 %collective-permute-start.29 = (bf16[24,1152]{1,0:T(8,128)(2,1)S(1)}, bf16[24,1152]{1,0:T(8,128)(2,1)S(1)}, u32[]{:S(2)}, u32[]{:S(2)}) collective-permute-start(bf16[24,1152]{1,0:T(8,128)(2,1)S(1)} %get-tuple-element.103), channel_id=1, source_target_pairs={{0,1},{1,0},{2,3},{3,2},{4,5},{5,4},{6,7},{7,6},{8,9},{9,8},{10,11... | collective-permute-start | bytes 165896 | tf_op jit(solution)/shard_map/ppermute | solution.py:43
  26.3 9.4 %collective-permute-start.6 = (bf16[48,384]{1,0:T(8,128)(2,1)S(1)}, bf16[48,384]{1,0:T(8,128)(2,1)S(1)}, u32[]{:S(2)}, u32[]{:S(2)}) collective-permute-start(bf16[48,384]{1,0:T(8,128)(2,1)S(1)} %maximum_select_fusion.13), channel_id=1, source_target_pairs={{0,8},{1,9},{2,10},{3,11},{4,12},{5,13},{6,14},{7,15},{8,0},{9,1},... | collective-permute-start | bytes 110600 | tf_op jit(solution)/shard_map/ppermute | solution.py:43
  28.3 7.9 %collective-permute-start.7 = (bf16[48,384]{1,0:T(8,128)(2,1)S(1)}, bf16[48,384]{1,0:T(8,128)(2,1)S(1)}, u32[]{:S(2)}, u32[]{:S(2)}) collective-permute-start(bf16[48,384]{1,0:T(8,128)(2,1)S(1)} %maximum_select_fusion.13), channel_id=1, source_target_pairs={{0,16},{1,17},{2,18},{3,19},{4,20},{5,21},{6,22},{7,23},{8,24},{9,... | collective-permute-start | bytes 110600 | tf_op jit(solution)/shard_map/ppermute | solution.py:43
  32.2 9.8 %collective-permute-start.23 = (bf16[48,384]{1,0:T(8,128)(2,1)S(1)}, bf16[48,384]{1,0:T(8,128)(2,1)S(1)}, u32[]{:S(2)}, u32[]{:S(2)}) collective-permute-start(bf16[48,384]{1,0:T(8,128)(2,1)S(1)} %maximum_select_fusion.15), channel_id=1, source_target_pairs={{0,16},{1,17},{2,18},{3,19},{4,20},{5,21},{6,22},{7,23},{8,24},{9,... | collective-permute-start | bytes 110600 | tf_op jit(solution)/shard_map/ppermute | solution.py:43
  37.8 8.9 %collective-permute-start.14 = (bf16[48,768]{1,0:T(8,128)(2,1)S(1)}, bf16[48,768]{1,0:T(8,128)(2,1)S(1)}, u32[]{:S(2)}, u32[]{:S(2)}) collective-permute-start(bf16[48,768]{1,0:T(8,128)(2,1)S(1)} %maximum_select_fusion.9), channel_id=1, source_target_pairs={{0,8},{1,9},{2,10},{3,11},{4,12},{5,13},{6,14},{7,15},{8,0},{9,1},... | collective-permute-start | bytes 221192 | tf_op jit(solution)/shard_map/ppermute | solution.py:43
  38.1 9.0 %collective-permute-start.15 = (bf16[48,768]{1,0:T(8,128)(2,1)S(1)}, bf16[48,768]{1,0:T(8,128)(2,1)S(1)}, u32[]{:S(2)}, u32[]{:S(2)}) collective-permute-start(bf16[48,768]{1,0:T(8,128)(2,1)S(1)} %maximum_select_fusion.9), channel_id=1, source_target_pairs={{0,16},{1,17},{2,18},{3,19},{4,20},{5,21},{6,22},{7,23},{8,24},{9,... | collective-permute-start | bytes 221192 | tf_op jit(solution)/shard_map/ppermute | solution.py:43
  42.4 8.2 %collective-permute-start.30 = (bf16[48,1152]{1,0:T(8,128)(2,1)S(1)}, bf16[48,1152]{1,0:T(8,128)(2,1)S(1)}, u32[]{:S(2)}, u32[]{:S(2)}) collective-permute-start(bf16[48,1152]{1,0:T(8,128)(2,1)S(1)} %maximum_select_fusion.4), channel_id=1, source_target_pairs={{0,8},{1,9},{2,10},{3,11},{4,12},{5,13},{6,14},{7,15},{8,0},{9,1},... | collective-permute-start | bytes 331784 | tf_op jit(solution)/shard_map/ppermute | solution.py:43
  42.8 15.8 %collective-permute-start.31 = (bf16[48,1152]{1,0:T(8,128)(2,1)S(1)}, bf16[48,1152]{1,0:T(8,128)(2,1)S(1)}, u32[]{:S(2)}, u32[]{:S(2)}) collective-permute-start(bf16[48,1152]{1,0:T(8,128)(2,1)S(1)} %maximum_select_fusion.4), channel_id=1, source_target_pairs={{0,16},{1,17},{2,18},{3,19},{4,20},{5,21},{6,22},{7,23},{8,24},{9,... | collective-permute-start | bytes 331784 | tf_op jit(solution)/shard_map/ppermute | solution.py:43
  46.7 12.4 %collective-permute-start.32 = (bf16[48,1152]{1,0:T(8,128)(2,1)S(1)}, bf16[48,1152]{1,0:T(8,128)(2,1)S(1)}, u32[]{:S(2)}, u32[]{:S(2)}) collective-permute-start(bf16[48,1152]{1,0:T(8,128)(2,1)S(1)} %maximum_select_fusion.4), channel_id=1, source_target_pairs={{0,24},{1,25},{2,26},{3,27},{4,28},{5,29},{6,30},{7,31},{8,16},{9,... | collective-permute-start | bytes 331784 | tf_op jit(solution)/shard_map/ppermute | solution.py:43
  47.1 21.5 %collective-permute-start.9 = (bf16[4,48,384]{2,1,0:T(8,128)(2,1)S(1)}, bf16[4,48,384]{2,1,0:T(8,128)(2,1)S(1)}, u32[]{:S(2)}, u32[]{:S(2)}) collective-permute-start(bf16[4,48,384]{2,1,0:T(8,128)(2,1)S(1)} %pad_maximum_fusion.3), channel_id=1, source_target_pairs={{0,4},{1,5},{2,6},{3,7},{4,0},{5,1},{6,2},{7,3},{8,12},{9,13},{10,... | collective-permute-start | bytes 442376 | tf_op jit(solution)/shard_map/ppermute | solution.py:43
  49.1 21.1 %collective-permute-start.25 = (bf16[4,48,384]{2,1,0:T(8,128)(2,1)S(1)}, bf16[4,48,384]{2,1,0:T(8,128)(2,1)S(1)}, u32[]{:S(2)}, u32[]{:S(2)}) collective-permute-start(bf16[4,48,384]{2,1,0:T(8,128)(2,1)S(1)} %pad_maximum_fusion.4), channel_id=1, source_target_pairs={{0,4},{1,5},{2,6},{3,7},{4,0},{5,1},{6,2},{7,3},{8,12},{9,13},{10,... | collective-permute-start | bytes 442376 | tf_op jit(solution)/shard_map/ppermute | solution.py:43
  50.7 20.1 %collective-permute-start.41 = (bf16[144,384]{1,0:T(8,128)(2,1)S(1)}, bf16[144,384]{1,0:T(8,128)(2,1)S(1)}, u32[]{:S(2)}, u32[]{:S(2)}) collective-permute-start(bf16[144,384]{1,0:T(8,128)(2,1)S(1)} %maximum_select_fusion.6), channel_id=1, source_target_pairs={{0,24},{1,25},{2,26},{3,27},{4,28},{5,29},{6,30},{7,31},{8,16},{9,... | collective-permute-start | bytes 331784 | tf_op jit(solution)/shard_map/ppermute | solution.py:43
  58.6 9.9 %collective-permute-start.17 = (bf16[4,48,768]{2,1,0:T(8,128)(2,1)S(1)}, bf16[4,48,768]{2,1,0:T(8,128)(2,1)S(1)}, u32[]{:S(2)}, u32[]{:S(2)}) collective-permute-start(bf16[4,48,768]{2,1,0:T(8,128)(2,1)S(1)} %pad_maximum_fusion.2), channel_id=1, source_target_pairs={{0,2},{1,3},{2,0},{3,1},{4,6},{5,7},{6,4},{7,5},{8,10},{9,11},{10,... | collective-permute-start | bytes 884744 | tf_op jit(solution)/shard_map/ppermute | solution.py:43
  59.1 17.1 %collective-permute-start.33 = (bf16[4,48,1152]{2,1,0:T(8,128)(2,1)S(1)}, bf16[4,48,1152]{2,1,0:T(8,128)(2,1)S(1)}, u32[]{:S(2)}, u32[]{:S(2)}) collective-permute-start(bf16[4,48,1152]{2,1,0:T(8,128)(2,1)S(1)} %pad_maximum_fusion), channel_id=1, source_target_pairs={{0,2},{1,3},{2,0},{3,1},{4,6},{5,7},{6,4},{7,5},{8,10},{9,11},{10,... | collective-permute-start | bytes 1327112 | tf_op jit(solution)/shard_map/ppermute | solution.py:43
  68.6 13.8 %collective-permute-start.18 = (bf16[8,48,768]{2,1,0:T(8,128)(2,1)S(1)}, bf16[8,48,768]{2,1,0:T(8,128)(2,1)}, u32[]{:S(2)}, u32[]{:S(2)}) collective-permute-start(bf16[8,48,768]{2,1,0:T(8,128)(2,1)S(1)} %constant_dynamic-update-slice_fusion.5.refs_0_.refs_14_), channel_id=1, source_target_pairs={{0,4},{1,5},{2,6},{3,7},{4,0},{5,1},{6,2},{7,3},{8,12},{9,13},{10,... | collective-permute-start | bytes 1769480 | tf_op jit(solution)/shard_map/ppermute | solution.py:43
  70.2 9.2 %collective-permute-start.10 = (bf16[8,48,384]{2,1,0:T(8,128)(2,1)S(1)}, bf16[8,48,384]{2,1,0:T(8,128)(2,1)S(1)}, u32[]{:S(2)}, u32[]{:S(2)}) collective-permute-start(bf16[8,48,384]{2,1,0:T(8,128)(2,1)S(1)} %constant_dynamic-update-slice_fusion.refs_0_.refs_10_), channel_id=1, source_target_pairs={{0,2},{1,3},{2,0},{3,1},{4,6},{5,7},{6,4},{7,5},{8,10},{9,11},{10,... | collective-permute-start | bytes 884744 | tf_op jit(solution)/shard_map/ppermute | solution.py:43
  70.8 8.6 %collective-permute-start.39 = (bf16[144,384]{1,0:T(8,128)(2,1)S(1)}, bf16[144,384]{1,0:T(8,128)(2,1)S(1)}, u32[]{:S(2)}, u32[]{:S(2)}) collective-permute-start(bf16[144,384]{1,0:T(8,128)(2,1)S(1)} %maximum_select_fusion.6), channel_id=1, source_target_pairs={{0,8},{1,9},{2,10},{3,11},{4,12},{5,13},{6,14},{7,15},{8,0},{9,1},... | collective-permute-start | bytes 331784 | tf_op jit(solution)/shard_map/ppermute | solution.py:43
  76.3 9.5 %collective-permute-start.26 = (bf16[8,48,384]{2,1,0:T(8,128)(2,1)S(1)}, bf16[8,48,384]{2,1,0:T(8,128)(2,1)S(1)}, u32[]{:S(2)}, u32[]{:S(2)}) collective-permute-start(bf16[8,48,384]{2,1,0:T(8,128)(2,1)S(1)} %constant_dynamic-update-slice_fusion.10.refs_11_), channel_id=1, source_target_pairs={{0,2},{1,3},{2,0},{3,1},{4,6},{5,7},{6,4},{7,5},{8,10},{9,11},{10,... | collective-permute-start | bytes 884744 | tf_op jit(solution)/shard_map/ppermute | solution.py:43
  79.4 7.9 %collective-permute-start.12 = (bf16[8,48,384]{2,1,0:T(8,128)(2,1)S(1)}, bf16[8,48,384]{2,1,0:T(8,128)(2,1)S(1)}, u32[]{:S(2)}, u32[]{:S(2)}) collective-permute-start(bf16[8,48,384]{2,1,0:T(8,128)(2,1)S(1)} %collective-permute-done.10.refs_1_.refs_11_), channel_id=1, source_target_pairs={{0,1},{1,0},{2,3},{3,2},{4,5},{5,4},{6,7},{7,6},{8,9},{9,8},{10,11... | collective-permute-start | bytes 884744 | tf_op jit(solution)/shard_map/ppermute | solution.py:43
  79.4 35.4 %collective-permute-start.34 = (bf16[8,48,1152]{2,1,0:T(8,128)(2,1)S(1)}, bf16[8,48,1152]{2,1,0:T(8,128)(2,1)S(1)}, u32[]{:S(2)}, u32[]{:S(2)}) collective-permute-start(bf16[8,48,1152]{2,1,0:T(8,128)(2,1)S(1)} %constant_dynamic-update-slice_fusion.15.refs_15_), channel_id=1, source_target_pairs={{0,4},{1,5},{2,6},{3,7},{4,0},{5,1},{6,2},{7,3},{8,12},{9,13},{10,... | collective-permute-start | bytes 2654216 | tf_op jit(solution)/shard_map/ppermute | solution.py:43
  82.2 32.2 %collective-permute-start.19 = (bf16[8,48,768]{2,1,0:T(8,128)(2,1)S(1)}, bf16[8,48,768]{2,1,0:T(8,128)(2,1)}, u32[]{:S(2)}, u32[]{:S(2)}) collective-permute-start(bf16[8,48,768]{2,1,0:T(8,128)(2,1)S(1)} %constant_dynamic-update-slice_fusion.5.refs_0_.refs_14_), channel_id=1, source_target_pairs={{0,1},{1,0},{2,3},{3,2},{4,5},{5,4},{6,7},{7,6},{8,9},{9,8},{10,11... | collective-permute-start | bytes 1769480 | tf_op jit(solution)/shard_map/ppermute | solution.py:43
  82.4 32.6 %collective-permute-start.20 = (bf16[8,48,768]{2,1,0:T(8,128)(2,1)}, bf16[8,48,768]{2,1,0:T(8,128)(2,1)}, u32[]{:S(2)}, u32[]{:S(2)}) collective-permute-start(bf16[8,48,768]{2,1,0:T(8,128)(2,1)} %collective-permute-done.18.refs_1_.refs_15_), channel_id=1, source_target_pairs={{0,1},{1,0},{2,3},{3,2},{4,5},{5,4},{6,7},{7,6},{8,9},{9,8},{10,11... | collective-permute-start | bytes 1769480 | tf_op jit(solution)/shard_map/ppermute | solution.py:43
  85.8 28.5 %collective-permute-start.42 = (bf16[4,144,384]{2,1,0:T(8,128)(2,1)S(1)}, bf16[4,144,384]{2,1,0:T(8,128)(2,1)}, u32[]{:S(2)}, u32[]{:S(2)}) collective-permute-start(bf16[4,144,384]{2,1,0:T(8,128)(2,1)S(1)} %pad_maximum_fusion.1.refs_19_.refs_18_), channel_id=1, source_target_pairs={{0,4},{1,5},{2,6},{3,7},{4,0},{5,1},{6,2},{7,3},{8,12},{9,13},{10,... | collective-permute-start | bytes 1327112 | tf_op jit(solution)/shard_map/ppermute | solution.py:43
  88.1 25.7 %collective-permute-start.27 = (bf16[8,48,384]{2,1,0:T(8,128)(2,1)S(1)}, bf16[8,48,384]{2,1,0:T(8,128)(2,1)}, u32[]{:S(2)}, u32[]{:S(2)}) collective-permute-start(bf16[8,48,384]{2,1,0:T(8,128)(2,1)S(1)} %constant_dynamic-update-slice_fusion.10.refs_11_), channel_id=1, source_target_pairs={{0,1},{1,0},{2,3},{3,2},{4,5},{5,4},{6,7},{7,6},{8,9},{9,8},{10,11... | collective-permute-start | bytes 884744 | tf_op jit(solution)/shard_map/ppermute | solution.py:43
  113.8 47.4 %collective-permute-start.43 = (bf16[4,144,384]{2,1,0:T(8,128)(2,1)S(1)}, bf16[4,144,384]{2,1,0:T(8,128)(2,1)S(1)}, u32[]{:S(2)}, u32[]{:S(2)}) collective-permute-start(bf16[4,144,384]{2,1,0:T(8,128)(2,1)S(1)} %pad_maximum_fusion.1.refs_19_.refs_18_), channel_id=1, source_target_pairs={{0,1},{1,0},{2,3},{3,2},{4,5},{5,4},{6,7},{7,6},{8,9},{9,8},{10,11... | collective-permute-start | bytes 1327112 | tf_op jit(solution)/shard_map/ppermute | solution.py:43
  114.3 46.9 %collective-permute-start.28 = (bf16[8,48,384]{2,1,0:T(8,128)(2,1)}, bf16[8,48,384]{2,1,0:T(8,128)(2,1)S(1)}, u32[]{:S(2)}, u32[]{:S(2)}) collective-permute-start(bf16[8,48,384]{2,1,0:T(8,128)(2,1)} %copy-done.23), channel_id=1, source_target_pairs={{0,1},{1,0},{2,3},{3,2},{4,5},{5,4},{6,7},{7,6},{8,9},{9,8},{10,11... | collective-permute-start | bytes 884744 | tf_op jit(solution)/shard_map/ppermute | solution.py:43
  114.4 46.8 %collective-permute-start.35 = (bf16[8,48,1152]{2,1,0:T(8,128)(2,1)S(1)}, bf16[8,48,1152]{2,1,0:T(8,128)(2,1)S(1)}, u32[]{:S(2)}, u32[]{:S(2)}) collective-permute-start(bf16[8,48,1152]{2,1,0:T(8,128)(2,1)S(1)} %constant_dynamic-update-slice_fusion.15.refs_15_), channel_id=1, source_target_pairs={{0,1},{1,0},{2,3},{3,2},{4,5},{5,4},{6,7},{7,6},{8,9},{9,8},{10,11... | collective-permute-start | bytes 2654216 | tf_op jit(solution)/shard_map/ppermute | solution.py:43
  114.8 46.4 %collective-permute-start.44 = (bf16[4,144,384]{2,1,0:T(8,128)(2,1)}, bf16[4,144,384]{2,1,0:T(8,128)(2,1)}, u32[]{:S(2)}, u32[]{:S(2)}) collective-permute-start(bf16[4,144,384]{2,1,0:T(8,128)(2,1)} %collective-permute-done.42.refs_20_.refs_19_), channel_id=1, source_target_pairs={{0,1},{1,0},{2,3},{3,2},{4,5},{5,4},{6,7},{7,6},{8,9},{9,8},{10,11... | collective-permute-start | bytes 1327112 | tf_op jit(solution)/shard_map/ppermute | solution.py:43
  114.9 46.3 %collective-permute-start.36 = (bf16[8,48,1152]{2,1,0:T(8,128)(2,1)S(1)}, bf16[8,48,1152]{2,1,0:T(8,128)(2,1)}, u32[]{:S(2)}, u32[]{:S(2)}) collective-permute-start(bf16[8,48,1152]{2,1,0:T(8,128)(2,1)S(1)} %collective-permute-done.34.refs_16_), channel_id=1, source_target_pairs={{0,1},{1,0},{2,3},{3,2},{4,5},{5,4},{6,7},{7,6},{8,9},{9,8},{10,11... | collective-permute-start | bytes 2654216 | tf_op jit(solution)/shard_map/ppermute | solution.py:43
  313.1 34.9 %collective-permute-start.52 = (bf16[16,48,768]{2,1,0:T(8,128)(2,1)}, bf16[16,48,768]{2,1,0:T(8,128)(2,1)S(1)}, u32[]{:S(2)}, u32[]{:S(2)}) collective-permute-start(bf16[16,48,768]{2,1,0:T(8,128)(2,1)} %get-tuple-element.54), channel_id=1, source_target_pairs={{0,1},{1,0},{2,3},{3,2},{4,5},{5,4},{6,7},{7,6},{8,9},{9,8},{10,11... | collective-permute-start | bytes 3538952 | tf_op jit(solution)/shard_map/ppermute | solution.py:43
  313.6 58.7 %collective-permute-start.66 = (bf16[16,48,1152]{2,1,0:T(8,128)(2,1)}, bf16[16,48,1152]{2,1,0:T(8,128)(2,1)}, u32[]{:S(2)}, u32[]{:S(2)}) collective-permute-start(bf16[16,48,1152]{2,1,0:T(8,128)(2,1)} %get-tuple-element.58), channel_id=1, source_target_pairs={{0,1},{1,0},{2,3},{3,2},{4,5},{5,4},{6,7},{7,6},{8,9},{9,8},{10,11... | collective-permute-start | bytes 5308424 | tf_op jit(solution)/shard_map/ppermute | solution.py:43
  315.8 17.8 %collective-permute-start.73 = (bf16[8,144,384]{2,1,0:T(8,128)(2,1)}, bf16[8,144,384]{2,1,0:T(8,128)(2,1)S(1)}, u32[]{:S(2)}, u32[]{:S(2)}) collective-permute-start(bf16[8,144,384]{2,1,0:T(8,128)(2,1)} %get-tuple-element.60), channel_id=1, source_target_pairs={{0,1},{1,0},{2,3},{3,2},{4,5},{5,4},{6,7},{7,6},{8,9},{9,8},{10,11... | collective-permute-start | bytes 2654216 | tf_op jit(solution)/shard_map/ppermute | solution.py:43
  317.2 9.8 %collective-permute-start.46 = (bf16[8,48,384]{2,1,0:T(8,128)(2,1)S(1)}, bf16[8,48,384]{2,1,0:T(8,128)(2,1)S(1)}, u32[]{:S(2)}, u32[]{:S(2)}) collective-permute-start(bf16[8,48,384]{2,1,0:T(8,128)(2,1)S(1)} %get-tuple-element.80), channel_id=1, source_target_pairs={{0,2},{1,3},{2,0},{3,1},{4,6},{5,7},{6,4},{7,5},{8,10},{9,11},{10,... | collective-permute-start | bytes 884744 | tf_op jit(solution)/shard_map/ppermute | solution.py:43
  319.8 13.1 %collective-permute-start.60 = (bf16[8,48,384]{2,1,0:T(8,128)(2,1)S(1)}, bf16[8,48,384]{2,1,0:T(8,128)(2,1)S(1)}, u32[]{:S(2)}, u32[]{:S(2)}) collective-permute-start(bf16[8,48,384]{2,1,0:T(8,128)(2,1)S(1)} %get-tuple-element.78), channel_id=1, source_target_pairs={{0,2},{1,3},{2,0},{3,1},{4,6},{5,7},{6,4},{7,5},{8,10},{9,11},{10,... | collective-permute-start | bytes 884744 | tf_op jit(solution)/shard_map/ppermute | solution.py:43
  345.5 12.7 %collective-permute-start.74 = (bf16[4,144,384]{2,1,0:T(8,128)(2,1)S(1)}, bf16[4,144,384]{2,1,0:T(8,128)(2,1)S(1)}, u32[]{:S(2)}, u32[]{:S(2)}) collective-permute-start(bf16[4,144,384]{2,1,0:T(8,128)(2,1)S(1)} %add_convert_fusion.5), channel_id=1, source_target_pairs={{0,4},{1,5},{2,6},{3,7},{4,0},{5,1},{6,2},{7,3},{8,12},{9,13},{10,... | collective-permute-start | bytes 1327112 | tf_op jit(solution)/shard_map/ppermute | solution.py:43
  347.3 13.4 %collective-permute-start.51 = (f32[24,384]{1,0:T(8,128)S(1)}, f32[24,384]{1,0:T(8,128)}, u32[]{:S(2)}, u32[]{:S(2)}) collective-permute-start(f32[24,384]{1,0:T(8,128)S(1)} %get-tuple-element.106), channel_id=1, source_target_pairs={{0,1},{1,0},{2,3},{3,2},{4,5},{5,4},{6,7},{7,6},{8,9},{9,8},{10,11... | collective-permute-start | bytes 110600 | tf_op jit(solution)/shard_map/ppermute | solution.py:43
  347.4 13.4 %collective-permute-start.65 = (f32[24,384]{1,0:T(8,128)S(1)}, f32[24,384]{1,0:T(8,128)S(1)}, u32[]{:S(2)}, u32[]{:S(2)}) collective-permute-start(f32[24,384]{1,0:T(8,128)S(1)} %get-tuple-element.104), channel_id=1, source_target_pairs={{0,1},{1,0},{2,3},{3,2},{4,5},{5,4},{6,7},{7,6},{8,9},{9,8},{10,11... | collective-permute-start | bytes 110600 | tf_op jit(solution)/shard_map/ppermute | solution.py:43
  349.1 20.8 %collective-permute-start.53 = (bf16[8,48,768]{2,1,0:T(8,128)(2,1)}, bf16[8,48,768]{2,1,0:T(8,128)(2,1)}, u32[]{:S(2)}, u32[]{:S(2)}) collective-permute-start(bf16[8,48,768]{2,1,0:T(8,128)(2,1)} %get-tuple-element.76), channel_id=1, source_target_pairs={{0,4},{1,5},{2,6},{3,7},{4,0},{5,1},{6,2},{7,3},{8,12},{9,13},{10,... | collective-permute-start | bytes 1769480 | tf_op jit(solution)/shard_map/ppermute | solution.py:43
  374.2 16.2 %collective-permute-start.67 = (bf16[8,48,1152]{2,1,0:T(8,128)(2,1)S(1)}, bf16[8,48,1152]{2,1,0:T(8,128)(2,1)S(1)}, u32[]{:S(2)}, u32[]{:S(2)}) collective-permute-start(bf16[8,48,1152]{2,1,0:T(8,128)(2,1)S(1)} %get-tuple-element.74), channel_id=1, source_target_pairs={{0,4},{1,5},{2,6},{3,7},{4,0},{5,1},{6,2},{7,3},{8,12},{9,13},{10,... | collective-permute-start | bytes 2654216 | tf_op jit(solution)/shard_map/ppermute | solution.py:43
  375.4 16.2 %collective-permute-start.79 = (f32[36,384]{1,0:T(8,128)S(1)}, f32[36,384]{1,0:T(8,128)S(1)}, u32[]{:S(2)}, u32[]{:S(2)}) collective-permute-start(f32[36,384]{1,0:T(8,128)S(1)} %get-tuple-element.100), channel_id=1, source_target_pairs={{0,1},{1,0},{2,3},{3,2},{4,5},{5,4},{6,7},{7,6},{8,9},{9,8},{10,11... | collective-permute-start | bytes 165896 | tf_op jit(solution)/shard_map/ppermute | solution.py:43
  378.8 12.6 %collective-permute-start.57 = (bf16[48,768]{1,0:T(8,128)(2,1)S(1)}, bf16[48,768]{1,0:T(8,128)(2,1)S(1)}, u32[]{:S(2)}, u32[]{:S(2)}) collective-permute-start(bf16[48,768]{1,0:T(8,128)(2,1)S(1)} %get-tuple-element.88), channel_id=1, source_target_pairs={{0,24},{1,25},{2,26},{3,27},{4,28},{5,29},{6,30},{7,31},{8,16},{9,... | collective-permute-start | bytes 221192 | tf_op jit(solution)/shard_map/ppermute | solution.py:43
  381.4 10.0 %collective-permute-start.56 = (bf16[48,768]{1,0:T(8,128)(2,1)S(1)}, bf16[48,768]{1,0:T(8,128)(2,1)S(1)}, u32[]{:S(2)}, u32[]{:S(2)}) collective-permute-start(bf16[48,768]{1,0:T(8,128)(2,1)S(1)} %get-tuple-element.89), channel_id=1, source_target_pairs={{0,16},{1,17},{2,18},{3,19},{4,20},{5,21},{6,22},{7,23},{8,24},{9,... | collective-permute-start | bytes 221192 | tf_op jit(solution)/shard_map/ppermute | solution.py:43
  381.7 9.7 %collective-permute-start.55 = (bf16[48,768]{1,0:T(8,128)(2,1)S(1)}, bf16[48,768]{1,0:T(8,128)(2,1)S(1)}, u32[]{:S(2)}, u32[]{:S(2)}) collective-permute-start(bf16[48,768]{1,0:T(8,128)(2,1)S(1)} %get-tuple-element.87), channel_id=1, source_target_pairs={{0,8},{1,9},{2,10},{3,11},{4,12},{5,13},{6,14},{7,15},{8,0},{9,1},... | collective-permute-start | bytes 221192 | tf_op jit(solution)/shard_map/ppermute | solution.py:43
  390.5 8.4 %collective-permute-start.68 = (bf16[4,48,1152]{2,1,0:T(8,128)(2,1)S(1)}, bf16[4,48,1152]{2,1,0:T(8,128)(2,1)S(1)}, u32[]{:S(2)}, u32[]{:S(2)}) collective-permute-start(bf16[4,48,1152]{2,1,0:T(8,128)(2,1)S(1)} %add_convert_fusion.8), channel_id=1, source_target_pairs={{0,2},{1,3},{2,0},{3,1},{4,6},{5,7},{6,4},{7,5},{8,10},{9,11},{10,... | collective-permute-start | bytes 1327112 | tf_op jit(solution)/shard_map/ppermute | solution.py:43
  (62 other events, 645.6 us)

commit v2 on v1

v2 whole, which is shorter than its diff:
```python
import functools

import jax
import jax.numpy as jnp
import numpy as np
from jax import lax
from jax.experimental import pallas as pl
from jax.experimental.pallas import tpu as pltpu
from jax.sharding import PartitionSpec as P

D = 768
HEADS = 12
HEAD = 64
FF = 1152
WIN = 128
LEN = 512
PAIR = 2 * HEAD
PAIRS = HEADS // 2
BLOCK = 128
SPAN = 2 * BLOCK
BLOCKS = LEN // BLOCK
STARTS = tuple(min(max(BLOCK * i - WIN // 2, 0), LEN - SPAN) for i in range(BLOCKS))
GROUPS = 3
EACH = PAIRS // GROUPS
WIDTH = EACH * 3 * PAIR
CORE, ALONG_X, ALONG_Y, ALONG_Z = 1, 2, 4, 8
NOWHERE = (0, 0, 0, 0, 0, 0, 0)
VMEM_LIMIT = 60 * 1024 * 1024
f32 = jnp.float32
bf16 = jnp.bfloat16


def dot_nn(left, right):
    return lax.dot_general(left, right, (((1,), (0,)), ((), ())), preferred_element_type=f32)


def dot_nt(left, right):
    return lax.dot_general(left, right, (((1,), (1,)), ((), ())), preferred_element_type=f32)


def dot_tn(left, right):
    return lax.dot_general(left, right, (((0,), (0,)), ((), ())), preferred_element_type=f32)


def swap(values, bits):
    return lax.ppermute(values, "fsdp", [(i, i ^ bits) for i in range(32)])


def bit_of(bits):
    return (lax.axis_index("fsdp") & bits) != 0


def ordered(bits, mine, other, axis):
    return jnp.where(
        bit_of(bits), jnp.concatenate([other, mine], axis), jnp.concatenate([mine, other], axis)
    )


def after(values, token):
    return jnp.where(token[(0,) * token.ndim].astype(f32) < jnp.inf, values, jnp.zeros_like(values))


def split_columns(shard):
    half = shard.shape[1] // 2
    low, high = shard[:, :half], shard[:, half:]
    other = swap(jnp.where(bit_of(CORE), low, high), CORE)
    return ordered(CORE, jnp.where(bit_of(CORE), high, low), other, 0)


def along_line(own):
    return jnp.stack([own] + [swap(own, ALONG_Z * j) for j in (1, 2, 3)])


def chip_flips(count, first, second):
    return [ALONG_Z * (at % 4) | first * (at // 4 % 2) | second * (at // 8) for at in range(count)]


def swap_half(values, bits):
    half = values.shape[0] // 2
    low, high = values[:half], values[half:]
    other = swap(jnp.where(bit_of(bits), low, high), bits)
    return jnp.where(bit_of(bits), high, low), other


def joined_sum(kept, received):
    return (kept.astype(f32) + received.astype(f32)).astype(bf16)


def halved(kept, received):
    half = kept.shape[0] // 2
    return (
        joined_sum(kept[:half], received[:half]),
        joined_sum(kept[half:], received[half:]),
    )


def summed_line(line):
    total = line[0].astype(f32)
    for j in (1, 2, 3):
        total = total + swap(line[j], ALONG_Z * j).astype(f32)
    return total


def join_columns(total):
    rows = total.shape[0] // 2
    low, high = total[:rows], total[rows:]
    other = swap(jnp.where(bit_of(CORE), low, high), CORE)
    return jnp.where(bit_of(CORE), high, low), other


def both_columns(joined, start, stop):
    mine, other = joined
    return ordered(CORE, mine[:, start:stop], other[:, start:stop], 1)


def place(me_ref, spot):
    flips, shift, rows, row, side, columns, column = spot
    me = me_ref[0]
    return (
        pl.multiple_of(((me ^ flips) >> shift) * rows + row, 16),
        pl.multiple_of(((me & 1) ^ side) * columns + column, 128),
    )


def load_pieces(me_ref, loads, spots, arrays, weights, sem):
    copies = []
    for at, (array, block, start, width, weight) in enumerate(loads):
        piece = arrays[array].at[block, :, pl.ds(start, width)]
        rows = arrays[array].shape[1]
        row, column = place(me_ref, spots[at])
        copy = pltpu.make_async_copy(piece, weights[weight].at[pl.ds(row, rows), pl.ds(column, width)], sem)
        copy.start()
        copies.append(copy)
    return copies


def store_blocks(me_ref, spots, total, outs):
    at = 0
    for out in outs:
        blocks, rows, columns = out.shape
        for block in range(blocks):
            row, column = place(me_ref, spots[at])
            out[block] = total[pl.ds(row, rows), pl.ds(column, columns)].astype(bf16)
            at += 1


def turn(values, tables, sign):
    cosine, sine_up, sine_down = tables
    up = pltpu.roll(values, HEAD // 2, 1)
    down = pltpu.roll(values, PAIR - HEAD // 2, 1)
    if sign > 0:
        return values * cosine + (up * sine_up + down * sine_down)
    return values * cosine - (up * sine_up + down * sine_down)


def norm_of(values):
    centered = values - jnp.mean(values, axis=-1, keepdims=True)
    spread = jnp.mean(centered * centered, axis=-1, keepdims=True)
    scale = lax.rsqrt(spread + 1e-05)
    return centered * scale, scale


def norm_back(grad, normed, scale):
    return scale * (
        grad
        - jnp.mean(grad, axis=-1, keepdims=True)
        - normed * jnp.mean(grad * normed, axis=-1, keepdims=True)
    )


def band(block):
    key = lax.broadcasted_iota(jnp.int32, (SPAN, SPAN), 0) + STARTS[block]
    query = lax.broadcasted_iota(jnp.int32, (SPAN, SPAN), 1) % BLOCK + block * BLOCK
    return jnp.abs(key - query) <= WIN // 2


def both_heads(values, masks_ref):
    return jnp.concatenate([values * masks_ref[0:1, :], values * masks_ref[1:2, :]], axis=0)


def apart(turned):
    nothing = jnp.zeros((HEAD, turned.shape[1]), turned.dtype)
    first = jnp.concatenate([turned[:HEAD], nothing], axis=0)
    second = jnp.concatenate([nothing, turned[HEAD:]], axis=0)
    return jnp.concatenate([first, second], axis=1)


def one_of_each(stacked):
    return jnp.concatenate([stacked[:HEAD, :BLOCK], stacked[HEAD:, BLOCK:]], axis=0)


def turned_windows(values):
    straight = values.T
    shifted = values[STARTS[1] : LEN - STARTS[1]].T
    return [
        straight[:, :SPAN],
        shifted[:, :SPAN],
        shifted[:, BLOCK : BLOCK + SPAN],
        straight[:, LEN - SPAN :],
    ]


def staggered(tiles, first, second, third):
    ones, twos = {}, {}
    for at in range(len(tiles) + 2):
        if at < len(tiles):
            ones[at] = first(*tiles[at])
        if 1 <= at <= len(tiles):
            twos[at - 1] = second(*tiles[at - 1], ones.pop(at - 1))
        if at >= 2:
            third(*tiles[at - 2], twos.pop(at - 2))


def forward_kernel(loads, spots, arrays_n, me_ref, rows_ref, gain_ref, tables_ref, masks_ref, *refs):
    arrays = refs[:arrays_n]
    qkv_ref, probs_ref, mix_ref, *normed_ref, weight, bias, sem = refs[arrays_n:]

    @pl.when(pl.program_id(0) == 0)
    def _():
        copies = load_pieces(me_ref, loads, spots, arrays, [weight], sem)
        for block in range(3):
            bias[block] = jnp.where(band(block if block < 2 else BLOCKS - 1), 0.0, -1e30)
        for copy in copies:
            copy.wait()

    if normed_ref:
        normed, _ = norm_of(rows_ref[...].astype(f32))
        normed_ref[0][...] = (normed * gain_ref[...]).astype(bf16)
        rows_ref = normed_ref[0]
    tables = (tables_ref[0], tables_ref[1], tables_ref[2])

    projected = dot_nn(rows_ref[...], weight[...])
    for pair in range(EACH):
        column = pair * 3 * PAIR
        queries = turn(projected[:, column : column + PAIR], tables, 1)
        key_rows = turn(projected[:, column + PAIR : column + 2 * PAIR], tables, 1)
        qkv_ref[:, column : column + PAIR] = queries.astype(bf16) * bf16(HEAD**-0.5)
        qkv_ref[:, column + PAIR : column + 2 * PAIR] = key_rows.astype(bf16)
        qkv_ref[:, column + 2 * PAIR : column + 3 * PAIR] = projected[
            :, column + 2 * PAIR : column + 3 * PAIR
        ].astype(bf16)

    turned_queries, values = [], []
    for pair in range(EACH):
        column = pair * 3 * PAIR
        turned_queries.append(qkv_ref[:, column : column + PAIR].T)
        values.append(turned_windows(qkv_ref[:, column + 2 * PAIR : column + 3 * PAIR]))
    mixed = [[None] * BLOCKS for _ in range(EACH)]

    def score(pair, block):
        key_column = pair * 3 * PAIR + PAIR
        rows = slice(block * BLOCK, (block + 1) * BLOCK)
        window = slice(STARTS[block], STARTS[block] + SPAN)
        return dot_nn(qkv_ref[window, key_column : key_column + PAIR], apart(turned_queries[pair][:, rows]))

    def weigh(pair, block, scores):
        scores = scores + bias[0 if block == 0 else (2 if block == BLOCKS - 1 else 1)]
        raised = jnp.exp(scores - jnp.max(scores, axis=0, keepdims=True))
        probs = (raised * (1.0 / jnp.sum(raised, axis=0, keepdims=True))).astype(bf16)
        probs_ref[0, 0, pair, block] = probs
        return probs

    def mix(pair, block, probs):
        mixed[pair][block] = one_of_each(dot_nn(values[pair][block], probs)).astype(bf16)
        if block == BLOCKS - 1:
            mix_ref[:, pair * PAIR : (pair + 1) * PAIR] = jnp.concatenate(mixed[pair], axis=1).T

    staggered([(pair, block) for pair in range(EACH) for block in range(BLOCKS)], score, weigh, mix)


def feed_kernel(loads, spots, arrays_n, backs, *refs):
    refs = list(refs)
    take = lambda n: [refs.pop(0) for _ in range(n)]
    (me_ref,) = take(1)
    tokens_ref, cot_ref, gain_ref = take(3)
    (mix_ref,) = take(1)
    arrays = take(arrays_n)
    hidden_ref, gated_ref, grad_hidden_ref = take(3)
    (grad_mix_ref,) = take(1)
    (gain_grad_ref,) = take(1)
    out_grads, in_grads, mlp_grads = (take(len(back[1])) for back in backs)
    w_out, w_in, w_mlp, t_out, t_in, t_mlp, sem = refs
    step = pl.program_id(0)

    @pl.when(step == 0)
    def _():
        copies = load_pieces(me_ref, loads, spots, arrays, [w_out, w_in, w_mlp], sem)
        t_out[...] = jnp.zeros_like(t_out)
        t_in[...] = jnp.zeros_like(t_in)
        t_mlp[...] = jnp.zeros_like(t_mlp)
        gain_grad_ref[...] = jnp.zeros_like(gain_grad_ref)
        for copy in copies:
            copy.wait()

    mixed = mix_ref[...]
    cot = cot_ref[...]
    hidden = tokens_ref[...].astype(f32) + dot_nn(mixed, w_out[...])
    hidden_ref[...] = hidden
    normed, scale = norm_of(hidden)
    gain = gain_ref[...]
    normed_mlp = (normed * gain).astype(bf16)
    grad_gated = dot_nt(cot, w_mlp[...])
    entry = dot_nn(normed_mlp, w_in[:, :FF])
    gate = dot_nn(normed_mlp, w_in[:, FF:])
    below = 0.5 * (1.0 + lax.erf(entry * 0.7071067811865476))
    density = jnp.exp(-0.5 * entry * entry) * 0.3989422804014327
    unit = entry * below
    gated = (unit * gate).astype(bf16)
    gated_ref[...] = gated
    grad_entry = ((below + entry * density) * (gate * grad_gated)).astype(bf16)
    grad_gate = (unit * grad_gated).astype(bf16)
    t_mlp[...] += dot_tn(gated, cot)
    turned = normed_mlp.T
    t_in[:, :FF] += dot_nn(turned, grad_entry)
    t_in[:, FF:] += dot_nn(turned, grad_gate)
    grad_normed = dot_nt(grad_entry, w_in[:, :FF]) + dot_nt(grad_gate, w_in[:, FF:])
    gain_grad_ref[...] += jnp.sum(grad_normed * normed, axis=0, keepdims=True)
    grad_hidden = cot.astype(f32) + norm_back(grad_normed * gain, normed, scale)
    grad_hidden_ref[...] = grad_hidden
    grad_out = grad_hidden.astype(bf16)
    t_out[...] += dot_tn(mixed, grad_out)
    grad_mix_ref[...] = dot_nt(grad_out, w_out[...]).astype(bf16)

    @pl.when(step == pl.num_programs(0) - 1)
    def _():
        store_blocks(me_ref, backs[0][0], t_out, out_grads)
        store_blocks(me_ref, backs[1][0], t_in, in_grads)
        store_blocks(me_ref, backs[2][0], t_mlp, mlp_grads)


def backward_kernel(
    spots, outs_n, me_ref, normed_ref, qkv_ref, probs_ref, grad_mix_ref, tables_ref, masks_ref, *refs
):
    grad_ref = refs[0]
    outs = refs[1 : 1 + outs_n]
    total, grad_keys, grad_values = refs[1 + outs_n :]
    step = pl.program_id(0)

    @pl.when(step == 0)
    def _():
        total[...] = jnp.zeros_like(total)

    tables = (tables_ref[0], tables_ref[1], tables_ref[2])

    grad_keys[...] = jnp.zeros_like(grad_keys)
    grad_values[...] = jnp.zeros_like(grad_values)
    turned_grads, turned_keys = [], []
    for pair in range(EACH):
        column = pair * 3 * PAIR + PAIR
        turned_grads.append(grad_mix_ref[:, pair * PAIR : (pair + 1) * PAIR].T)
        turned_keys.append(turned_windows(qkv_ref[:, column : column + PAIR]))
    grad_queries = [[None] * BLOCKS for _ in range(EACH)]

    def soften(pair, block):
        column = pair * 3 * PAIR + 2 * PAIR
        rows = slice(block * BLOCK, (block + 1) * BLOCK)
        window = slice(STARTS[block], STARTS[block] + SPAN)
        return dot_nn(qkv_ref[window, column : column + PAIR], apart(turned_grads[pair][:, rows]))

    def score(pair, block, grad_soft):
        soft = probs_ref[0, 0, pair, block].astype(f32)
        inner = jnp.sum(soft * grad_soft, axis=0, keepdims=True)
        return (soft * (grad_soft - inner)).astype(bf16)

    def spread(pair, block, grad_scores):
        column = pair * 3 * PAIR
        own = slice(pair * PAIR, (pair + 1) * PAIR)
        rows = slice(block * BLOCK, (block + 1) * BLOCK)
        window = slice(STARTS[block], STARTS[block] + SPAN)
        queries = both_heads(qkv_ref[rows, column : column + PAIR], masks_ref)
        grad_mix = both_heads(grad_mix_ref[rows, own], masks_ref)
        grad_values[window, own] += dot_nn(probs_ref[0, 0, pair, block], grad_mix)
        grad_keys[window, own] += dot_nn(grad_scores, queries)
        grad_queries[pair][block] = one_of_each(dot_nn(turned_keys[pair][block], grad_scores))
        if block == BLOCKS - 1:
            turned = jnp.concatenate(grad_queries[pair], axis=1).T * HEAD**-0.5
            grad_ref[:, column : column + PAIR] = turn(turned, tables, -1).astype(bf16)
            grad_ref[:, column + PAIR : column + 2 * PAIR] = turn(grad_keys[:, own], tables, -1).astype(bf16)
            grad_ref[:, column + 2 * PAIR : column + 3 * PAIR] = grad_values[:, own].astype(bf16)

    staggered([(pair, block) for pair in range(EACH) for block in range(BLOCKS)], soften, score, spread)
    total[...] += dot_tn(normed_ref[...], grad_ref[...])

    @pl.when(step == pl.num_programs(0) - 1)
    def _():
        store_blocks(me_ref, spots, total, outs)


def final_kernel(loads, spots, arrays_n, me_ref, tokens_ref, gain_ref, grad_hidden_ref, grad_ref, *refs):
    arrays = refs[:arrays_n]
    tokens_grad_ref, gain_grad_ref, weight, sem = refs[arrays_n:]

    @pl.when(pl.program_id(0) == 0)
    def _():
        copies = load_pieces(me_ref, loads, spots, arrays, [weight], sem)
        gain_grad_ref[...] = jnp.zeros_like(gain_grad_ref)
        for copy in copies:
            copy.wait()

    grad_normed = dot_nt(grad_ref[...], weight[...])
    normed, scale = norm_of(tokens_ref[...].astype(f32))
    gain_grad_ref[...] += jnp.sum(grad_normed * normed, axis=0, keepdims=True)
    tokens_grad_ref[...] = grad_hidden_ref[...] + norm_back(grad_normed * gain_ref[...], normed, scale)


def output_kernel(loads, spots, arrays_n, me_ref, hidden_ref, gated_ref, *refs):
    arrays = refs[:arrays_n]
    output_ref, weight, sem = refs[-3:]

    @pl.when(pl.program_id(0) == 0)
    def _():
        for copy in load_pieces(me_ref, loads, spots, arrays, [weight], sem):
            copy.wait()

    output_ref[...] = (hidden_ref[...] + dot_nn(gated_ref[...], weight[...])).astype(bf16)


SMEM = pl.BlockSpec(memory_space=pltpu.SMEM)
ANYWHERE = pl.BlockSpec(memory_space=pl.ANY)


def rows_spec(rows, columns):
    return pl.BlockSpec((rows, columns), lambda i: (i, 0))


def whole_spec(*shape):
    return pl.BlockSpec(shape, lambda i: (0,) * len(shape))


def call(kernel, steps, inputs, outputs, scratch, flops, nbytes, waits=(), through=(), into=()):
    extra = list(waits) + list(through) + list(into)
    n_in, n_out, n_through = len(inputs), len(outputs), len(through)
    begin = n_in + len(extra)

    def trimmed(*refs):
        kernel(*refs[:n_in], *refs[begin : begin + n_out], *refs[begin + n_out + n_through :])

    aliases = {n_in + len(waits) + at: n_out + at for at in range(n_through)}
    aliases.update({n_in + len(waits) + n_through + at: at for at in range(len(into))})
    results = pl.pallas_call(
        trimmed,
        grid=(steps,),
        in_specs=[spec for _, spec in inputs] + [ANYWHERE] * len(extra),
        out_specs=[spec for _, _, spec in outputs] + [ANYWHERE] * n_through,
        out_shape=[jax.ShapeDtypeStruct(shape, dtype) for shape, dtype, _ in outputs]
        + [jax.ShapeDtypeStruct(array.shape, array.dtype) for array in through],
        scratch_shapes=scratch,
        input_output_aliases=aliases,
        compiler_params=pltpu.CompilerParams(
            dimension_semantics=("arbitrary",), vmem_limit_bytes=VMEM_LIMIT
        ),
        cost_estimate=pl.CostEstimate(flops=int(flops), bytes_accessed=int(nbytes), transcendentals=0),
    )(*[array for array, _ in inputs], *extra)
    if not through:
        return results
    return results[:n_out], results[n_out:]


def rope_constants():
    inverse = 10000.0 ** (-np.arange(0, HEAD, 2, dtype=np.float64) / HEAD)
    angles = np.arange(LEN, dtype=np.float64)[:, None] * inverse[None, :]
    angles = np.concatenate([angles] * 4, axis=-1)
    upper = (np.arange(PAIR) % HEAD >= HEAD // 2)[None, :]
    sine = np.sin(angles)
    return np.stack([np.cos(angles), np.where(upper, sine, 0.0), np.where(upper, 0.0, -sine)]).astype(
        np.float32
    )


def spread_loads(arrays, flips, start, width, weight, column):
    loads, spots = [], []
    for index, blocks, first_chip, other in arrays:
        for block in range(blocks):
            loads.append((index, block, start, width, weight))
            spots.append((flips[first_chip + block], 1, 48, 0, other, width, column))
    return loads, spots


def gather_weights(qkv_weight, out_weight, in_weight, mlp_weight, norm_gains):
    by_pair = qkv_weight.reshape(24, 3, PAIRS, PAIR).transpose(0, 2, 1, 3).reshape(24, PAIRS, 3 * PAIR)
    gain_row = jnp.pad(norm_gains.reshape(1, 48), ((0, 23), (0, 80)))
    early = split_columns(
        jnp.concatenate([by_pair[:, 0], gain_row, by_pair[:, 1], gain_row], axis=1)
    )
    later = split_columns(
        jnp.concatenate([by_pair[:, 2], by_pair[:, 4], by_pair[:, 3], by_pair[:, 5]], axis=1)
    )
    own_in = split_columns(in_weight.reshape(24, 2 * FF))
    own_out = split_columns(out_weight.reshape(24, D))
    own_mlp = split_columns(mlp_weight.reshape(36, D))
    own_mlp = ordered(ALONG_X, own_mlp, swap(own_mlp, ALONG_X), 0)

    line = along_line(early)
    plane = jnp.concatenate([line, swap(line, ALONG_X)])
    far = swap(plane, ALONG_Y)
    first_arrays = [plane, far, swap(plane, CORE), swap(far, CORE)]
    chips = chip_flips(16, ALONG_X, ALONG_Y)
    slots = [(0, 8, 0, 0), (1, 8, 8, 0), (2, 8, 0, 1), (3, 8, 8, 1)]
    first = (first_arrays, *spread_loads(slots, chips, 0, 3 * PAIR, 0, 0))
    scales = jnp.concatenate([plane, far])[:, :, 3 * PAIR : 3 * PAIR + 48]
    scales = jnp.concatenate([scales[:, 0], scales[:, 24]], axis=1)
    held = (lax.axis_index("fsdp") ^ np.asarray(chips, np.int32)) // 2
    spot = held[None, :] == np.arange(16, dtype=np.int32)[:, None]
    gains = dot_nn(spot.astype(bf16), scales).reshape(-1)

    line = along_line(after(later, line))
    early_plane = plane
    plane = jnp.concatenate([line, swap(line, ALONG_Y)])
    far = swap(plane, ALONG_X)
    other_arrays = [plane, far, swap(plane, CORE), swap(far, CORE)]
    chips = chip_flips(16, ALONG_Y, ALONG_X)
    others = [
        (other_arrays, *spread_loads(slots, chips, 3 * PAIR * at, 3 * PAIR, 0, 0)) for at in range(2)
    ]

    rows = own_mlp.shape[0] // 3
    thirds = [own_mlp[rows * i : rows * (i + 1)] for i in range(3)]
    own = after(jnp.concatenate([own_in, own_out] + thirds, axis=1), early_plane)
    start_out, start_mlp = FF, FF + D // 2
    parts = [own] + [swap(own, ALONG_Z * j) for j in (1, 2, 3)]
    rest_arrays = []

    def near(own_mlp):
        thirds = [own_mlp[rows * i : rows * (i + 1)] for i in range(3)]
        own = jnp.concatenate([own_in, own_out] + thirds, axis=1)
        line = jnp.stack([own] + parts[1:])
        return line, line[:, :, :start_mlp], swap(line, ALONG_Y)

    def far(line, head, beside):
        mlp = jnp.concatenate([line[:, :, start_mlp:], beside[:, :, start_mlp:]])
        other_head = beside[:, :, :start_mlp]
        return other_head, swap(jnp.concatenate([head, other_head]), ALONG_X), mlp, swap(mlp, CORE)

    def across(head, other_head, beyond, mlp, mlp_other):
        both = jnp.concatenate([head, other_head, beyond])
        rest_arrays.extend([both, swap(both, CORE), mlp, mlp_other])

    chips = chip_flips(16, ALONG_Y, ALONG_X)
    rest_slots = [(0, 16, 0, 0), (1, 16, 0, 1)]
    in_loads, in_spots = spread_loads(rest_slots, chips, 0, FF, 1, 0)
    out_loads, out_spots = spread_loads(rest_slots, chips, start_out, D // 2, 0, 0)
    mlp_loads, mlp_spots = [], []
    for other in (0, 1):
        for block, flips in enumerate(chip_flips(8, ALONG_Y, 0)):
            for third in range(3):
                mlp_loads.append((2 + other, block, third * (D // 2), D // 2, 2))
                mlp_spots.append((flips, 2, 144, third * 48, other, D // 2, 0))
    rest = (rest_arrays, out_loads + in_loads + mlp_loads, out_spots + in_spots + mlp_spots)

    last_loads, last_spots = list(first[1]), list(first[2])
    for group in range(2):
        column = WIDTH * (group + 1)
        more = spread_loads(slots, chips, 3 * PAIR * group, 3 * PAIR, 0, column)
        last_loads += [(load[0] + 4,) + load[1:] for load in more[0]]
        last_spots += more[1]
    end_loads = [(load[0] - 2,) + load[1:4] + (0,) for load in mlp_loads]
    last = lambda: (first_arrays + other_arrays, last_loads, last_spots)
    ends = lambda: (rest_arrays[2:], end_loads, mlp_spots)
    return gains, [first] + others, rest, last, ends, (own_mlp, parts[1:], near, far, across)


def gather_simply(qkv_weight, out_weight, in_weight, mlp_weight, norm_gains):
    whole = lambda w: lax.all_gather(w, "fsdp", axis=0, tiled=True)
    by_pair = whole(qkv_weight).reshape(D, 3, PAIRS, PAIR).transpose(0, 2, 1, 3)
    w_qkv = by_pair.reshape(1, D, 3 * D)
    w_in, w_out = whole(in_weight).reshape(1, D, 2 * FF), whole(out_weight).reshape(1, D, D)
    w_mlp = whole(mlp_weight).reshape(1, FF, D)
    groups = [([w_qkv], [(0, 0, at * WIDTH, WIDTH, 0)], [NOWHERE]) for at in range(GROUPS)]
    rest = (
        [w_out, w_in, w_mlp],
        [(0, 0, 0, D, 0), (1, 0, 0, 2 * FF, 1), (2, 0, 0, D, 2)],
        [NOWHERE] * 3,
    )
    last = lambda: ([w_qkv], [(0, 0, 0, 3 * D, 0)], [NOWHERE])
    ends = lambda: ([w_mlp], [(0, 0, 0, D, 0)], [NOWHERE])
    return whole(norm_gains), groups, rest, last, ends, None


def shards(devices, tokens, qkv_weight, out_weight, in_weight, mlp_weight, norm_gains, cotangent):
    count = tokens.shape[0]
    sequences = count // LEN
    fast = devices == 32
    gather = gather_weights if fast else gather_simply
    gains, groups, rest, last, ends, rounds = gather(
        qkv_weight, out_weight, in_weight, mlp_weight, norm_gains
    )
    gains = gains.astype(f32)
    gain_attn, gain_mlp = gains[:D].reshape(1, D), gains[D:].reshape(1, D)
    me = lax.axis_index("fsdp").astype(jnp.int32).reshape(1)

    def back_places(rows, columns, first, second):
        if not fast:
            return [NOWHERE], [(1, rows, columns)]
        half = columns // 2
        blocks = 8 if second is None else 16
        rows = rows // blocks
        spots = [
            (flips, 2 if second is None else 1, rows, 0, other, half, 0)
            for other in (0, 1)
            for flips in chip_flips(blocks, first, second or 0)
        ]
        return spots, [(blocks, rows, half)] * 2

    tables = jnp.asarray(rope_constants())
    masks = np.arange(PAIR)[None, :] // HEAD == np.arange(2)[:, None]
    masks = jnp.asarray(masks.astype(np.float32)).astype(bf16)
    probs_shape = (GROUPS, sequences, EACH, BLOCKS, SPAN, SPAN)
    probs_spec = lambda at: pl.BlockSpec((1, 1) + probs_shape[2:], lambda i: (at, i, 0, 0, 0, 0))
    group_spec = lambda at, columns: pl.BlockSpec((LEN, columns), lambda i: (i, at))

    kept = []

    def forward(at, waits, through):
        arrays, loads, spots = groups[at]
        outputs = [
            ((count, 3 * D), bf16, group_spec(at, WIDTH)),
            (probs_shape, bf16, probs_spec(at)),
            ((count, D), bf16, group_spec(at, EACH * PAIR)),
        ]
        if at == 0:
            outputs.append(((count, D), bf16, rows_spec(LEN, D)))
        results = call(
            functools.partial(forward_kernel, loads, spots, len(arrays)),
            sequences,
            [
                (me, SMEM),
                (kept[3] if kept else tokens, rows_spec(LEN, D)),
                (gain_attn, whole_spec(1, D)),
                (tables, whole_spec(3, LEN, PAIR)),
                (masks, whole_spec(2, PAIR)),
            ]
            + [(array, ANYWHERE) for array in arrays],
            outputs,
            [
                pltpu.VMEM((D, WIDTH), bf16),
                pltpu.VMEM((3, SPAN, SPAN), f32),
                pltpu.SemaphoreType.DMA,
            ],
            4 * count * D * WIDTH,
            count * WIDTH * 8,
            waits=waits,
            through=through,
            into=kept[:3],
        )
        results, handed = results if through else (results, [])
        kept[: len(results)] = results
        return handed

    if fast:
        own_mlp, parts, near, far, across = rounds
        (own_mlp,) = forward(0, [], [own_mlp])
        line, head, beside = near(own_mlp)
        (head,) = forward(1, parts, [head])
        other_head, beyond, mlp, mlp_other = far(line, head, beside)
        (head,) = forward(2, [], [head])
        across(head, other_head, beyond, mlp, mlp_other)
    else:
        for at in range(GROUPS):
            forward(at, [], [])
    qkv, probs, mix, normed = kept

    step_rows = 256
    arrays, loads, spots = rest
    backs = (
        back_places(D, D, ALONG_X, ALONG_Y),
        back_places(D, 2 * FF, ALONG_Y, ALONG_X),
        back_places(FF, D, ALONG_Y, None),
    )
    results = call(
        functools.partial(feed_kernel, loads, spots, len(arrays), backs),
        count // step_rows,
        [(me, SMEM)]
        + [
            (tokens, rows_spec(step_rows, D)),
            (cotangent, rows_spec(step_rows, D)),
            (gain_mlp, whole_spec(1, D)),
        ]
        + [(mix, rows_spec(step_rows, D))]
        + [(array, ANYWHERE) for array in arrays],
        [
            ((count, D), f32, rows_spec(step_rows, D)),
            ((count, FF), bf16, rows_spec(step_rows, FF)),
            ((count, D), f32, rows_spec(step_rows, D)),
        ]
        + [((count, D), bf16, rows_spec(step_rows, D)), ((1, D), f32, whole_spec(1, D))]
        + [(shape, bf16, whole_spec(*shape)) for _, shapes in backs for shape in shapes],
        [
            pltpu.VMEM((D, D), bf16),
            pltpu.VMEM((D, 2 * FF), bf16),
            pltpu.VMEM((FF, D), bf16),
            pltpu.VMEM((D, D), f32),
            pltpu.VMEM((D, 2 * FF), f32),
            pltpu.VMEM((FF, D), f32),
            pltpu.SemaphoreType.DMA,
        ],
        2 * count * (3 * D * D + 8 * D * FF),
        count * D * 16,
    )
    hidden, gated, grad_hidden, grad_mix, gain_mlp_grad = results[:5]
    weight_grads = results[5:]

    grad_blocks = [None] * GROUPS
    grads = []

    def attention_back(at, waits, through):
        order = (ALONG_X, ALONG_Y) if at == 0 else (ALONG_Y, ALONG_X)
        spots, shapes = back_places(D, WIDTH, *order)
        results = call(
            functools.partial(backward_kernel, spots, len(shapes)),
            sequences,
            [
                (me, SMEM),
                (normed, rows_spec(LEN, D)),
                (qkv, group_spec(at, WIDTH)),
                (probs, probs_spec(at)),
                (grad_mix, group_spec(at, EACH * PAIR)),
                (tables, whole_spec(3, LEN, PAIR)),
                (masks, whole_spec(2, PAIR)),
            ],
            [((count, 3 * D), bf16, group_spec(at, WIDTH))]
            + [(shape, bf16, whole_spec(*shape)) for shape in shapes],
            [pltpu.VMEM((D, WIDTH), f32)] + [pltpu.VMEM((LEN, EACH * PAIR), f32)] * 2,
            4 * count * D * WIDTH,
            count * WIDTH * 8,
            waits=waits,
            through=through,
            into=grads,
        )
        results, handed = results if through else (results, [])
        grads[:] = results[:1]
        grad_blocks[at] = results[1:]
        return handed

    last_rows = 256
    halves = 2
    steps = count // last_rows // halves

    def last_part(part, before, waits, through):
        arrays, loads, spots = last()
        part_rows = lambda columns: pl.BlockSpec((last_rows, columns), lambda i: (i + part * steps, 0))
        inputs = (
            [
                (me, SMEM),
                (tokens, part_rows(D)),
                (gain_attn, whole_spec(1, D)),
                (grad_hidden, part_rows(D)),
                (grads[0], part_rows(3 * D)),
            ]
            + [(array, ANYWHERE) for array in arrays]
        )
        return call(
            functools.partial(final_kernel, loads, spots, len(arrays)),
            steps,
            inputs,
            [((count, D), f32, part_rows(D)), ((1, D), f32, whole_spec(1, D))],
            [pltpu.VMEM((D, 3 * D), bf16), pltpu.SemaphoreType.DMA],
            6 * count * D * D // halves,
            count * D * 20 // halves,
            waits=waits,
            through=through,
            into=before,
        )

    def layer_output(waits, through):
        arrays, loads, spots = ends()
        return call(
            functools.partial(output_kernel, loads, spots, len(arrays)),
            count // last_rows,
            [(me, SMEM), (hidden, rows_spec(last_rows, D)), (gated, rows_spec(last_rows, FF))]
            + [(array, ANYWHERE) for array in arrays],
            [((count, D), bf16, rows_spec(last_rows, D))],
            [pltpu.VMEM((FF, D), bf16), pltpu.SemaphoreType.DMA],
            2 * count * FF * D,
            count * D * 12,
            waits=waits,
            through=through,
        )

    if fast:
        (out_keep, out_send), (in_keep, in_send), (mlp_keep, mlp_send) = (
            weight_grads[:2],
            weight_grads[2:4],
            weight_grads[4:],
        )
        out_got, in_got, mlp_got = swap(out_send, CORE), swap(in_send, CORE), swap(mlp_send, CORE)
        in_keep, out_keep, mlp_keep = attention_back(2, [], [in_keep, out_keep, mlp_keep])
        in_keep, in_send = halved(in_keep, in_got)
        out_keep, out_send = halved(out_keep, out_got)
        mlp_keep, mlp_send = halved(mlp_keep, mlp_got)
        in_got, out_got, mlp_got = swap(in_send, ALONG_X), swap(out_send, ALONG_Y), swap(mlp_send, ALONG_Y)
        in_keep, out_keep, mlp_keep = attention_back(1, [], [in_keep, out_keep, mlp_keep])
        in_keep, in_send = halved(in_keep, in_got)
        out_keep, out_send = halved(out_keep, out_got)
        mlp_line = joined_sum(mlp_keep, mlp_got)
        in_got, out_got = swap(in_send, ALONG_Y), swap(out_send, ALONG_X)
        mlp_got = [swap(mlp_line[j], ALONG_Z * j) for j in (1, 2, 3)]
        later_got = [swap(grad_blocks[at][1], CORE) for at in (1, 2)]
        in_keep, out_keep, mlp_own, *later = attention_back(
            0, [mlp_line], [in_keep, out_keep, mlp_line[0], grad_blocks[1][0], grad_blocks[2][0]]
        )
        line = jnp.concatenate([joined_sum(in_keep, in_got), joined_sum(out_keep, out_got)], axis=2)
        line_got = [swap(line[j], ALONG_Z * j) for j in (1, 2, 3)]
        later = [halved(kept, got) for kept, got in zip(later, later_got)]
        later_keep = jnp.concatenate([keep for keep, _ in later], axis=2)
        later_got = swap(jnp.concatenate([send for _, send in later], axis=2), ALONG_X)
        early_got = swap(grad_blocks[0][1], CORE)
        total_mlp = mlp_own.astype(f32)
        for got in mlp_got:
            total_mlp = total_mlp + got.astype(f32)
        rows = total_mlp.shape[0] // 2
        low, high = total_mlp[:rows], total_mlp[rows:]
        mlp_other = swap(jnp.where(bit_of(ALONG_X), low, high).astype(bf16), ALONG_X)
        mlp_own = jnp.where(bit_of(ALONG_X), high, low)
        (tokens_grad, gain_first), (later_keep, early_keep, line_own, mlp_own) = last_part(
            0, [], [], [later_keep, grad_blocks[0][0], line[0], mlp_own]
        )
        later_keep, later_send = halved(later_keep, later_got)
        later_got = swap(later_send, ALONG_Y)
        early_keep, early_send = halved(early_keep, early_got)
        early_got = swap(early_send, ALONG_Y)
        total = line_own.astype(f32)
        for got in line_got:
            total = total + got.astype(f32)
        total_mlp = mlp_own + mlp_other.astype(f32)
        joined_mlp = join_columns(total_mlp)
        joined_rest = join_columns(total)
        (tokens_grad, gain_last), (later_keep, early_keep) = last_part(
            1, [tokens_grad], line_got + [mlp_other], [later_keep, early_keep]
        )
        gains_grad = jnp.concatenate([(gain_first + gain_last).reshape(-1), gain_mlp_grad.reshape(-1)])
        gains_keep, gains_got = swap_half(gains_grad, 2 * ALONG_Z)
        early_keep, early_send = halved(early_keep, early_got)
        early_got = swap(early_send, ALONG_X)
        later_line = joined_sum(later_keep, later_got)
        (output,), (early_keep, gains_keep) = layer_output([later_line], [early_keep, gains_keep])
        gains_share = gains_keep + gains_got
        for bits in (ALONG_Z, ALONG_Y, ALONG_X, CORE):
            gains_keep, gains_got = swap_half(gains_share, bits)
            gains_share = gains_keep + gains_got
        early_line = joined_sum(early_keep, early_got)
        early_later = summed_line(jnp.concatenate([early_line, later_line], axis=2))
        mlp_share = both_columns(joined_mlp, 0, D // 2).reshape(-1)
        in_share = both_columns(joined_rest, 0, FF).reshape(-1)
        out_share = both_columns(joined_rest, FF, FF + D // 2).reshape(-1)
        joined = join_columns(early_later)
        qkv_share = [both_columns(joined, at * 3 * PAIR, (at + 1) * 3 * PAIR) for at in range(GROUPS)]
        qkv_share = jnp.concatenate(qkv_share, axis=1).reshape(24, PAIRS, 3, PAIR)
        qkv_share = qkv_share.transpose(0, 2, 1, 3).reshape(-1)
    else:
        for at in reversed(range(GROUPS)):
            attention_back(at, [], [])
        tokens_grad, gain_first = last_part(0, [], [], [])
        tokens_grad, gain_last = last_part(1, [tokens_grad], [], [])
        (output,) = layer_output([], [])
        add = lambda grad: lax.psum_scatter(
            grad.astype(f32).reshape(-1), "fsdp", scatter_dimension=0, tiled=True
        )
        out_share, in_share, mlp_share = (add(grad) for grad in weight_grads)
        qkv_grad = jnp.concatenate([blocks[0].reshape(D, EACH, 3, PAIR) for blocks in grad_blocks], axis=1)
        qkv_share = add(qkv_grad.transpose(0, 2, 1, 3))
        gains_share = add(jnp.concatenate([gain_first + gain_last, gain_mlp_grad]))
    return (output, tokens_grad, qkv_share, out_share, in_share, mlp_share, gains_share)


def solution(mesh):
    placed = (P("fsdp", None),) + (P("fsdp"),) * 5 + (P("fsdp", None),)
    return jax.shard_map(
        functools.partial(shards, mesh.shape["fsdp"]),
        mesh=mesh,
        in_specs=placed,
        out_specs=(P("fsdp", None),) * 2 + (P("fsdp"),) * 5,
        check_vma=False,
    )
```

time: 411 us -> 366 us (0.89); the launches traced: 410 us -> 360 us
  Pallas kernels: 208 us -> 181 us
  waiting for transfers between devices: 88 us -> 61.6 us
  starting transfers between devices: 84.4 us -> 64.9 us
  other arithmetic: 14.2 us -> 32.2 us
  local copies, waits for them, and re-layouts: 13.6 us -> 17.8 us
    pallas_call x6 -> x10, Pallas kernels: 208 us -> 181 us  [call(): pl.pallas_call(trimmed, grid=(steps,), in_specs=[spec for _, spec in inpu...]
    ppermute x85 -> x60, waiting for transfers between devices: 88 us -> 61.6 us  [swap(): return lax.ppermute(values, 'fsdp', [(i, i ^ bits) for i in range(32)])]
    ppermute x85 -> x60, starting transfers between devices: 84.4 us -> 64.9 us  [swap(): return lax.ppermute(values, 'fsdp', [(i, i ^ bits) for i in range(32)])]
    convert_element_type x14 -> x15, other arithmetic: 6.13 us -> 15.6 us  [joined_sum(): return (kept.astype(f32) + received.astype(f32)).astype(bf16)]
    concatenate x0 -> x5, other arithmetic: none -> 5.21 us  [the longest x1 3.02 us: across(): both = jnp.concatenate([head, other_head, beyond])]
  transfers between devices with their start and end apart: 85 -> 60, of which waited for: 32 -> 15; matrix products, arithmetic and copies ran while one was open for 6% -> 11% of each run, Pallas kernels for 17% -> 34%
where the time goes in v2:
time: 366 us; the launch traced here: 360 us
  Pallas kernels  181 us (49%)
  starting transfers between devices  64.9 us (18%)
  waiting for transfers between devices  61.6 us (17%)
  other arithmetic  32.2 us (9%)
  local copies, waits for them, and re-layouts  17.8 us (5%)
    pallas_call x10, Pallas kernels, call(): pl.pallas_call(trimmed, grid=(steps,), in_specs=[spec for _, spec in inpu...  181 us
    ppermute x60, starting transfers between devices, swap(): return lax.ppermute(values, 'fsdp', [(i, i ^ bits) for i in range(32)])  64.9 us
    ppermute x60, waiting for transfers between devices, swap(): return lax.ppermute(values, 'fsdp', [(i, i ^ bits) for i in range(32)])  61.6 us
    convert_element_type x15, other arithmetic, joined_sum(): return (kept.astype(f32) + received.astype(f32)).astype(bf16)  15.6 us
  transfers between devices with their start and end apart: 60, of which 15 were waited for; matrix products, arithmetic and copies ran while one was open for 11% of the time, Pallas kernels for 34%

profile of v2, /device:TPU:0, one launch (start us, length us, event | category | flops | bytes accessed | tf_op | source)
XLA Modules:
  0.0 360.2 jit_solution(14332918052926510506)
XLA Ops:
  8.3 2.6 collective-permute-start.1
  11.6 2.7 collective-permute-start.2
  14.4 1.8 collective-permute-start.9
  17.7 3.5 collective-permute-start.12
  23.8 2.7 collective-permute-start.22
  26.5 1.6 collective-permute-done.13
  28.2 1.6 collective-permute-start.14
  30.5 7.7 %collective-permute-done.14 = bf16[4,48,768]{2,1,0:T(8,128)(2,1)S(1)} collective-permute-done((bf16[4,48,768]{2,1,0:T(8,128)(2,1)S(1)}, bf16[4,48,768]{2,1,0:T(8,128)(2,1)S(1)}, u32[]{:S(2)}, u32[]{:S(2)}) %collective-permute-start.14) | collective-permute-done | bytes 294944 | tf_op jit(solution)/shard_map/ppermute | solution.py:46
  38.7 3.9 %collective-permute-done.5.refs_6_ = bf16[8,48,512]{2,1,0:T(8,128)(2,1)S(1)} collective-permute-done((bf16[8,48,512]{2,1,0:T(8,128)(2,1)S(1)}, bf16[8,48,512]{2,1,0:T(8,128)(2,1)S(1)}, u32[]{:S(2)}, u32[]{:S(2)}) %collective-permute-start.5) | collective-permute-done | bytes 393248 | tf_op jit(solution)/shard_map/ppermute | solution.py:46
  43.6 8.4 %collective-permute-start.20 = (bf16[48,2688]{1,0:T(8,128)(2,1)}, bf16[48,2688]{1,0:T(8,128)(2,1)S(1)}, u32[]{:S(2)}, u32[]{:S(2)}) collective-permute-start(bf16[48,2688]{1,0:T(8,128)(2,1)} %broadcast_select_fusion), channel_id=1, source_target_pairs={{0,8},{1,9},{2,10},{3,11},{4,12},{5,13},{6,14},{7,15},{8,0},{9,1},... | collective-permute-start | bytes 774152 | tf_op jit(solution)/shard_map/ppermute | solution.py:46
  52.5 14.5 %shard_map.162 = (bf16[2048,2304]{1,0:T(8,128)(2,1)}, bf16[3,4,2,4,256,256]{5,4,3,2,1,0:T(8,128)(2,1)}, bf16[2048,768]{1,0:T(8,128)(2,1)}, bf16[2048,768]{1,0:T(8,128)(2,1)}, bf16[144,384]{1,0:T(8,128)(2,1)}) custom-call(s32[1]{0:T(128)} %bitcast.refs_0_, bf16[2048,768]{1,0:T(8,128)(2,1)} %refs_1_.7, ...), custom_call_target="tpu_custom_call", output_to_operand_aliasing={{4}: (9, {})} | custom-call | flops 4831838208 | bytes 12582912 | tf_op jit(solution)/shard_map/pallas_call | solution.py:440
  70.8 1.6 collective-permute-start.23
  74.3 13.1 %shard_map.163 = (bf16[2048,2304]{1,0:T(8,128)(2,1)}, bf16[3,4,2,4,256,256]{5,4,3,2,1,0:T(8,128)(2,1)}, bf16[2048,768]{1,0:T(8,128)(2,1)}, bf16[4,48,1536]{2,1,0:T(8,128)(2,1)}) custom-call(s32[1]{0:T(128)} %bitcast.refs_0_, ...), custom_call_target="tpu_custom_call", output_to_operand_aliasing={{3}: (12, {}), {0}: (13, {}), {1}: (14, {}), {2}: (15, {})} | custom-call | flops 4831838208 | bytes 12582912 | tf_op jit(solution)/shard_map/pallas_call | solution.py:440
  87.4 8.5 %collective-permute-done.23 = bf16[4,48,2688]{2,1,0:T(8,128)(2,1)} collective-permute-done((bf16[4,48,2688]{2,1,0:T(8,128)(2,1)S(1)}, bf16[4,48,2688]{2,1,0:T(8,128)(2,1)}, u32[]{:S(2)}, u32[]{:S(2)}) %collective-permute-start.23) | collective-permute-done | bytes 1032224 | tf_op jit(solution)/shard_map/ppermute | solution.py:46
  98.8 13.1 %shard_map.164 = (bf16[2048,2304]{1,0:T(8,128)(2,1)}, bf16[3,4,2,4,256,256]{5,4,3,2,1,0:T(8,128)(2,1)}, bf16[2048,768]{1,0:T(8,128)(2,1)}, bf16[4,48,1536]{2,1,0:T(8,128)(2,1)}) custom-call(s32[1]{0:T(128)} %bitcast.refs_0_, bf16[2048,768]{1,0:T(8,128)(2,1)} %get-tuple-element.64.refs_1_, ...), custom_call_target="tpu_custom_call", output_to_operand_aliasing={{3}: (9, {}), {0}: (10, {}), {1}: (11, {}), {2}: (12, {})} | custom-call | flops 4831838208 | bytes 12582912 | tf_op jit(solution)/shard_map/pallas_call | solution.py:440
  112.0 13.7 %collective-permute-done.24 = bf16[8,48,1536]{2,1,0:T(8,128)(2,1)} collective-permute-done((bf16[8,48,1536]{2,1,0:T(8,128)(2,1)S(1)}, bf16[8,48,1536]{2,1,0:T(8,128)(2,1)}, u32[]{:S(2)}, u32[]{:S(2)}) %collective-permute-start.24) | collective-permute-done | bytes 1179680 | tf_op jit(solution)/shard_map/ppermute | solution.py:46
  125.7 3.0 pad_maximum_fusion.refs_5_
  131.1 3.4 collective-permute-done.26.refs_8_.refs_4_
  135.4 57.5 %shard_map.165 = (f32[2048,768]{1,0:T(8,128)}, bf16[2048,1152]{1,0:T(8,128)(2,1)}, f32[2048,768]{1,0:T(8,128)}, bf16[2048,768]{1,0:T(8,128)(2,1)}, f32[1,768]{1,...) custom-call(s32[1]{0:T(128)} %bitcast.refs_0_, ...), custom_call_target="tpu_custom_call" | custom-call | flops 36238786560 | bytes 25165824 | tf_op jit(solution)/shard_map/pallas_call | solution.py:440
  193.6 13.3 %shard_map.166 = (bf16[2048,2304]{1,0:T(8,128)(2,1)}, bf16[16,48,384]{2,1,0:T(8,128)(2,1)}, bf16[16,48,384]{2,1,0:T(8,128)(2,1)}, bf16[16,48,1152]{2,1,0:T(8,128...) custom-call(s32[1]{0:T(128)} %bitcast.refs_0_, ...), custom_call_target="tpu_custom_call", output_to_operand_aliasing={{3}: (7, {}), {4}: (8, {}), {5}: (9, {})} | custom-call | flops 4831838208 | bytes 12582912 | tf_op jit(solution)/shard_map/pallas_call | solution.py:440
  207.4 2.3 add_convert_fusion.17
  209.7 1.5 collective-permute-start.32
  211.2 2.1 add_convert_fusion.7
  215.8 22.8 %shard_map.167 = (bf16[2048,2304]{1,0:T(8,128)(2,1)}, bf16[16,48,384]{2,1,0:T(8,128)(2,1)}, bf16[16,48,384]{2,1,0:T(8,128)(2,1)}, bf16[8,48,1152]{2,1,0:T(8,128)...) custom-call(s32[1]{0:T(128)} %bitcast.refs_0_, ...), custom_call_target="tpu_custom_call", output_to_operand_aliasing={{3}: (7, {}), {4}: (8, {}), {5}: (9, {}), {0}: (10, {})} | custom-call | flops 4831838208 | bytes 12582912 | tf_op jit(solution)/shard_map/pallas_call | solution.py:440
  240.8 6.2 %collective-permute-start.40 = (bf16[144,384]{1,0:T(8,128)(2,1)S(1)}, bf16[144,384]{1,0:T(8,128)(2,1)}, u32[]{:S(2)}, u32[]{:S(2)}) collective-permute-start(bf16[144,384]{1,0:T(8,128)(2,1)S(1)} %get-tuple-element.157), channel_id=1, source_target_pairs={{0,24},{1,25},{2,26},{3,27},{4,28},{5,29},{6,30},{7,31},{8,16},{9,... | collective-permute-start | bytes 331784 | tf_op jit(solution)/shard_map/ppermute | solution.py:46
  250.3 13.3 %shard_map.168 = (bf16[2048,2304]{1,0:T(8,128)(2,1)}, bf16[16,48,384]{2,1,0:T(8,128)(2,1)}, bf16[16,48,384]{2,1,0:T(8,128)(2,1)}, bf16[4,48,1152]{2,1,0:T(8,128)...) custom-call(s32[1]{0:T(128)} %bitcast.refs_0_, ...), custom_call_target="tpu_custom_call", output_to_operand_aliasing={{3}: (8, {}), {4}: (9, {}), {5}: (10, {}), {6}: (11, {}), {... | custom-call | flops 4831838208 | bytes 12582912 | tf_op jit(solution)/shard_map/pallas_call | solution.py:440
  263.6 1.6 collective-permute-start.34
  265.2 1.5 collective-permute-start.33
  270.5 1.5 collective-permute-start.41
  272.9 3.9 %collective-permute-done.33 = bf16[4,48,1152]{2,1,0:T(8,128)(2,1)S(1)} collective-permute-done((bf16[4,48,1152]{2,1,0:T(8,128)(2,1)S(1)}, bf16[4,48,1152]{2,1,0:T(8,128)(2,1)S(1)}, u32[]{:S(2)}, u32[]{:S(2)}) %collective-permute-start.33) | collective-permute-done | bytes 442400 | tf_op jit(solution)/shard_map/ppermute | solution.py:46
  277.7 1.4 collective-permute-start.35
  279.1 2.0 collective-permute-start.36
  281.1 10.9 %shard_map.169 = (f32[2048,768]{1,0:T(8,128)}, f32[1,768]{1,0:T(1,128)}, bf16[8,48,768]{2,1,0:T(8,128)(2,1)}, bf16[16,48,384]{2,1,0:T(8,128)(2,1)}, bf16[48,1536]{1,0:T(8,128)(2,1)}, /*index=5*/f32[72,384]{1,0:T(8,128)}) custom-call(s32[1]{0:T(128)} %bitcast.refs_0_, ...), custom_call_target="tpu_custom_call", output_to_operand_aliasing={{2}: (13, {}), {3}: (14, {}), {4}: (15, {}), {5}: (16, {})} | custom-call | flops 3623878656 | bytes 15728640 | tf_op jit(solution)/shard_map/pallas_call | solution.py:440
  294.1 5.0 %collective-permute-done.37.refs_15_ = bf16[48,1536]{1,0:T(8,128)(2,1)S(1)} collective-permute-done((bf16[48,1536]{1,0:T(8,128)(2,1)S(1)}, bf16[48,1536]{1,0:T(8,128)(2,1)S(1)}, u32[]{:S(2)}, u32[]{:S(2)}) %collective-permute-start.37) | collective-permute-done | bytes 147488 | tf_op jit(solution)/shard_map/ppermute | solution.py:46
  301.2 1.5 collective-permute-start.46
  304.2 10.8 %shard_map.170 = (f32[2048,768]{1,0:T(8,128)}, f32[1,768]{1,0:T(1,128)}, bf16[4,48,768]{2,1,0:T(8,128)(2,1)}, bf16[8,48,384]{2,1,0:T(8,128)(2,1)}) custom-call(s32[1]{0:T(128)} %bitcast.refs_0_, bf16[2048,768]{1,0:T(8,128)(2,1)} %refs_1_.7, f32[1,768]{1,0:T(1,128)} %reshape.324.refs_2_, ...), custom_call_target="tpu_custom_call", output_to_operand_aliasing={{2}: (17, {}), {3}: (18, {}), {0}: (19, {})} | custom-call | flops 3623878656 | bytes 15728640 | tf_op jit(solution)/shard_map/pallas_call | solution.py:440
  317.1 1.8 add_convert_fusion.9.refs_5_
  318.9 1.7 add_convert_fusion.20
  320.6 11.6 %shard_map.171 = (bf16[2048,768]{1,0:T(8,128)(2,1)}, bf16[4,48,384]{2,1,0:T(8,128)(2,1)}, f32[768]{0:T(1024)}) custom-call(s32[1]{0:T(128)} %bitcast.refs_0_, f32[2048,768]{1,0:T(8,128)} %get-tuple-element.75.refs_1_, bf16[2048,1152]{1,0:T(8,128)(2,1)} %get-tuple-element.76.refs_2_, ...), custom_call_target="tpu_custom_call", output_to_operand_aliasing={{1}: (6, {}), {2}: (7, {})} | custom-call | flops 3623878656 | bytes 18874368 | tf_op jit(solution)/shard_map/pallas_call | solution.py:440
  334.4 2.2 collective-permute-done.56
  336.7 1.5 collective-permute-start.57
  338.2 2.0 collective-permute-done.57
  342.2 1.6 collective-permute-start.48
  344.1 3.3 collective-permute-done.48
  347.4 2.6 collective-permute-start.51
  350.0 1.9 collective-permute-start.49
  352.5 1.7 collective-permute-done.51
  354.2 3.2 collective-permute-done.50
  (259 shorter events, 56.2 us)
Async XLA Ops:
  4.0 10.4 %collective-permute-start.18 = (bf16[24,1152]{1,0:T(8,128)(2,1)S(1)}, bf16[24,1152]{1,0:T(8,128)(2,1)S(1)}, u32[]{:S(2)}, u32[]{:S(2)}) collective-permute-start(bf16[24,1152]{1,0:T(8,128)(2,1)S(1)} %get-tuple-element.175), channel_id=1, source_target_pairs={{0,1},{1,0},{2,3},{3,2},{4,5},{5,4},{6,7},{7,6},{8,9},{9,8},{10,11... | collective-permute-start | bytes 165896 | tf_op jit(solution)/shard_map/ppermute | solution.py:46
  5.0 11.2 %collective-permute-start.19 = (bf16[24,384]{1,0:T(8,128)(2,1)S(1)}, bf16[24,384]{1,0:T(8,128)(2,1)S(1)}, u32[]{:S(2)}, u32[]{:S(2)}) collective-permute-start(bf16[24,384]{1,0:T(8,128)(2,1)S(1)} %get-tuple-element.195), channel_id=1, source_target_pairs={{0,1},{1,0},{2,3},{3,2},{4,5},{5,4},{6,7},{7,6},{8,9},{9,8},{10,11... | collective-permute-start | bytes 55304 | tf_op jit(solution)/shard_map/ppermute | solution.py:46
  6.6 7.7 %collective-permute-start.10 = (bf16[24,768]{1,0:T(8,128)(2,1)S(1)}, bf16[24,768]{1,0:T(8,128)(2,1)S(1)}, u32[]{:S(2)}, u32[]{:S(2)}) collective-permute-start(bf16[24,768]{1,0:T(8,128)(2,1)S(1)} %get-tuple-element.183), channel_id=1, source_target_pairs={{0,1},{1,0},{2,3},{3,2},{4,5},{5,4},{6,7},{7,6},{8,9},{9,8},{10,11... | collective-permute-start | bytes 110600 | tf_op jit(solution)/shard_map/ppermute | solution.py:46
  8.3 9.4 %collective-permute-start.1 = (bf16[48,512]{1,0:T(8,128)(2,1)S(1)}, bf16[48,512]{1,0:T(8,128)(2,1)S(1)}, u32[]{:S(2)}, u32[]{:S(2)}) collective-permute-start(bf16[48,512]{1,0:T(8,128)(2,1)S(1)} %maximum_select_fusion.12), channel_id=1, source_target_pairs={{0,8},{1,9},{2,10},{3,11},{4,12},{5,13},{6,14},{7,15},{8,0},{9,1},... | collective-permute-start | bytes 147464 | tf_op jit(solution)/shard_map/ppermute | solution.py:46
  11.6 9.6 %collective-permute-start.2 = (bf16[48,512]{1,0:T(8,128)(2,1)S(1)}, bf16[48,512]{1,0:T(8,128)(2,1)S(1)}, u32[]{:S(2)}, u32[]{:S(2)}) collective-permute-start(bf16[48,512]{1,0:T(8,128)(2,1)S(1)} %maximum_select_fusion.12), channel_id=1, source_target_pairs={{0,16},{1,17},{2,18},{3,19},{4,20},{5,21},{6,22},{7,23},{8,24},{9,... | collective-permute-start | bytes 147464 | tf_op jit(solution)/shard_map/ppermute | solution.py:46
  14.3 7.2 %collective-permute-start.3 = (bf16[48,512]{1,0:T(8,128)(2,1)S(1)}, bf16[48,512]{1,0:T(8,128)(2,1)S(1)}, u32[]{:S(2)}, u32[]{:S(2)}) collective-permute-start(bf16[48,512]{1,0:T(8,128)(2,1)S(1)} %maximum_select_fusion.12), channel_id=1, source_target_pairs={{0,24},{1,25},{2,26},{3,27},{4,28},{5,29},{6,30},{7,31},{8,16},{9,... | collective-permute-start | bytes 147464 | tf_op jit(solution)/shard_map/ppermute | solution.py:46
  14.4 8.6 %collective-permute-start.9 = (bf16[72,384]{1,0:T(8,128)(2,1)S(1)}, bf16[72,384]{1,0:T(8,128)(2,1)S(1)}, u32[]{:S(2)}, u32[]{:S(2)}) collective-permute-start(bf16[72,384]{1,0:T(8,128)(2,1)S(1)} %maximum_select_fusion.10), channel_id=1, source_target_pairs={{0,2},{1,3},{2,0},{3,1},{4,6},{5,7},{6,4},{7,5},{8,10},{9,11},{10,... | collective-permute-start | bytes 165896 | tf_op jit(solution)/shard_map/ppermute | solution.py:46
  16.2 10.3 %collective-permute-start.11 = (bf16[48,768]{1,0:T(8,128)(2,1)S(1)}, bf16[48,768]{1,0:T(8,128)(2,1)S(1)}, u32[]{:S(2)}, u32[]{:S(2)}) collective-permute-start(bf16[48,768]{1,0:T(8,128)(2,1)S(1)} %fusion.17), channel_id=1, source_target_pairs={{0,8},{1,9},{2,10},{3,11},{4,12},{5,13},{6,14},{7,15},{8,0},{9,1},... | collective-permute-start | bytes 221192 | tf_op jit(solution)/shard_map/ppermute | solution.py:46
  17.7 8.8 %collective-permute-start.12 = (bf16[48,768]{1,0:T(8,128)(2,1)S(1)}, bf16[48,768]{1,0:T(8,128)(2,1)S(1)}, u32[]{:S(2)}, u32[]{:S(2)}) collective-permute-start(bf16[48,768]{1,0:T(8,128)(2,1)S(1)} %fusion.17), channel_id=1, source_target_pairs={{0,16},{1,17},{2,18},{3,19},{4,20},{5,21},{6,22},{7,23},{8,24},{9,... | collective-permute-start | bytes 221192 | tf_op jit(solution)/shard_map/ppermute | solution.py:46
  21.5 8.3 %collective-permute-start.4 = (bf16[4,48,512]{2,1,0:T(8,128)(2,1)S(1)}, bf16[4,48,512]{2,1,0:T(8,128)(2,1)S(1)}, u32[]{:S(2)}, u32[]{:S(2)}) collective-permute-start(bf16[4,48,512]{2,1,0:T(8,128)(2,1)S(1)} %pad_maximum_fusion.7), channel_id=1, source_target_pairs={{0,2},{1,3},{2,0},{3,1},{4,6},{5,7},{6,4},{7,5},{8,10},{9,11},{10,... | collective-permute-start | bytes 589832 | tf_op jit(solution)/shard_map/ppermute | solution.py:46
  23.8 45.7 %collective-permute-start.22 = (bf16[48,2688]{1,0:T(8,128)(2,1)}, bf16[48,2688]{1,0:T(8,128)(2,1)}, u32[]{:S(2)}, u32[]{:S(2)}) collective-permute-start(bf16[48,2688]{1,0:T(8,128)(2,1)} %broadcast_select_fusion), channel_id=1, source_target_pairs={{0,24},{1,25},{2,26},{3,27},{4,28},{5,29},{6,30},{7,31},{8,16},{9,... | collective-permute-start | bytes 774152 | tf_op jit(solution)/shard_map/ppermute | solution.py:46
  26.5 42.9 %collective-permute-start.21 = (bf16[48,2688]{1,0:T(8,128)(2,1)}, bf16[48,2688]{1,0:T(8,128)(2,1)}, u32[]{:S(2)}, u32[]{:S(2)}) collective-permute-start(bf16[48,2688]{1,0:T(8,128)(2,1)} %broadcast_select_fusion), channel_id=1, source_target_pairs={{0,16},{1,17},{2,18},{3,19},{4,20},{5,21},{6,22},{7,23},{8,24},{9,... | collective-permute-start | bytes 774152 | tf_op jit(solution)/shard_map/ppermute | solution.py:46
  28.2 10.0 %collective-permute-start.14 = (bf16[4,48,768]{2,1,0:T(8,128)(2,1)S(1)}, bf16[4,48,768]{2,1,0:T(8,128)(2,1)S(1)}, u32[]{:S(2)}, u32[]{:S(2)}) collective-permute-start(bf16[4,48,768]{2,1,0:T(8,128)(2,1)S(1)} %pad_maximum_fusion.6), channel_id=1, source_target_pairs={{0,4},{1,5},{2,6},{3,7},{4,0},{5,1},{6,2},{7,3},{8,12},{9,13},{10,... | collective-permute-start | bytes 884744 | tf_op jit(solution)/shard_map/ppermute | solution.py:46
  29.9 12.7 %collective-permute-start.5 = (bf16[8,48,512]{2,1,0:T(8,128)(2,1)S(1)}, bf16[8,48,512]{2,1,0:T(8,128)(2,1)S(1)}, u32[]{:S(2)}, u32[]{:S(2)}) collective-permute-start(bf16[8,48,512]{2,1,0:T(8,128)(2,1)S(1)} %get-tuple-element.164.refs_5_), channel_id=1, source_target_pairs={{0,4},{1,5},{2,6},{3,7},{4,0},{5,1},{6,2},{7,3},{8,12},{9,13},{10,... | collective-permute-start | bytes 1179656 | tf_op jit(solution)/shard_map/ppermute | solution.py:46
  30.4 13.1 %collective-permute-start.6 = (bf16[8,48,512]{2,1,0:T(8,128)(2,1)S(1)}, bf16[8,48,512]{2,1,0:T(8,128)(2,1)S(1)}, u32[]{:S(2)}, u32[]{:S(2)}) collective-permute-start(bf16[8,48,512]{2,1,0:T(8,128)(2,1)S(1)} %get-tuple-element.164.refs_5_), channel_id=1, source_target_pairs={{0,1},{1,0},{2,3},{3,2},{4,5},{5,4},{6,7},{7,6},{8,9},{9,8},{10,11... | collective-permute-start | bytes 1179656 | tf_op jit(solution)/shard_map/ppermute | solution.py:46
  38.3 13.8 %collective-permute-start.15 = (bf16[8,48,768]{2,1,0:T(8,128)(2,1)S(1)}, bf16[8,48,768]{2,1,0:T(8,128)(2,1)S(1)}, u32[]{:S(2)}, u32[]{:S(2)}) collective-permute-start(bf16[8,48,768]{2,1,0:T(8,128)(2,1)S(1)} %constant_dynamic-update-slice_fusion.11.refs_5_.refs_9_), channel_id=1, source_target_pairs={{0,2},{1,3},{2,0},{3,1},{4,6},{5,7},{6,4},{7,5},{8,10},{9,11},{10,... | collective-permute-start | bytes 1769480 | tf_op jit(solution)/shard_map/ppermute | solution.py:46
  42.6 9.6 %collective-permute-start.7 = (bf16[8,48,512]{2,1,0:T(8,128)(2,1)S(1)}, bf16[8,48,512]{2,1,0:T(8,128)(2,1)}, u32[]{:S(2)}, u32[]{:S(2)}) collective-permute-start(bf16[8,48,512]{2,1,0:T(8,128)(2,1)S(1)} %collective-permute-done.5.refs_6_), channel_id=1, source_target_pairs={{0,1},{1,0},{2,3},{3,2},{4,5},{5,4},{6,7},{7,6},{8,9},{9,8},{10,11... | collective-permute-start | bytes 1179656 | tf_op jit(solution)/shard_map/ppermute | solution.py:46
  43.6 25.9 %collective-permute-start.20 = (bf16[48,2688]{1,0:T(8,128)(2,1)}, bf16[48,2688]{1,0:T(8,128)(2,1)S(1)}, u32[]{:S(2)}, u32[]{:S(2)}) collective-permute-start(bf16[48,2688]{1,0:T(8,128)(2,1)} %broadcast_select_fusion), channel_id=1, source_target_pairs={{0,8},{1,9},{2,10},{3,11},{4,12},{5,13},{6,14},{7,15},{8,0},{9,1},... | collective-permute-start | bytes 774152 | tf_op jit(solution)/shard_map/ppermute | solution.py:46
  52.0 21.3 %collective-permute-start.16 = (bf16[8,48,768]{2,1,0:T(8,128)(2,1)S(1)}, bf16[8,48,768]{2,1,0:T(8,128)(2,1)S(1)}, u32[]{:S(2)}, u32[]{:S(2)}) collective-permute-start(bf16[8,48,768]{2,1,0:T(8,128)(2,1)S(1)} %constant_dynamic-update-slice_fusion.11.refs_5_.refs_9_), channel_id=1, source_target_pairs={{0,1},{1,0},{2,3},{3,2},{4,5},{5,4},{6,7},{7,6},{8,9},{9,8},{10,11... | collective-permute-start | bytes 1769480 | tf_op jit(solution)/shard_map/ppermute | solution.py:46
  52.2 21.1 %collective-permute-start.17 = (bf16[8,48,768]{2,1,0:T(8,128)(2,1)S(1)}, bf16[8,48,768]{2,1,0:T(8,128)(2,1)S(1)}, u32[]{:S(2)}, u32[]{:S(2)}) collective-permute-start(bf16[8,48,768]{2,1,0:T(8,128)(2,1)S(1)} %collective-permute-done.15.refs_6_.refs_10_), channel_id=1, source_target_pairs={{0,1},{1,0},{2,3},{3,2},{4,5},{5,4},{6,7},{7,6},{8,9},{9,8},{10,11... | collective-permute-start | bytes 1769480 | tf_op jit(solution)/shard_map/ppermute | solution.py:46
  70.8 25.1 %collective-permute-start.23 = (bf16[4,48,2688]{2,1,0:T(8,128)(2,1)S(1)}, bf16[4,48,2688]{2,1,0:T(8,128)(2,1)}, u32[]{:S(2)}, u32[]{:S(2)}) collective-permute-start(bf16[4,48,2688]{2,1,0:T(8,128)(2,1)S(1)} %pad_maximum_fusion.2), channel_id=1, source_target_pairs={{0,4},{1,5},{2,6},{3,7},{4,0},{5,1},{6,2},{7,3},{8,12},{9,13},{10,... | collective-permute-start | bytes 3096584 | tf_op jit(solution)/shard_map/ppermute | solution.py:46
  98.2 27.4 %collective-permute-start.24 = (bf16[8,48,1536]{2,1,0:T(8,128)(2,1)S(1)}, bf16[8,48,1536]{2,1,0:T(8,128)(2,1)}, u32[]{:S(2)}, u32[]{:S(2)}) collective-permute-start(bf16[8,48,1536]{2,1,0:T(8,128)(2,1)S(1)} %pad_maximum_fusion.1), channel_id=1, source_target_pairs={{0,2},{1,3},{2,0},{3,1},{4,6},{5,7},{6,4},{7,5},{8,10},{9,11},{10,... | collective-permute-start | bytes 3538952 | tf_op jit(solution)/shard_map/ppermute | solution.py:46
  192.9 21.0 %collective-permute-start.27 = (bf16[16,48,1152]{2,1,0:T(8,128)(2,1)}, bf16[16,48,1152]{2,1,0:T(8,128)(2,1)S(1)}, u32[]{:S(2)}, u32[]{:S(2)}) collective-permute-start(bf16[16,48,1152]{2,1,0:T(8,128)(2,1)} %get-tuple-element.85), channel_id=1, source_target_pairs={{0,1},{1,0},{2,3},{3,2},{4,5},{5,4},{6,7},{7,6},{8,9},{9,8},{10,11... | collective-permute-start | bytes 5308424 | tf_op jit(solution)/shard_map/ppermute | solution.py:46
  193.1 18.1 %collective-permute-start.29 = (bf16[8,144,384]{2,1,0:T(8,128)(2,1)}, bf16[8,144,384]{2,1,0:T(8,128)(2,1)S(1)}, u32[]{:S(2)}, u32[]{:S(2)}) collective-permute-start(bf16[8,144,384]{2,1,0:T(8,128)(2,1)} %get-tuple-element.89), channel_id=1, source_target_pairs={{0,1},{1,0},{2,3},{3,2},{4,5},{5,4},{6,7},{7,6},{8,9},{9,8},{10,11... | collective-permute-start | bytes 2654216 | tf_op jit(solution)/shard_map/ppermute | solution.py:46
  193.5 13.9 %collective-permute-start.28 = (bf16[16,48,384]{2,1,0:T(8,128)(2,1)}, bf16[16,48,384]{2,1,0:T(8,128)(2,1)}, u32[]{:S(2)}, u32[]{:S(2)}) collective-permute-start(bf16[16,48,384]{2,1,0:T(8,128)(2,1)} %get-tuple-element.87), channel_id=1, source_target_pairs={{0,1},{1,0},{2,3},{3,2},{4,5},{5,4},{6,7},{7,6},{8,9},{9,8},{10,11... | collective-permute-start | bytes 1769480 | tf_op jit(solution)/shard_map/ppermute | solution.py:46
  207.0 61.5 %collective-permute-start.43 = (bf16[16,48,384]{2,1,0:T(8,128)(2,1)}, bf16[16,48,384]{2,1,0:T(8,128)(2,1)S(1)}, u32[]{:S(2)}, u32[]{:S(2)}) collective-permute-start(bf16[16,48,384]{2,1,0:T(8,128)(2,1)} %get-tuple-element.104), channel_id=1, source_target_pairs={{0,1},{1,0},{2,3},{3,2},{4,5},{5,4},{6,7},{7,6},{8,9},{9,8},{10,11... | collective-permute-start | bytes 1769480 | tf_op jit(solution)/shard_map/ppermute | solution.py:46
  209.7 37.4 %collective-permute-start.32 = (bf16[8,48,384]{2,1,0:T(8,128)(2,1)}, bf16[8,48,384]{2,1,0:T(8,128)(2,1)S(1)}, u32[]{:S(2)}, u32[]{:S(2)}) collective-permute-start(bf16[8,48,384]{2,1,0:T(8,128)(2,1)} %get-tuple-element.141), channel_id=1, source_target_pairs={{0,4},{1,5},{2,6},{3,7},{4,0},{5,1},{6,2},{7,3},{8,12},{9,13},{10,... | collective-permute-start | bytes 884744 | tf_op jit(solution)/shard_map/ppermute | solution.py:46
  213.3 25.4 %collective-permute-start.30 = (bf16[4,144,384]{2,1,0:T(8,128)(2,1)S(1)}, bf16[4,144,384]{2,1,0:T(8,128)(2,1)}, u32[]{:S(2)}, u32[]{:S(2)}) collective-permute-start(bf16[4,144,384]{2,1,0:T(8,128)(2,1)S(1)} %get-tuple-element.132), channel_id=1, source_target_pairs={{0,4},{1,5},{2,6},{3,7},{4,0},{5,1},{6,2},{7,3},{8,12},{9,13},{10,... | collective-permute-start | bytes 1327112 | tf_op jit(solution)/shard_map/ppermute | solution.py:46
  215.2 33.7 %collective-permute-start.31 = (bf16[8,48,1152]{2,1,0:T(8,128)(2,1)S(1)}, bf16[8,48,1152]{2,1,0:T(8,128)(2,1)S(1)}, u32[]{:S(2)}, u32[]{:S(2)}) collective-permute-start(bf16[8,48,1152]{2,1,0:T(8,128)(2,1)S(1)} %get-tuple-element.127), channel_id=1, source_target_pairs={{0,2},{1,3},{2,0},{3,1},{4,6},{5,7},{6,4},{7,5},{8,10},{9,11},{10,... | collective-permute-start | bytes 2654216 | tf_op jit(solution)/shard_map/ppermute | solution.py:46
  238.6 31.1 %collective-permute-start.42 = (bf16[16,48,384]{2,1,0:T(8,128)(2,1)}, bf16[16,48,384]{2,1,0:T(8,128)(2,1)S(1)}, u32[]{:S(2)}, u32[]{:S(2)}) collective-permute-start(bf16[16,48,384]{2,1,0:T(8,128)(2,1)} %get-tuple-element.102), channel_id=1, source_target_pairs={{0,1},{1,0},{2,3},{3,2},{4,5},{5,4},{6,7},{7,6},{8,9},{9,8},{10,11... | collective-permute-start | bytes 1769480 | tf_op jit(solution)/shard_map/ppermute | solution.py:46
  240.8 22.8 %collective-permute-start.40 = (bf16[144,384]{1,0:T(8,128)(2,1)S(1)}, bf16[144,384]{1,0:T(8,128)(2,1)}, u32[]{:S(2)}, u32[]{:S(2)}) collective-permute-start(bf16[144,384]{1,0:T(8,128)(2,1)S(1)} %get-tuple-element.157), channel_id=1, source_target_pairs={{0,24},{1,25},{2,26},{3,27},{4,28},{5,29},{6,30},{7,31},{8,16},{9,... | collective-permute-start | bytes 331784 | tf_op jit(solution)/shard_map/ppermute | solution.py:46
  247.0 18.2 %collective-permute-start.39 = (bf16[144,384]{1,0:T(8,128)(2,1)S(1)}, bf16[144,384]{1,0:T(8,128)(2,1)}, u32[]{:S(2)}, u32[]{:S(2)}) collective-permute-start(bf16[144,384]{1,0:T(8,128)(2,1)S(1)} %get-tuple-element.158), channel_id=1, source_target_pairs={{0,16},{1,17},{2,18},{3,19},{4,20},{5,21},{6,22},{7,23},{8,24},{9,... | collective-permute-start | bytes 331784 | tf_op jit(solution)/shard_map/ppermute | solution.py:46
  248.9 17.8 %collective-permute-start.38 = (bf16[144,384]{1,0:T(8,128)(2,1)S(1)}, bf16[144,384]{1,0:T(8,128)(2,1)S(1)}, u32[]{:S(2)}, u32[]{:S(2)}) collective-permute-start(bf16[144,384]{1,0:T(8,128)(2,1)S(1)} %get-tuple-element.156), channel_id=1, source_target_pairs={{0,8},{1,9},{2,10},{3,11},{4,12},{5,13},{6,14},{7,15},{8,0},{9,1},... | collective-permute-start | bytes 331784 | tf_op jit(solution)/shard_map/ppermute | solution.py:46
  263.6 9.3 %collective-permute-start.34 = (bf16[4,48,384]{2,1,0:T(8,128)(2,1)}, bf16[4,48,384]{2,1,0:T(8,128)(2,1)S(1)}, u32[]{:S(2)}, u32[]{:S(2)}) collective-permute-start(bf16[4,48,384]{2,1,0:T(8,128)(2,1)} %get-tuple-element.151), channel_id=1, source_target_pairs={{0,2},{1,3},{2,0},{3,1},{4,6},{5,7},{6,4},{7,5},{8,10},{9,11},{10,... | collective-permute-start | bytes 442376 | tf_op jit(solution)/shard_map/ppermute | solution.py:46
  265.2 11.7 %collective-permute-start.33 = (bf16[4,48,1152]{2,1,0:T(8,128)(2,1)S(1)}, bf16[4,48,1152]{2,1,0:T(8,128)(2,1)S(1)}, u32[]{:S(2)}, u32[]{:S(2)}) collective-permute-start(bf16[4,48,1152]{2,1,0:T(8,128)(2,1)S(1)} %get-tuple-element.129), channel_id=1, source_target_pairs={{0,4},{1,5},{2,6},{3,7},{4,0},{5,1},{6,2},{7,3},{8,12},{9,13},{10,... | collective-permute-start | bytes 1327112 | tf_op jit(solution)/shard_map/ppermute | solution.py:46
  269.9 30.4 %collective-permute-start.44 = (bf16[8,48,768]{2,1,0:T(8,128)(2,1)S(1)}, bf16[8,48,768]{2,1,0:T(8,128)(2,1)S(1)}, u32[]{:S(2)}, u32[]{:S(2)}) collective-permute-start(bf16[8,48,768]{2,1,0:T(8,128)(2,1)S(1)} %pad_maximum_fusion.5), channel_id=1, source_target_pairs={{0,2},{1,3},{2,0},{3,1},{4,6},{5,7},{6,4},{7,5},{8,10},{9,11},{10,... | collective-permute-start | bytes 1769480 | tf_op jit(solution)/shard_map/ppermute | solution.py:46
  270.5 21.5 %collective-permute-start.41 = (bf16[72,384]{1,0:T(8,128)(2,1)S(1)}, bf16[72,384]{1,0:T(8,128)(2,1)S(1)}, u32[]{:S(2)}, u32[]{:S(2)}) collective-permute-start(bf16[72,384]{1,0:T(8,128)(2,1)S(1)} %select_convert_fusion), channel_id=1, source_target_pairs={{0,2},{1,3},{2,0},{3,1},{4,6},{5,7},{6,4},{7,5},{8,10},{9,11},{10,... | collective-permute-start | bytes 165896 | tf_op jit(solution)/shard_map/ppermute | solution.py:46
  272.0 30.7 %collective-permute-start.45 = (bf16[16,48,384]{2,1,0:T(8,128)(2,1)}, bf16[16,48,384]{2,1,0:T(8,128)(2,1)S(1)}, u32[]{:S(2)}, u32[]{:S(2)}) collective-permute-start(bf16[16,48,384]{2,1,0:T(8,128)(2,1)} %get-tuple-element.108), channel_id=1, source_target_pairs={{0,1},{1,0},{2,3},{3,2},{4,5},{5,4},{6,7},{7,6},{8,9},{9,8},{10,11... | collective-permute-start | bytes 1769480 | tf_op jit(solution)/shard_map/ppermute | solution.py:46
  277.7 16.3 %collective-permute-start.35 = (bf16[48,1536]{1,0:T(8,128)(2,1)S(1)}, bf16[48,1536]{1,0:T(8,128)(2,1)S(1)}, u32[]{:S(2)}, u32[]{:S(2)}) collective-permute-start(bf16[48,1536]{1,0:T(8,128)(2,1)S(1)} %get-tuple-element.148), channel_id=1, source_target_pairs={{0,8},{1,9},{2,10},{3,11},{4,12},{5,13},{6,14},{7,15},{8,0},{9,1},... | collective-permute-start | bytes 442376 | tf_op jit(solution)/shard_map/ppermute | solution.py:46
  279.1 15.0 %collective-permute-start.36 = (bf16[48,1536]{1,0:T(8,128)(2,1)S(1)}, bf16[48,1536]{1,0:T(8,128)(2,1)S(1)}, u32[]{:S(2)}, u32[]{:S(2)}) collective-permute-start(bf16[48,1536]{1,0:T(8,128)(2,1)S(1)} %get-tuple-element.149), channel_id=1, source_target_pairs={{0,16},{1,17},{2,18},{3,19},{4,20},{5,21},{6,22},{7,23},{8,24},{9,... | collective-permute-start | bytes 442376 | tf_op jit(solution)/shard_map/ppermute | solution.py:46
  294.0 39.7 %collective-permute-start.54 = (f32[36,384]{1,0:T(8,128)S(1)}, f32[36,384]{1,0:T(8,128)S(1)}, u32[]{:S(2)}, u32[]{:S(2)}) collective-permute-start(f32[36,384]{1,0:T(8,128)S(1)} %get-tuple-element.166), channel_id=1, source_target_pairs={{0,1},{1,0},{2,3},{3,2},{4,5},{5,4},{6,7},{7,6},{8,9},{9,8},{10,11... | collective-permute-start | bytes 165896 | tf_op jit(solution)/shard_map/ppermute | solution.py:46
  300.2 34.2 %collective-permute-start.53 = (f32[24,1536]{1,0:T(8,128)S(1)}, f32[24,1536]{1,0:T(8,128)S(1)}, u32[]{:S(2)}, u32[]{:S(2)}) collective-permute-start(f32[24,1536]{1,0:T(8,128)S(1)} %get-tuple-element.160), channel_id=1, source_target_pairs={{0,1},{1,0},{2,3},{3,2},{4,5},{5,4},{6,7},{7,6},{8,9},{9,8},{10,11... | collective-permute-start | bytes 442376 | tf_op jit(solution)/shard_map/ppermute | solution.py:46
  301.2 16.0 %collective-permute-start.46 = (bf16[4,48,768]{2,1,0:T(8,128)(2,1)S(1)}, bf16[4,48,768]{2,1,0:T(8,128)(2,1)S(1)}, u32[]{:S(2)}, u32[]{:S(2)}) collective-permute-start(bf16[4,48,768]{2,1,0:T(8,128)(2,1)S(1)} %get-tuple-element.136), channel_id=1, source_target_pairs={{0,4},{1,5},{2,6},{3,7},{4,0},{5,1},{6,2},{7,3},{8,12},{9,13},{10,... | collective-permute-start | bytes 884744 | tf_op jit(solution)/shard_map/ppermute | solution.py:46
  303.6 15.3 %collective-permute-start.47 = (bf16[8,48,384]{2,1,0:T(8,128)(2,1)S(1)}, bf16[8,48,384]{2,1,0:T(8,128)(2,1)S(1)}, u32[]{:S(2)}, u32[]{:S(2)}) collective-permute-start(bf16[8,48,384]{2,1,0:T(8,128)(2,1)S(1)} %get-tuple-element.133), channel_id=1, source_target_pairs={{0,4},{1,5},{2,6},{3,7},{4,0},{5,1},{6,2},{7,3},{8,12},{9,13},{10,... | collective-permute-start | bytes 884744 | tf_op jit(solution)/shard_map/ppermute | solution.py:46
  316.3 16.0 %collective-permute-start.55 = (f32[768]{0:T(1024)S(1)}, f32[768]{0:T(1024)S(1)}, u32[]{:S(2)}, u32[]{:S(2)}) collective-permute-start(f32[768]{0:T(1024)S(1)} %get-tuple-element.121), channel_id=1, source_target_pairs={{0,16},{1,17},{2,18},{3,19},{4,20},{5,21},{6,22},{7,23},{8,24},{9,... | collective-permute-start | bytes 9224 | tf_op jit(solution)/shard_map/ppermute | solution.py:46
  344.1 7.8 %collective-permute-start.59 = (f32[48]{0:T(128)S(1)}, f32[48]{0:T(128)S(1)}, u32[]{:S(2)}, u32[]{:S(2)}) collective-permute-start(f32[48]{0:T(128)S(1)} %broadcast_select_fusion.16), channel_id=1, source_target_pairs={{0,1},{1,0},{2,3},{3,2},{4,5},{5,4},{6,7},{7,6},{8,9},{9,8},{10,11... | collective-permute-start | bytes 584 | tf_op jit(solution)/shard_map/ppermute | solution.py:46
  350.0 7.4 %collective-permute-start.50 = (bf16[48,1152]{1,0:T(8,128)(2,1)S(1)}, bf16[48,1152]{1,0:T(8,128)(2,1)S(1)}, u32[]{:S(2)}, u32[]{:S(2)}) collective-permute-start(bf16[48,1152]{1,0:T(8,128)(2,1)S(1)} %get-tuple-element.155), channel_id=1, source_target_pairs={{0,16},{1,17},{2,18},{3,19},{4,20},{5,21},{6,22},{7,23},{8,24},{9,... | collective-permute-start | bytes 331784 | tf_op jit(solution)/shard_map/ppermute | solution.py:46
  350.0 7.4 %collective-permute-start.49 = (bf16[48,1152]{1,0:T(8,128)(2,1)S(1)}, bf16[48,1152]{1,0:T(8,128)(2,1)S(1)}, u32[]{:S(2)}, u32[]{:S(2)}) collective-permute-start(bf16[48,1152]{1,0:T(8,128)(2,1)S(1)} %get-tuple-element.153), channel_id=1, source_target_pairs={{0,8},{1,9},{2,10},{3,11},{4,12},{5,13},{6,14},{7,15},{8,0},{9,1},... | collective-permute-start | bytes 331784 | tf_op jit(solution)/shard_map/ppermute | solution.py:46
  (41 other events, 345.4 us)

commit v3 on v2

--- a/solution.py
+++ b/solution.py
@@ -485,9 +485,9 @@
     later = split_columns(
         jnp.concatenate([by_pair[:, 2], by_pair[:, 4], by_pair[:, 3], by_pair[:, 5]], axis=1)
     )
-    own_in = split_columns(in_weight.reshape(24, 2 * FF))
-    own_out = split_columns(out_weight.reshape(24, D))
-    own_mlp = split_columns(mlp_weight.reshape(36, D))
+    own_in = split_columns(after(in_weight.reshape(24, 2 * FF), early))
+    own_out = split_columns(after(out_weight.reshape(24, D), early))
+    own_mlp = split_columns(after(mlp_weight.reshape(36, D), early))
     own_mlp = ordered(ALONG_X, own_mlp, swap(own_mlp, ALONG_X), 0)
 
     line = along_line(early)
@@ -524,21 +524,29 @@
         thirds = [own_mlp[rows * i : rows * (i + 1)] for i in range(3)]
         own = jnp.concatenate([own_in, own_out] + thirds, axis=1)
         line = jnp.stack([own] + parts[1:])
-        return line, line[:, :, :start_mlp], swap(line, ALONG_Y)
+        beside = swap(line[:, :, :start_out], ALONG_X), swap(line[:, :, start_out:], ALONG_Y)
+        return line, line[:, :, :start_mlp], beside
 
     def far(line, head, beside):
-        mlp = jnp.concatenate([line[:, :, start_mlp:], beside[:, :, start_mlp:]])
-        other_head = beside[:, :, :start_mlp]
-        return other_head, swap(jnp.concatenate([head, other_head]), ALONG_X), mlp, swap(mlp, CORE)
-
-    def across(head, other_head, beyond, mlp, mlp_other):
-        both = jnp.concatenate([head, other_head, beyond])
+        beside_in, beside_rest = beside
+        beside_out = beside_rest[:, :, : D // 2]
+        mlp = jnp.concatenate([line[:, :, start_mlp:], beside_rest[:, :, D // 2 :]])
+        far_in = swap(jnp.concatenate([head[:, :, :start_out], beside_in]), ALONG_Y)
+        far_out = swap(jnp.concatenate([head[:, :, start_out:], beside_out]), ALONG_X)
+        return (beside_in, beside_out), (far_in, far_out), mlp, swap(mlp, CORE)
+
+    def across(head, beside, beyond, mlp, mlp_other):
+        all_in = jnp.concatenate([head[:, :, :start_out], beside[0], beyond[0]])
+        all_out = jnp.concatenate([head[:, :, start_out:], beside[1], beyond[1]])
+        both = jnp.concatenate([all_in, all_out], axis=2)
         rest_arrays.extend([both, swap(both, CORE), mlp, mlp_other])
 
-    chips = chip_flips(16, ALONG_Y, ALONG_X)
-    rest_slots = [(0, 16, 0, 0), (1, 16, 0, 1)]
-    in_loads, in_spots = spread_loads(rest_slots, chips, 0, FF, 1, 0)
-    out_loads, out_spots = spread_loads(rest_slots, chips, start_out, D // 2, 0, 0)
+    in_loads, in_spots = spread_loads(
+        [(0, 16, 0, 0), (1, 16, 0, 1)], chip_flips(16, ALONG_X, ALONG_Y), 0, FF, 1, 0
+    )
+    out_loads, out_spots = spread_loads(
+        [(0, 16, 0, 0), (1, 16, 0, 1)], chip_flips(16, ALONG_Y, ALONG_X), start_out, D // 2, 0, 0
+    )
     mlp_loads, mlp_spots = [], []
     for other in (0, 1):
         for block, flips in enumerate(chip_flips(8, ALONG_Y, 0)):
@@ -651,9 +659,9 @@
         (own_mlp,) = forward(0, [], [own_mlp])
         line, head, beside = near(own_mlp)
         (head,) = forward(1, parts, [head])
-        other_head, beyond, mlp, mlp_other = far(line, head, beside)
-        (head,) = forward(2, [], [head])
-        across(head, other_head, beyond, mlp, mlp_other)
+        beside, beyond, mlp, mlp_other = far(line, head, beside)
+        (head,) = forward(2, list(beside), [head])
+        across(head, beside, beyond, mlp, mlp_other)
     else:
         for at in range(GROUPS):
             forward(at, [], [])
@@ -811,33 +819,35 @@
         low, high = total_mlp[:rows], total_mlp[rows:]
         mlp_other = swap(jnp.where(bit_of(ALONG_X), low, high).astype(bf16), ALONG_X)
         mlp_own = jnp.where(bit_of(ALONG_X), high, low)
-        (tokens_grad, gain_first), (later_keep, early_keep, line_own, mlp_own) = last_part(
-            0, [], [], [later_keep, grad_blocks[0][0], line[0], mlp_own]
+        (tokens_grad, gain_first), (later_keep, early_keep) = last_part(
+            0, [], [], [later_keep, grad_blocks[0][0]]
         )
         later_keep, later_send = halved(later_keep, later_got)
         later_got = swap(later_send, ALONG_Y)
         early_keep, early_send = halved(early_keep, early_got)
         early_got = swap(early_send, ALONG_Y)
+        (tokens_grad, gain_last), (later_keep, early_keep) = last_part(
+            1, [tokens_grad], [], [later_keep, early_keep]
+        )
+        gains_grad = jnp.concatenate([(gain_first + gain_last).reshape(-1), gain_mlp_grad.reshape(-1)])
+        gains_keep, gains_got = swap_half(gains_grad, 2 * ALONG_Z)
+        early_keep, early_send = halved(early_keep, early_got)
+        early_got = swap(early_send, ALONG_X)
+        later_line = joined_sum(later_keep, later_got)
+        (output,), (early_keep, line_own, mlp_own) = layer_output(
+            [later_line, gains_got], [early_keep, line[0], mlp_own]
+        )
         total = line_own.astype(f32)
         for got in line_got:
             total = total + got.astype(f32)
         total_mlp = mlp_own + mlp_other.astype(f32)
         joined_mlp = join_columns(total_mlp)
         joined_rest = join_columns(total)
-        (tokens_grad, gain_last), (later_keep, early_keep) = last_part(
-            1, [tokens_grad], line_got + [mlp_other], [later_keep, early_keep]
-        )
-        gains_grad = jnp.concatenate([(gain_first + gain_last).reshape(-1), gain_mlp_grad.reshape(-1)])
-        gains_keep, gains_got = swap_half(gains_grad, 2 * ALONG_Z)
-        early_keep, early_send = halved(early_keep, early_got)
-        early_got = swap(early_send, ALONG_X)
-        later_line = joined_sum(later_keep, later_got)
-        (output,), (early_keep, gains_keep) = layer_output([later_line], [early_keep, gains_keep])
-        gains_share = gains_keep + gains_got
+        early_line = joined_sum(early_keep, early_got)
+        gains_share = after(gains_keep + gains_got, early_line)
         for bits in (ALONG_Z, ALONG_Y, ALONG_X, CORE):
             gains_keep, gains_got = swap_half(gains_share, bits)
             gains_share = gains_keep + gains_got
-        early_line = joined_sum(early_keep, early_got)
         early_later = summed_line(jnp.concatenate([early_line, later_line], axis=2))
         mlp_share = both_columns(joined_mlp, 0, D // 2).reshape(-1)
         in_share = both_columns(joined_rest, 0, FF).reshape(-1)

time: 366 us -> 341 us (0.932)
  waiting for transfers between devices: 61.6 us -> 34.3 us
  starting transfers between devices: 64.9 us -> 54.7 us
  local copies, waits for them, and re-layouts: 17.8 us -> 26 us
    ppermute x60 -> x62, waiting for transfers between devices: 61.6 us -> 34.3 us  [swap(): return lax.ppermute(values, 'fsdp', [(i, i ^ bits) for i in range(32)])]
    ppermute x60 -> x62, starting transfers between devices: 64.9 us -> 54.7 us  [swap(): return lax.ppermute(values, 'fsdp', [(i, i ^ bits) for i in range(32)])]
    slice x4 -> x8, local copies, waits for them, and re-layouts: 3.07 us -> 8.27 us  [the longest x2 2.22 us: far(): mlp = jnp.concatenate([line[:, :, start_mlp:], beside_rest[:, :, D // 2:]])]
    convert_element_type x15, other arithmetic: 15.6 us -> 19.7 us  [joined_sum(): return (kept.astype(f32) + received.astype(f32)).astype(bf16)]
  transfers between devices with their start and end apart: 60 -> 62, of which waited for: 15 -> 12; matrix products, arithmetic and copies ran while one was open for 11% -> 17% of each run, Pallas kernels for 34% -> 37%
where the time goes in v3:
time: 341 us; the launch traced here: 335 us
  Pallas kernels  181 us (53%)
  starting transfers between devices  54.7 us (16%)
  other arithmetic  35.3 us (10%)
  waiting for transfers between devices  34.3 us (10%)
  local copies, waits for them, and re-layouts  26 us (8%)
  between operations  3.71 us (1%)
    pallas_call x10, Pallas kernels, call(): pl.pallas_call(trimmed, grid=(steps,), in_specs=[spec for _, spec in inpu...  181 us
    ppermute x62, starting transfers between devices, swap(): return lax.ppermute(values, 'fsdp', [(i, i ^ bits) for i in range(32)])  54.7 us
    ppermute x62, waiting for transfers between devices, swap(): return lax.ppermute(values, 'fsdp', [(i, i ^ bits) for i in range(32)])  34.3 us
    convert_element_type x15, other arithmetic, joined_sum(): return (kept.astype(f32) + received.astype(f32)).astype(bf16)  19.7 us
  transfers between devices with their start and end apart: 62, of which 12 were waited for; matrix products, arithmetic and copies ran while one was open for 17% of the time, Pallas kernels for 37%

profile of v3, /device:TPU:0, one launch (start us, length us, event | category | flops | bytes accessed | tf_op | source)
XLA Modules:
  0.0 335.3 jit_solution(10116510527469151675)
XLA Ops:
  3.8 3.1 collective-permute-start.1
  6.9 2.6 collective-permute-start.2
  18.8 3.5 %collective-permute-start.12 = (bf16[48,768]{1,0:T(8,128)(2,1)S(1)}, bf16[48,768]{1,0:T(8,128)(2,1)S(1)}, u32[]{:S(2)}, u32[]{:S(2)}) collective-permute-start(bf16[48,768]{1,0:T(8,128)(2,1)S(1)} %fusion.17), channel_id=1, source_target_pairs={{0,16},{1,17},{2,18},{3,19},{4,20},{5,21},{6,22},{7,23},{8,24},{9,... | collective-permute-start | bytes 221192 | tf_op jit(solution)/shard_map/ppermute | solution.py:46
  23.6 1.8 collective-permute-start.9
  26.5 1.9 collective-permute-done.9
  29.8 3.8 %collective-permute-start.21 = (bf16[48,2688]{1,0:T(8,128)(2,1)}, bf16[48,2688]{1,0:T(8,128)(2,1)}, u32[]{:S(2)}, u32[]{:S(2)}) collective-permute-start(bf16[48,2688]{1,0:T(8,128)(2,1)} %broadcast_select_fusion), channel_id=1, source_target_pairs={{0,16},{1,17},{2,18},{3,19},{4,20},{5,21},{6,22},{7,23},{8,24},{9,... | collective-permute-start | bytes 774152 | tf_op jit(solution)/shard_map/ppermute | solution.py:46
  33.7 1.6 collective-permute-start.14
  36.6 7.1 %collective-permute-done.14 = bf16[4,48,768]{2,1,0:T(8,128)(2,1)S(1)} collective-permute-done((bf16[4,48,768]{2,1,0:T(8,128)(2,1)S(1)}, bf16[4,48,768]{2,1,0:T(8,128)(2,1)S(1)}, u32[]{:S(2)}, u32[]{:S(2)}) %collective-permute-start.14) | collective-permute-done | bytes 294944 | tf_op jit(solution)/shard_map/ppermute | solution.py:46
  43.7 1.6 collective-permute-start.15
  45.3 3.1 collective-permute-done.5.refs_6_
  51.5 2.2 collective-permute-done.15.refs_6_.refs_10_
  54.2 14.6 %shard_map.162 = (bf16[2048,2304]{1,0:T(8,128)(2,1)}, bf16[3,4,2,4,256,256]{5,4,3,2,1,0:T(8,128)(2,1)}, bf16[2048,768]{1,0:T(8,128)(2,1)}, bf16[2048,768]{1,0:T(8,128)(2,1)}, bf16[144,384]{1,0:T(8,128)(2,1)}) custom-call(s32[1]{0:T(128)} %bitcast.refs_0_, bf16[2048,768]{1,0:T(8,128)(2,1)} %refs_1_.7, ...), custom_call_target="tpu_custom_call", output_to_operand_aliasing={{4}: (9, {})} | custom-call | flops 4831838208 | bytes 12582912 | tf_op jit(solution)/shard_map/pallas_call | solution.py:440
  71.2 1.3 pad_maximum_fusion
  73.3 1.5 collective-permute-start.23
  76.0 1.5 collective-permute-start.24
  78.5 13.1 %shard_map.163 = (bf16[2048,2304]{1,0:T(8,128)(2,1)}, bf16[3,4,2,4,256,256]{5,4,3,2,1,0:T(8,128)(2,1)}, bf16[2048,768]{1,0:T(8,128)(2,1)}, bf16[4,48,1536]{2,1,0:T(8,128)(2,1)}) custom-call(s32[1]{0:T(128)} %bitcast.refs_0_, ...), custom_call_target="tpu_custom_call", output_to_operand_aliasing={{3}: (12, {}), {0}: (13, {}), {1}: (14, {}), {2}: (15, {})} | custom-call | flops 4831838208 | bytes 12582912 | tf_op jit(solution)/shard_map/pallas_call | solution.py:440
  96.0 13.1 %shard_map.164 = (bf16[2048,2304]{1,0:T(8,128)(2,1)}, bf16[3,4,2,4,256,256]{5,4,3,2,1,0:T(8,128)(2,1)}, bf16[2048,768]{1,0:T(8,128)(2,1)}, bf16[4,48,1536]{2,1,0:T(8,128)(2,1)}) custom-call(s32[1]{0:T(128)} %bitcast.refs_0_, ...), custom_call_target="tpu_custom_call", output_to_operand_aliasing={{3}: (11, {}), {0}: (12, {}), {1}: (13, {}), {2}: (14, {})} | custom-call | flops 4831838208 | bytes 12582912 | tf_op jit(solution)/shard_map/pallas_call | solution.py:440
  111.1 2.8 collective-permute-done.25
  114.0 1.3 maximum_maximum_fusion.refs_5_
  115.3 1.4 slice.494
  117.7 3.5 %collective-permute-done.28.refs_8_.refs_4_ = bf16[8,48,1152]{2,1,0:T(8,128)(2,1)} collective-permute-done((bf16[8,48,1152]{2,1,0:T(8,128)(2,1)S(1)}, bf16[8,48,1152]{2,1,0:T(8,128)(2,1)}, u32[]{:S(2)}, u32[]{:S(2)}) %collective-permute-start.28) | collective-permute-done | bytes 884768 | tf_op jit(solution)/shard_map/ppermute | solution.py:46
  121.3 57.4 %shard_map.165 = (f32[2048,768]{1,0:T(8,128)}, bf16[2048,1152]{1,0:T(8,128)(2,1)}, f32[2048,768]{1,0:T(8,128)}, bf16[2048,768]{1,0:T(8,128)(2,1)}, f32[1,768]{1,...) custom-call(s32[1]{0:T(128)} %bitcast.refs_0_, ...), custom_call_target="tpu_custom_call" | custom-call | flops 36238786560 | bytes 25165824 | tf_op jit(solution)/shard_map/pallas_call | solution.py:440
  179.4 13.2 %shard_map.166 = (bf16[2048,2304]{1,0:T(8,128)(2,1)}, bf16[16,48,384]{2,1,0:T(8,128)(2,1)}, bf16[16,48,384]{2,1,0:T(8,128)(2,1)}, bf16[16,48,1152]{2,1,0:T(8,128...) custom-call(s32[1]{0:T(128)} %bitcast.refs_0_, ...), custom_call_target="tpu_custom_call", output_to_operand_aliasing={{3}: (7, {}), {4}: (8, {}), {5}: (9, {})} | custom-call | flops 4831838208 | bytes 12582912 | tf_op jit(solution)/shard_map/pallas_call | solution.py:440
  193.1 2.3 add_convert_fusion.17
  195.9 2.1 add_convert_fusion.7
  198.0 1.5 collective-permute-start.32
  199.6 1.4 add_convert_fusion
  201.4 22.9 %shard_map.167 = (bf16[2048,2304]{1,0:T(8,128)(2,1)}, bf16[16,48,384]{2,1,0:T(8,128)(2,1)}, bf16[16,48,384]{2,1,0:T(8,128)(2,1)}, bf16[8,48,1152]{2,1,0:T(8,128)...) custom-call(s32[1]{0:T(128)} %bitcast.refs_0_, ...), custom_call_target="tpu_custom_call", output_to_operand_aliasing={{3}: (7, {}), {4}: (8, {}), {5}: (9, {}), {0}: (10, {})} | custom-call | flops 4831838208 | bytes 12582912 | tf_op jit(solution)/shard_map/pallas_call | solution.py:440
  224.4 1.8 add_convert_fusion.22
  226.2 1.6 collective-permute-start.43
  232.5 13.3 %shard_map.168 = (bf16[2048,2304]{1,0:T(8,128)(2,1)}, bf16[16,48,384]{2,1,0:T(8,128)(2,1)}, bf16[16,48,384]{2,1,0:T(8,128)(2,1)}, bf16[4,48,1152]{2,1,0:T(8,128)...) custom-call(s32[1]{0:T(128)} %bitcast.refs_0_, ...), custom_call_target="tpu_custom_call", output_to_operand_aliasing={{3}: (8, {}), {4}: (9, {}), {5}: (10, {}), {6}: (11, {}), {... | custom-call | flops 4831838208 | bytes 12582912 | tf_op jit(solution)/shard_map/pallas_call | solution.py:440
  245.8 2.9 collective-permute-start.44
  253.3 1.6 collective-permute-start.56
  256.5 11.0 %shard_map.169 = (f32[2048,768]{1,0:T(8,128)}, f32[1,768]{1,0:T(1,128)}, bf16[8,48,768]{2,1,0:T(8,128)(2,1)}, bf16[16,48,384]{2,1,0:T(8,128)(2,1)}) custom-call(s32[1]{0:T(128)} %bitcast.refs_0_, bf16[2048,768]{1,0:T(8,128)(2,1)} %refs_1_.7, f32[1,768]{1,0:T(1,128)} %reshape.333.refs_2_, ...), custom_call_target="tpu_custom_call", output_to_operand_aliasing={{2}: (13, {}), {3}: (14, {})} | custom-call | flops 3623878656 | bytes 15728640 | tf_op jit(solution)/shard_map/pallas_call | solution.py:440
  269.9 1.9 add_convert_fusion.12
  271.9 1.5 collective-permute-start.39
  274.7 10.8 %shard_map.170 = (f32[2048,768]{1,0:T(8,128)}, f32[1,768]{1,0:T(1,128)}, bf16[4,48,768]{2,1,0:T(8,128)(2,1)}, bf16[8,48,384]{2,1,0:T(8,128)(2,1)}) custom-call(s32[1]{0:T(128)} %bitcast.refs_0_, bf16[2048,768]{1,0:T(8,128)(2,1)} %refs_1_.7, f32[1,768]{1,0:T(1,128)} %reshape.333.refs_2_, ...), custom_call_target="tpu_custom_call", output_to_operand_aliasing={{2}: (13, {}), {3}: (14, {}), {0}: (15, {})} | custom-call | flops 3623878656 | bytes 15728640 | tf_op jit(solution)/shard_map/pallas_call | solution.py:440
  286.3 2.9 collective-permute-start.52
  289.2 1.7 add_convert_fusion.9.refs_5_
  291.0 1.7 add_convert_fusion.20
  292.7 2.8 collective-permute-done.40.refs_6_
  296.1 11.6 %shard_map.171 = (bf16[2048,768]{1,0:T(8,128)(2,1)}, bf16[4,48,384]{2,1,0:T(8,128)(2,1)}, bf16[48,1536]{1,0:T(8,128)(2,1)}, f32[72,384]{1,0:T(8,128)}) custom-call(s32[1]{0:T(128)} %bitcast.refs_0_, f32[2048,768]{1,0:T(8,128)} %get-tuple-element.74.refs_1_, ...), custom_call_target="tpu_custom_call", output_to_operand_aliasing={{1}: (7, {}), {2}: (8, {}), {3}: (9, {})} | custom-call | flops 3623878656 | bytes 18874368 | tf_op jit(solution)/shard_map/pallas_call | solution.py:440
  310.9 3.1 collective-permute-done.47
  317.5 2.9 collective-permute-done.58
  320.5 1.5 collective-permute-start.59
  322.1 1.3 collective-permute-start.50
  323.6 2.9 collective-permute-start.48
  327.2 3.0 collective-permute-done.60
  (267 shorter events, 62.4 us)
Async XLA Ops:
  3.0 12.4 %collective-permute-start.10 = (bf16[24,768]{1,0:T(8,128)(2,1)S(1)}, bf16[24,768]{1,0:T(8,128)(2,1)S(1)}, u32[]{:S(2)}, u32[]{:S(2)}) collective-permute-start(bf16[24,768]{1,0:T(8,128)(2,1)S(1)} %get-tuple-element.185), channel_id=1, source_target_pairs={{0,1},{1,0},{2,3},{3,2},{4,5},{5,4},{6,7},{7,6},{8,9},{9,8},{10,11... | collective-permute-start | bytes 110600 | tf_op jit(solution)/shard_map/ppermute | solution.py:46
  3.8 13.4 %collective-permute-start.1 = (bf16[48,512]{1,0:T(8,128)(2,1)S(1)}, bf16[48,512]{1,0:T(8,128)(2,1)S(1)}, u32[]{:S(2)}, u32[]{:S(2)}) collective-permute-start(bf16[48,512]{1,0:T(8,128)(2,1)S(1)} %maximum_select_fusion.12), channel_id=1, source_target_pairs={{0,8},{1,9},{2,10},{3,11},{4,12},{5,13},{6,14},{7,15},{8,0},{9,1},... | collective-permute-start | bytes 147464 | tf_op jit(solution)/shard_map/ppermute | solution.py:46
  6.9 11.9 %collective-permute-start.2 = (bf16[48,512]{1,0:T(8,128)(2,1)S(1)}, bf16[48,512]{1,0:T(8,128)(2,1)S(1)}, u32[]{:S(2)}, u32[]{:S(2)}) collective-permute-start(bf16[48,512]{1,0:T(8,128)(2,1)S(1)} %maximum_select_fusion.12), channel_id=1, source_target_pairs={{0,16},{1,17},{2,18},{3,19},{4,20},{5,21},{6,22},{7,23},{8,24},{9,... | collective-permute-start | bytes 147464 | tf_op jit(solution)/shard_map/ppermute | solution.py:46
  9.5 13.5 %collective-permute-start.3 = (bf16[48,512]{1,0:T(8,128)(2,1)S(1)}, bf16[48,512]{1,0:T(8,128)(2,1)S(1)}, u32[]{:S(2)}, u32[]{:S(2)}) collective-permute-start(bf16[48,512]{1,0:T(8,128)(2,1)S(1)} %maximum_select_fusion.12), channel_id=1, source_target_pairs={{0,24},{1,25},{2,26},{3,27},{4,28},{5,29},{6,30},{7,31},{8,16},{9,... | collective-permute-start | bytes 147464 | tf_op jit(solution)/shard_map/ppermute | solution.py:46
  12.4 11.2 %collective-permute-start.18 = (bf16[24,1152]{1,0:T(8,128)(2,1)S(1)}, bf16[24,1152]{1,0:T(8,128)(2,1)S(1)}, u32[]{:S(2)}, u32[]{:S(2)}) collective-permute-start(bf16[24,1152]{1,0:T(8,128)(2,1)S(1)} %get-tuple-element.177), channel_id=1, source_target_pairs={{0,1},{1,0},{2,3},{3,2},{4,5},{5,4},{6,7},{7,6},{8,9},{9,8},{10,11... | collective-permute-start | bytes 165896 | tf_op jit(solution)/shard_map/ppermute | solution.py:46
  16.8 8.6 %collective-permute-start.19 = (bf16[24,384]{1,0:T(8,128)(2,1)S(1)}, bf16[24,384]{1,0:T(8,128)(2,1)S(1)}, u32[]{:S(2)}, u32[]{:S(2)}) collective-permute-start(bf16[24,384]{1,0:T(8,128)(2,1)S(1)} %get-tuple-element.197), channel_id=1, source_target_pairs={{0,1},{1,0},{2,3},{3,2},{4,5},{5,4},{6,7},{7,6},{8,9},{9,8},{10,11... | collective-permute-start | bytes 55304 | tf_op jit(solution)/shard_map/ppermute | solution.py:46
  17.2 12.6 %collective-permute-start.11 = (bf16[48,768]{1,0:T(8,128)(2,1)S(1)}, bf16[48,768]{1,0:T(8,128)(2,1)S(1)}, u32[]{:S(2)}, u32[]{:S(2)}) collective-permute-start(bf16[48,768]{1,0:T(8,128)(2,1)S(1)} %fusion.17), channel_id=1, source_target_pairs={{0,8},{1,9},{2,10},{3,11},{4,12},{5,13},{6,14},{7,15},{8,0},{9,1},... | collective-permute-start | bytes 221192 | tf_op jit(solution)/shard_map/ppermute | solution.py:46
  18.8 14.8 %collective-permute-start.12 = (bf16[48,768]{1,0:T(8,128)(2,1)S(1)}, bf16[48,768]{1,0:T(8,128)(2,1)S(1)}, u32[]{:S(2)}, u32[]{:S(2)}) collective-permute-start(bf16[48,768]{1,0:T(8,128)(2,1)S(1)} %fusion.17), channel_id=1, source_target_pairs={{0,16},{1,17},{2,18},{3,19},{4,20},{5,21},{6,22},{7,23},{8,24},{9,... | collective-permute-start | bytes 221192 | tf_op jit(solution)/shard_map/ppermute | solution.py:46
  22.9 10.7 %collective-permute-start.13 = (bf16[48,768]{1,0:T(8,128)(2,1)S(1)}, bf16[48,768]{1,0:T(8,128)(2,1)S(1)}, u32[]{:S(2)}, u32[]{:S(2)}) collective-permute-start(bf16[48,768]{1,0:T(8,128)(2,1)S(1)} %fusion.17), channel_id=1, source_target_pairs={{0,24},{1,25},{2,26},{3,27},{4,28},{5,29},{6,30},{7,31},{8,16},{9,... | collective-permute-start | bytes 221192 | tf_op jit(solution)/shard_map/ppermute | solution.py:46
  25.4 9.9 %collective-permute-start.4 = (bf16[4,48,512]{2,1,0:T(8,128)(2,1)S(1)}, bf16[4,48,512]{2,1,0:T(8,128)(2,1)S(1)}, u32[]{:S(2)}, u32[]{:S(2)}) collective-permute-start(bf16[4,48,512]{2,1,0:T(8,128)(2,1)S(1)} %pad_maximum_fusion.7), channel_id=1, source_target_pairs={{0,2},{1,3},{2,0},{3,1},{4,6},{5,7},{6,4},{7,5},{8,10},{9,11},{10,... | collective-permute-start | bytes 589832 | tf_op jit(solution)/shard_map/ppermute | solution.py:46
  29.2 41.9 %collective-permute-start.20 = (bf16[48,2688]{1,0:T(8,128)(2,1)}, bf16[48,2688]{1,0:T(8,128)(2,1)}, u32[]{:S(2)}, u32[]{:S(2)}) collective-permute-start(bf16[48,2688]{1,0:T(8,128)(2,1)} %broadcast_select_fusion), channel_id=1, source_target_pairs={{0,8},{1,9},{2,10},{3,11},{4,12},{5,13},{6,14},{7,15},{8,0},{9,1},... | collective-permute-start | bytes 774152 | tf_op jit(solution)/shard_map/ppermute | solution.py:46
  29.8 41.3 %collective-permute-start.21 = (bf16[48,2688]{1,0:T(8,128)(2,1)}, bf16[48,2688]{1,0:T(8,128)(2,1)}, u32[]{:S(2)}, u32[]{:S(2)}) collective-permute-start(bf16[48,2688]{1,0:T(8,128)(2,1)} %broadcast_select_fusion), channel_id=1, source_target_pairs={{0,16},{1,17},{2,18},{3,19},{4,20},{5,21},{6,22},{7,23},{8,24},{9,... | collective-permute-start | bytes 774152 | tf_op jit(solution)/shard_map/ppermute | solution.py:46
  33.7 10.0 %collective-permute-start.14 = (bf16[4,48,768]{2,1,0:T(8,128)(2,1)S(1)}, bf16[4,48,768]{2,1,0:T(8,128)(2,1)S(1)}, u32[]{:S(2)}, u32[]{:S(2)}) collective-permute-start(bf16[4,48,768]{2,1,0:T(8,128)(2,1)S(1)} %pad_maximum_fusion.5), channel_id=1, source_target_pairs={{0,4},{1,5},{2,6},{3,7},{4,0},{5,1},{6,2},{7,3},{8,12},{9,13},{10,... | collective-permute-start | bytes 884744 | tf_op jit(solution)/shard_map/ppermute | solution.py:46
  36.0 12.4 %collective-permute-start.5 = (bf16[8,48,512]{2,1,0:T(8,128)(2,1)S(1)}, bf16[8,48,512]{2,1,0:T(8,128)(2,1)S(1)}, u32[]{:S(2)}, u32[]{:S(2)}) collective-permute-start(bf16[8,48,512]{2,1,0:T(8,128)(2,1)S(1)} %get-tuple-element.166.refs_5_), channel_id=1, source_target_pairs={{0,4},{1,5},{2,6},{3,7},{4,0},{5,1},{6,2},{7,3},{8,12},{9,13},{10,... | collective-permute-start | bytes 1179656 | tf_op jit(solution)/shard_map/ppermute | solution.py:46
  36.5 14.5 %collective-permute-start.6 = (bf16[8,48,512]{2,1,0:T(8,128)(2,1)S(1)}, bf16[8,48,512]{2,1,0:T(8,128)(2,1)S(1)}, u32[]{:S(2)}, u32[]{:S(2)}) collective-permute-start(bf16[8,48,512]{2,1,0:T(8,128)(2,1)S(1)} %get-tuple-element.166.refs_5_), channel_id=1, source_target_pairs={{0,1},{1,0},{2,3},{3,2},{4,5},{5,4},{6,7},{7,6},{8,9},{9,8},{10,11... | collective-permute-start | bytes 1179656 | tf_op jit(solution)/shard_map/ppermute | solution.py:46
  43.7 9.9 %collective-permute-start.15 = (bf16[8,48,768]{2,1,0:T(8,128)(2,1)S(1)}, bf16[8,48,768]{2,1,0:T(8,128)(2,1)S(1)}, u32[]{:S(2)}, u32[]{:S(2)}) collective-permute-start(bf16[8,48,768]{2,1,0:T(8,128)(2,1)S(1)} %constant_dynamic-update-slice_fusion.11.refs_5_.refs_9_), channel_id=1, source_target_pairs={{0,2},{1,3},{2,0},{3,1},{4,6},{5,7},{6,4},{7,5},{8,10},{9,11},{10,... | collective-permute-start | bytes 1769480 | tf_op jit(solution)/shard_map/ppermute | solution.py:46
  51.0 20.2 %collective-permute-start.22 = (bf16[48,2688]{1,0:T(8,128)(2,1)}, bf16[48,2688]{1,0:T(8,128)(2,1)S(1)}, u32[]{:S(2)}, u32[]{:S(2)}) collective-permute-start(bf16[48,2688]{1,0:T(8,128)(2,1)} %broadcast_select_fusion), channel_id=1, source_target_pairs={{0,24},{1,25},{2,26},{3,27},{4,28},{5,29},{6,30},{7,31},{8,16},{9,... | collective-permute-start | bytes 774152 | tf_op jit(solution)/shard_map/ppermute | solution.py:46
  53.7 23.8 %collective-permute-start.16 = (bf16[8,48,768]{2,1,0:T(8,128)(2,1)S(1)}, bf16[8,48,768]{2,1,0:T(8,128)(2,1)S(1)}, u32[]{:S(2)}, u32[]{:S(2)}) collective-permute-start(bf16[8,48,768]{2,1,0:T(8,128)(2,1)S(1)} %constant_dynamic-update-slice_fusion.11.refs_5_.refs_9_), channel_id=1, source_target_pairs={{0,1},{1,0},{2,3},{3,2},{4,5},{5,4},{6,7},{7,6},{8,9},{9,8},{10,11... | collective-permute-start | bytes 1769480 | tf_op jit(solution)/shard_map/ppermute | solution.py:46
  53.7 23.8 %collective-permute-start.17 = (bf16[8,48,768]{2,1,0:T(8,128)(2,1)S(1)}, bf16[8,48,768]{2,1,0:T(8,128)(2,1)S(1)}, u32[]{:S(2)}, u32[]{:S(2)}) collective-permute-start(bf16[8,48,768]{2,1,0:T(8,128)(2,1)S(1)} %collective-permute-done.15.refs_6_.refs_10_), channel_id=1, source_target_pairs={{0,1},{1,0},{2,3},{3,2},{4,5},{5,4},{6,7},{7,6},{8,9},{9,8},{10,11... | collective-permute-start | bytes 1769480 | tf_op jit(solution)/shard_map/ppermute | solution.py:46
  73.3 19.4 %collective-permute-start.23 = (bf16[4,48,1152]{2,1,0:T(8,128)(2,1)S(1)}, bf16[4,48,1152]{2,1,0:T(8,128)(2,1)S(1)}, u32[]{:S(2)}, u32[]{:S(2)}) collective-permute-start(bf16[4,48,1152]{2,1,0:T(8,128)(2,1)S(1)} %get-tuple-element.142), channel_id=1, source_target_pairs={{0,2},{1,3},{2,0},{3,1},{4,6},{5,7},{6,4},{7,5},{8,10},{9,11},{10,... | collective-permute-start | bytes 1327112 | tf_op jit(solution)/shard_map/ppermute | solution.py:46
  76.0 18.4 %collective-permute-start.24 = (bf16[4,48,1536]{2,1,0:T(8,128)(2,1)}, bf16[4,48,1536]{2,1,0:T(8,128)(2,1)}, u32[]{:S(2)}, u32[]{:S(2)}) collective-permute-start(bf16[4,48,1536]{2,1,0:T(8,128)(2,1)} %get-tuple-element.144), channel_id=1, source_target_pairs={{0,4},{1,5},{2,6},{3,7},{4,0},{5,1},{6,2},{7,3},{8,12},{9,13},{10,... | collective-permute-start | bytes 1769480 | tf_op jit(solution)/shard_map/ppermute | solution.py:46
  92.8 21.1 %collective-permute-start.25 = (bf16[8,48,1152]{2,1,0:T(8,128)(2,1)S(1)}, bf16[8,48,1152]{2,1,0:T(8,128)(2,1)S(1)}, u32[]{:S(2)}, u32[]{:S(2)}) collective-permute-start(bf16[8,48,1152]{2,1,0:T(8,128)(2,1)S(1)} %pad_maximum_fusion.1), channel_id=1, source_target_pairs={{0,4},{1,5},{2,6},{3,7},{4,0},{5,1},{6,2},{7,3},{8,12},{9,13},{10,... | collective-permute-start | bytes 2654216 | tf_op jit(solution)/shard_map/ppermute | solution.py:46
  95.3 15.8 %collective-permute-start.26 = (bf16[8,48,384]{2,1,0:T(8,128)(2,1)S(1)}, bf16[8,48,384]{2,1,0:T(8,128)(2,1)S(1)}, u32[]{:S(2)}, u32[]{:S(2)}) collective-permute-start(bf16[8,48,384]{2,1,0:T(8,128)(2,1)S(1)} %pad_maximum_fusion.6), channel_id=1, source_target_pairs={{0,2},{1,3},{2,0},{3,1},{4,6},{5,7},{6,4},{7,5},{8,10},{9,11},{10,... | collective-permute-start | bytes 884744 | tf_op jit(solution)/shard_map/ppermute | solution.py:46
  178.7 20.9 %collective-permute-start.29 = (bf16[16,48,1152]{2,1,0:T(8,128)(2,1)}, bf16[16,48,1152]{2,1,0:T(8,128)(2,1)S(1)}, u32[]{:S(2)}, u32[]{:S(2)}) collective-permute-start(bf16[16,48,1152]{2,1,0:T(8,128)(2,1)} %get-tuple-element.84), channel_id=1, source_target_pairs={{0,1},{1,0},{2,3},{3,2},{4,5},{5,4},{6,7},{7,6},{8,9},{9,8},{10,11... | collective-permute-start | bytes 5308424 | tf_op jit(solution)/shard_map/ppermute | solution.py:46
  178.9 17.0 %collective-permute-start.31 = (bf16[8,144,384]{2,1,0:T(8,128)(2,1)}, bf16[8,144,384]{2,1,0:T(8,128)(2,1)S(1)}, u32[]{:S(2)}, u32[]{:S(2)}) collective-permute-start(bf16[8,144,384]{2,1,0:T(8,128)(2,1)} %get-tuple-element.88), channel_id=1, source_target_pairs={{0,1},{1,0},{2,3},{3,2},{4,5},{5,4},{6,7},{7,6},{8,9},{9,8},{10,11... | collective-permute-start | bytes 2654216 | tf_op jit(solution)/shard_map/ppermute | solution.py:46
  179.3 13.8 %collective-permute-start.30 = (bf16[16,48,384]{2,1,0:T(8,128)(2,1)}, bf16[16,48,384]{2,1,0:T(8,128)(2,1)}, u32[]{:S(2)}, u32[]{:S(2)}) collective-permute-start(bf16[16,48,384]{2,1,0:T(8,128)(2,1)} %get-tuple-element.86), channel_id=1, source_target_pairs={{0,1},{1,0},{2,3},{3,2},{4,5},{5,4},{6,7},{7,6},{8,9},{9,8},{10,11... | collective-permute-start | bytes 1769480 | tf_op jit(solution)/shard_map/ppermute | solution.py:46
  192.7 53.2 %collective-permute-start.36 = (bf16[16,48,384]{2,1,0:T(8,128)(2,1)}, bf16[16,48,384]{2,1,0:T(8,128)(2,1)S(1)}, u32[]{:S(2)}, u32[]{:S(2)}) collective-permute-start(bf16[16,48,384]{2,1,0:T(8,128)(2,1)} %get-tuple-element.100), channel_id=1, source_target_pairs={{0,1},{1,0},{2,3},{3,2},{4,5},{5,4},{6,7},{7,6},{8,9},{9,8},{10,11... | collective-permute-start | bytes 1769480 | tf_op jit(solution)/shard_map/ppermute | solution.py:46
  195.4 29.0 %collective-permute-start.34 = (bf16[8,48,384]{2,1,0:T(8,128)(2,1)}, bf16[8,48,384]{2,1,0:T(8,128)(2,1)S(1)}, u32[]{:S(2)}, u32[]{:S(2)}) collective-permute-start(bf16[8,48,384]{2,1,0:T(8,128)(2,1)} %get-tuple-element.139), channel_id=1, source_target_pairs={{0,4},{1,5},{2,6},{3,7},{4,0},{5,1},{6,2},{7,3},{8,12},{9,13},{10,... | collective-permute-start | bytes 884744 | tf_op jit(solution)/shard_map/ppermute | solution.py:46
  198.0 29.7 %collective-permute-start.32 = (bf16[4,144,384]{2,1,0:T(8,128)(2,1)S(1)}, bf16[4,144,384]{2,1,0:T(8,128)(2,1)}, u32[]{:S(2)}, u32[]{:S(2)}) collective-permute-start(bf16[4,144,384]{2,1,0:T(8,128)(2,1)S(1)} %get-tuple-element.130), channel_id=1, source_target_pairs={{0,4},{1,5},{2,6},{3,7},{4,0},{5,1},{6,2},{7,3},{8,12},{9,13},{10,... | collective-permute-start | bytes 1327112 | tf_op jit(solution)/shard_map/ppermute | solution.py:46
  200.9 30.1 %collective-permute-start.33 = (bf16[8,48,1152]{2,1,0:T(8,128)(2,1)S(1)}, bf16[8,48,1152]{2,1,0:T(8,128)(2,1)S(1)}, u32[]{:S(2)}, u32[]{:S(2)}) collective-permute-start(bf16[8,48,1152]{2,1,0:T(8,128)(2,1)S(1)} %get-tuple-element.125), channel_id=1, source_target_pairs={{0,2},{1,3},{2,0},{3,1},{4,6},{5,7},{6,4},{7,5},{8,10},{9,11},{10,... | collective-permute-start | bytes 2654216 | tf_op jit(solution)/shard_map/ppermute | solution.py:46
  224.3 25.7 %collective-permute-start.35 = (bf16[16,48,384]{2,1,0:T(8,128)(2,1)}, bf16[16,48,384]{2,1,0:T(8,128)(2,1)S(1)}, u32[]{:S(2)}, u32[]{:S(2)}) collective-permute-start(bf16[16,48,384]{2,1,0:T(8,128)(2,1)} %get-tuple-element.98), channel_id=1, source_target_pairs={{0,1},{1,0},{2,3},{3,2},{4,5},{5,4},{6,7},{7,6},{8,9},{9,8},{10,11... | collective-permute-start | bytes 1769480 | tf_op jit(solution)/shard_map/ppermute | solution.py:46
  226.2 29.4 %collective-permute-start.43 = (bf16[4,48,384]{2,1,0:T(8,128)(2,1)}, bf16[4,48,384]{2,1,0:T(8,128)(2,1)S(1)}, u32[]{:S(2)}, u32[]{:S(2)}) collective-permute-start(bf16[4,48,384]{2,1,0:T(8,128)(2,1)} %get-tuple-element.153), channel_id=1, source_target_pairs={{0,2},{1,3},{2,0},{3,1},{4,6},{5,7},{6,4},{7,5},{8,10},{9,11},{10,... | collective-permute-start | bytes 442376 | tf_op jit(solution)/shard_map/ppermute | solution.py:46
  229.8 21.9 %collective-permute-start.46 = (bf16[144,384]{1,0:T(8,128)(2,1)}, bf16[144,384]{1,0:T(8,128)(2,1)}, u32[]{:S(2)}, u32[]{:S(2)}) collective-permute-start(bf16[144,384]{1,0:T(8,128)(2,1)} %get-tuple-element.159), channel_id=1, source_target_pairs={{0,24},{1,25},{2,26},{3,27},{4,28},{5,29},{6,30},{7,31},{8,16},{9,... | collective-permute-start | bytes 331784 | tf_op jit(solution)/shard_map/ppermute | solution.py:46
  231.1 20.7 %collective-permute-start.45 = (bf16[144,384]{1,0:T(8,128)(2,1)}, bf16[144,384]{1,0:T(8,128)(2,1)S(1)}, u32[]{:S(2)}, u32[]{:S(2)}) collective-permute-start(bf16[144,384]{1,0:T(8,128)(2,1)} %get-tuple-element.160), channel_id=1, source_target_pairs={{0,16},{1,17},{2,18},{3,19},{4,20},{5,21},{6,22},{7,23},{8,24},{9,... | collective-permute-start | bytes 331784 | tf_op jit(solution)/shard_map/ppermute | solution.py:46
  251.2 18.7 %collective-permute-start.37 = (bf16[8,48,768]{2,1,0:T(8,128)(2,1)S(1)}, bf16[8,48,768]{2,1,0:T(8,128)(2,1)S(1)}, u32[]{:S(2)}, u32[]{:S(2)}) collective-permute-start(bf16[8,48,768]{2,1,0:T(8,128)(2,1)S(1)} %pad_maximum_fusion.4), channel_id=1, source_target_pairs={{0,2},{1,3},{2,0},{3,1},{4,6},{5,7},{6,4},{7,5},{8,10},{9,11},{10,... | collective-permute-start | bytes 1769480 | tf_op jit(solution)/shard_map/ppermute | solution.py:46
  251.8 21.6 %collective-permute-start.38 = (bf16[16,48,384]{2,1,0:T(8,128)(2,1)}, bf16[16,48,384]{2,1,0:T(8,128)(2,1)S(1)}, u32[]{:S(2)}, u32[]{:S(2)}) collective-permute-start(bf16[16,48,384]{2,1,0:T(8,128)(2,1)} %get-tuple-element.104), channel_id=1, source_target_pairs={{0,1},{1,0},{2,3},{3,2},{4,5},{5,4},{6,7},{7,6},{8,9},{9,8},{10,11... | collective-permute-start | bytes 1769480 | tf_op jit(solution)/shard_map/ppermute | solution.py:46
  251.8 15.8 %collective-permute-start.42 = (bf16[4,48,1152]{2,1,0:T(8,128)(2,1)}, bf16[4,48,1152]{2,1,0:T(8,128)(2,1)S(1)}, u32[]{:S(2)}, u32[]{:S(2)}) collective-permute-start(bf16[4,48,1152]{2,1,0:T(8,128)(2,1)} %get-tuple-element.127), channel_id=1, source_target_pairs={{0,4},{1,5},{2,6},{3,7},{4,0},{5,1},{6,2},{7,3},{8,12},{9,13},{10,... | collective-permute-start | bytes 1327112 | tf_op jit(solution)/shard_map/ppermute | solution.py:46
  253.3 56.0 %collective-permute-start.56 = (bf16[72,384]{1,0:T(8,128)(2,1)S(1)}, bf16[72,384]{1,0:T(8,128)(2,1)S(1)}, u32[]{:S(2)}, u32[]{:S(2)}) collective-permute-start(bf16[72,384]{1,0:T(8,128)(2,1)S(1)} %select_convert_fusion), channel_id=1, source_target_pairs={{0,2},{1,3},{2,0},{3,1},{4,6},{5,7},{6,4},{7,5},{8,10},{9,11},{10,... | collective-permute-start | bytes 165896 | tf_op jit(solution)/shard_map/ppermute | solution.py:46
  268.4 39.3 %collective-permute-start.54 = (bf16[48,1536]{1,0:T(8,128)(2,1)S(1)}, bf16[48,1536]{1,0:T(8,128)(2,1)S(1)}, u32[]{:S(2)}, u32[]{:S(2)}) collective-permute-start(bf16[48,1536]{1,0:T(8,128)(2,1)S(1)} %get-tuple-element.149), channel_id=1, source_target_pairs={{0,24},{1,25},{2,26},{3,27},{4,28},{5,29},{6,30},{7,31},{8,16},{9,... | collective-permute-start | bytes 442376 | tf_op jit(solution)/shard_map/ppermute | solution.py:46
  269.6 38.1 %collective-permute-start.53 = (bf16[48,1536]{1,0:T(8,128)(2,1)S(1)}, bf16[48,1536]{1,0:T(8,128)(2,1)S(1)}, u32[]{:S(2)}, u32[]{:S(2)}) collective-permute-start(bf16[48,1536]{1,0:T(8,128)(2,1)S(1)} %get-tuple-element.150), channel_id=1, source_target_pairs={{0,16},{1,17},{2,18},{3,19},{4,20},{5,21},{6,22},{7,23},{8,24},{9,... | collective-permute-start | bytes 442376 | tf_op jit(solution)/shard_map/ppermute | solution.py:46
  271.9 14.5 %collective-permute-start.39 = (bf16[4,48,768]{2,1,0:T(8,128)(2,1)S(1)}, bf16[4,48,768]{2,1,0:T(8,128)(2,1)S(1)}, u32[]{:S(2)}, u32[]{:S(2)}) collective-permute-start(bf16[4,48,768]{2,1,0:T(8,128)(2,1)S(1)} %get-tuple-element.134), channel_id=1, source_target_pairs={{0,4},{1,5},{2,6},{3,7},{4,0},{5,1},{6,2},{7,3},{8,12},{9,13},{10,... | collective-permute-start | bytes 884744 | tf_op jit(solution)/shard_map/ppermute | solution.py:46
  274.2 16.8 %collective-permute-start.41 = (bf16[8,48,384]{2,1,0:T(8,128)(2,1)S(1)}, bf16[8,48,384]{2,1,0:T(8,128)(2,1)S(1)}, u32[]{:S(2)}, u32[]{:S(2)}) collective-permute-start(bf16[8,48,384]{2,1,0:T(8,128)(2,1)S(1)} %get-tuple-element.131), channel_id=1, source_target_pairs={{0,4},{1,5},{2,6},{3,7},{4,0},{5,1},{6,2},{7,3},{8,12},{9,13},{10,... | collective-permute-start | bytes 884744 | tf_op jit(solution)/shard_map/ppermute | solution.py:46
  286.3 21.4 %collective-permute-start.52 = (bf16[48,1536]{1,0:T(8,128)(2,1)S(1)}, bf16[48,1536]{1,0:T(8,128)(2,1)S(1)}, u32[]{:S(2)}, u32[]{:S(2)}) collective-permute-start(bf16[48,1536]{1,0:T(8,128)(2,1)S(1)} %get-tuple-element.147), channel_id=1, source_target_pairs={{0,8},{1,9},{2,10},{3,11},{4,12},{5,13},{6,14},{7,15},{8,0},{9,1},... | collective-permute-start | bytes 442376 | tf_op jit(solution)/shard_map/ppermute | solution.py:46
  309.4 17.2 %collective-permute-start.55 = (f32[24,1536]{1,0:T(8,128)S(1)}, f32[24,1536]{1,0:T(8,128)S(1)}, u32[]{:S(2)}, u32[]{:S(2)}) collective-permute-start(f32[24,1536]{1,0:T(8,128)S(1)} %get-tuple-element.162), channel_id=1, source_target_pairs={{0,1},{1,0},{2,3},{3,2},{4,5},{5,4},{6,7},{7,6},{8,9},{9,8},{10,11... | collective-permute-start | bytes 442376 | tf_op jit(solution)/shard_map/ppermute | solution.py:46
  310.3 6.6 %collective-permute-start.57 = (f32[36,384]{1,0:T(8,128)S(1)}, f32[36,384]{1,0:T(8,128)S(1)}, u32[]{:S(2)}, u32[]{:S(2)}) collective-permute-start(f32[36,384]{1,0:T(8,128)S(1)} %get-tuple-element.168), channel_id=1, source_target_pairs={{0,1},{1,0},{2,3},{3,2},{4,5},{5,4},{6,7},{7,6},{8,9},{9,8},{10,11... | collective-permute-start | bytes 165896 | tf_op jit(solution)/shard_map/ppermute | solution.py:46
  322.1 10.3 %collective-permute-start.50 = (bf16[48,1152]{1,0:T(8,128)(2,1)S(1)}, bf16[48,1152]{1,0:T(8,128)(2,1)S(1)}, u32[]{:S(2)}, u32[]{:S(2)}) collective-permute-start(bf16[48,1152]{1,0:T(8,128)(2,1)S(1)} %get-tuple-element.156), channel_id=1, source_target_pairs={{0,24},{1,25},{2,26},{3,27},{4,28},{5,29},{6,30},{7,31},{8,16},{9,... | collective-permute-start | bytes 331784 | tf_op jit(solution)/shard_map/ppermute | solution.py:46
  323.4 9.0 %collective-permute-start.49 = (bf16[48,1152]{1,0:T(8,128)(2,1)S(1)}, bf16[48,1152]{1,0:T(8,128)(2,1)S(1)}, u32[]{:S(2)}, u32[]{:S(2)}) collective-permute-start(bf16[48,1152]{1,0:T(8,128)(2,1)S(1)} %get-tuple-element.157), channel_id=1, source_target_pairs={{0,16},{1,17},{2,18},{3,19},{4,20},{5,21},{6,22},{7,23},{8,24},{9,... | collective-permute-start | bytes 331784 | tf_op jit(solution)/shard_map/ppermute | solution.py:46
  323.6 8.7 %collective-permute-start.48 = (bf16[48,1152]{1,0:T(8,128)(2,1)S(1)}, bf16[48,1152]{1,0:T(8,128)(2,1)S(1)}, u32[]{:S(2)}, u32[]{:S(2)}) collective-permute-start(bf16[48,1152]{1,0:T(8,128)(2,1)S(1)} %get-tuple-element.155), channel_id=1, source_target_pairs={{0,8},{1,9},{2,10},{3,11},{4,12},{5,13},{6,14},{7,15},{8,0},{9,1},... | collective-permute-start | bytes 331784 | tf_op jit(solution)/shard_map/ppermute | solution.py:46
  (40 other events, 249.0 us)

commit v4 on v3

--- a/solution.py
+++ b/solution.py
@@ -835,7 +835,7 @@
         early_got = swap(early_send, ALONG_X)
         later_line = joined_sum(later_keep, later_got)
         (output,), (early_keep, line_own, mlp_own) = layer_output(
-            [later_line, gains_got], [early_keep, line[0], mlp_own]
+            [later_line], [early_keep, line[0], mlp_own]
         )
         total = line_own.astype(f32)
         for got in line_got:

time: 341 us -> 338 us (level)
  waiting for transfers between devices: 34.3 us -> 29.8 us
    ppermute x62, waiting for transfers between devices: 34.3 us -> 29.8 us  [swap(): return lax.ppermute(values, 'fsdp', [(i, i ^ bits) for i in range(32)])]
  transfers between devices with their start and end apart: 62 -> 62, of which waited for: 12 -> 11; matrix products, arithmetic and copies ran while one was open for 17% -> 17% of each run, Pallas kernels for 37% -> 37%
where the time goes in v4:
time: 338 us; the launch traced here: 331 us
  Pallas kernels  181 us (54%)
  starting transfers between devices  56.5 us (17%)
  other arithmetic  34.6 us (10%)
  waiting for transfers between devices  29.8 us (9%)
  local copies, waits for them, and re-layouts  25.4 us (8%)
  between operations  3.73 us (1%)
    pallas_call x10, Pallas kernels, call(): pl.pallas_call(trimmed, grid=(steps,), in_specs=[spec for _, spec in inpu...  181 us
    ppermute x62, starting transfers between devices, swap(): return lax.ppermute(values, 'fsdp', [(i, i ^ bits) for i in range(32)])  56.5 us
    ppermute x62, waiting for transfers between devices, swap(): return lax.ppermute(values, 'fsdp', [(i, i ^ bits) for i in range(32)])  29.8 us
    convert_element_type x15, other arithmetic, joined_sum(): return (kept.astype(f32) + received.astype(f32)).astype(bf16)  19.7 us
  transfers between devices with their start and end apart: 62, of which 11 were waited for; matrix products, arithmetic and copies ran while one was open for 17% of the time, Pallas kernels for 37%

profile of v4, /device:TPU:0, one launch (start us, length us, event | category | flops | bytes accessed | tf_op | source)
XLA Modules:
  0.0 331.3 jit_solution(1179598659072717305)
XLA Ops:
  3.8 3.1 collective-permute-start.1
  6.9 2.6 collective-permute-start.2
  18.8 3.5 %collective-permute-start.12 = (bf16[48,768]{1,0:T(8,128)(2,1)S(1)}, bf16[48,768]{1,0:T(8,128)(2,1)S(1)}, u32[]{:S(2)}, u32[]{:S(2)}) collective-permute-start(bf16[48,768]{1,0:T(8,128)(2,1)S(1)} %fusion.17), channel_id=1, source_target_pairs={{0,16},{1,17},{2,18},{3,19},{4,20},{5,21},{6,22},{7,23},{8,24},{9,... | collective-permute-start | bytes 221192 | tf_op jit(solution)/shard_map/ppermute | solution.py:46
  23.6 1.8 collective-permute-start.9
  26.5 1.9 collective-permute-done.9
  29.8 3.8 %collective-permute-start.21 = (bf16[48,2688]{1,0:T(8,128)(2,1)}, bf16[48,2688]{1,0:T(8,128)(2,1)}, u32[]{:S(2)}, u32[]{:S(2)}) collective-permute-start(bf16[48,2688]{1,0:T(8,128)(2,1)} %broadcast_select_fusion), channel_id=1, source_target_pairs={{0,16},{1,17},{2,18},{3,19},{4,20},{5,21},{6,22},{7,23},{8,24},{9,... | collective-permute-start | bytes 774152 | tf_op jit(solution)/shard_map/ppermute | solution.py:46
  33.7 1.6 collective-permute-start.14
  36.6 7.1 %collective-permute-done.14 = bf16[4,48,768]{2,1,0:T(8,128)(2,1)S(1)} collective-permute-done((bf16[4,48,768]{2,1,0:T(8,128)(2,1)S(1)}, bf16[4,48,768]{2,1,0:T(8,128)(2,1)S(1)}, u32[]{:S(2)}, u32[]{:S(2)}) %collective-permute-start.14) | collective-permute-done | bytes 294944 | tf_op jit(solution)/shard_map/ppermute | solution.py:46
  43.7 1.6 collective-permute-start.15
  45.3 3.1 collective-permute-done.5.refs_6_
  51.5 2.2 collective-permute-done.15.refs_6_.refs_10_
  54.2 14.5 %shard_map.162 = (bf16[2048,2304]{1,0:T(8,128)(2,1)}, bf16[3,4,2,4,256,256]{5,4,3,2,1,0:T(8,128)(2,1)}, bf16[2048,768]{1,0:T(8,128)(2,1)}, bf16[2048,768]{1,0:T(8,128)(2,1)}, bf16[144,384]{1,0:T(8,128)(2,1)}) custom-call(s32[1]{0:T(128)} %bitcast.refs_0_, bf16[2048,768]{1,0:T(8,128)(2,1)} %refs_1_.7, ...), custom_call_target="tpu_custom_call", output_to_operand_aliasing={{4}: (9, {})} | custom-call | flops 4831838208 | bytes 12582912 | tf_op jit(solution)/shard_map/pallas_call | solution.py:440
  71.2 1.3 pad_maximum_fusion
  73.3 1.5 collective-permute-start.23
  76.0 1.5 collective-permute-start.24
  78.5 13.1 %shard_map.163 = (bf16[2048,2304]{1,0:T(8,128)(2,1)}, bf16[3,4,2,4,256,256]{5,4,3,2,1,0:T(8,128)(2,1)}, bf16[2048,768]{1,0:T(8,128)(2,1)}, bf16[4,48,1536]{2,1,0:T(8,128)(2,1)}) custom-call(s32[1]{0:T(128)} %bitcast.refs_0_, ...), custom_call_target="tpu_custom_call", output_to_operand_aliasing={{3}: (12, {}), {0}: (13, {}), {1}: (14, {}), {2}: (15, {})} | custom-call | flops 4831838208 | bytes 12582912 | tf_op jit(solution)/shard_map/pallas_call | solution.py:440
  95.9 13.1 %shard_map.164 = (bf16[2048,2304]{1,0:T(8,128)(2,1)}, bf16[3,4,2,4,256,256]{5,4,3,2,1,0:T(8,128)(2,1)}, bf16[2048,768]{1,0:T(8,128)(2,1)}, bf16[4,48,1536]{2,1,0:T(8,128)(2,1)}) custom-call(s32[1]{0:T(128)} %bitcast.refs_0_, ...), custom_call_target="tpu_custom_call", output_to_operand_aliasing={{3}: (11, {}), {0}: (12, {}), {1}: (13, {}), {2}: (14, {})} | custom-call | flops 4831838208 | bytes 12582912 | tf_op jit(solution)/shard_map/pallas_call | solution.py:440
  111.1 2.8 collective-permute-done.25
  113.9 1.3 maximum_maximum_fusion.refs_5_
  115.3 1.4 slice.494
  117.7 3.5 %collective-permute-done.28.refs_8_.refs_4_ = bf16[8,48,1152]{2,1,0:T(8,128)(2,1)} collective-permute-done((bf16[8,48,1152]{2,1,0:T(8,128)(2,1)S(1)}, bf16[8,48,1152]{2,1,0:T(8,128)(2,1)}, u32[]{:S(2)}, u32[]{:S(2)}) %collective-permute-start.28) | collective-permute-done | bytes 884768 | tf_op jit(solution)/shard_map/ppermute | solution.py:46
  121.2 57.5 %shard_map.165 = (f32[2048,768]{1,0:T(8,128)}, bf16[2048,1152]{1,0:T(8,128)(2,1)}, f32[2048,768]{1,0:T(8,128)}, bf16[2048,768]{1,0:T(8,128)(2,1)}, f32[1,768]{1,...) custom-call(s32[1]{0:T(128)} %bitcast.refs_0_, ...), custom_call_target="tpu_custom_call" | custom-call | flops 36238786560 | bytes 25165824 | tf_op jit(solution)/shard_map/pallas_call | solution.py:440
  179.4 13.3 %shard_map.166 = (bf16[2048,2304]{1,0:T(8,128)(2,1)}, bf16[16,48,384]{2,1,0:T(8,128)(2,1)}, bf16[16,48,384]{2,1,0:T(8,128)(2,1)}, bf16[16,48,1152]{2,1,0:T(8,128...) custom-call(s32[1]{0:T(128)} %bitcast.refs_0_, ...), custom_call_target="tpu_custom_call", output_to_operand_aliasing={{3}: (7, {}), {4}: (8, {}), {5}: (9, {})} | custom-call | flops 4831838208 | bytes 12582912 | tf_op jit(solution)/shard_map/pallas_call | solution.py:440
  193.2 2.3 add_convert_fusion.17
  196.0 2.1 add_convert_fusion.7
  198.2 1.5 collective-permute-start.32
  199.7 1.4 add_convert_fusion
  201.5 22.8 %shard_map.167 = (bf16[2048,2304]{1,0:T(8,128)(2,1)}, bf16[16,48,384]{2,1,0:T(8,128)(2,1)}, bf16[16,48,384]{2,1,0:T(8,128)(2,1)}, bf16[8,48,1152]{2,1,0:T(8,128)...) custom-call(s32[1]{0:T(128)} %bitcast.refs_0_, ...), custom_call_target="tpu_custom_call", output_to_operand_aliasing={{3}: (7, {}), {4}: (8, {}), {5}: (9, {}), {0}: (10, {})} | custom-call | flops 4831838208 | bytes 12582912 | tf_op jit(solution)/shard_map/pallas_call | solution.py:440
  224.4 1.8 add_convert_fusion.22
  226.2 1.6 collective-permute-start.42
  227.8 1.3 add_convert_fusion.5.refs_7_
  229.9 1.2 collective-permute-start.45
  232.6 13.3 %shard_map.168 = (bf16[2048,2304]{1,0:T(8,128)(2,1)}, bf16[16,48,384]{2,1,0:T(8,128)(2,1)}, bf16[16,48,384]{2,1,0:T(8,128)(2,1)}, bf16[4,48,1152]{2,1,0:T(8,128)...) custom-call(s32[1]{0:T(128)} %bitcast.refs_0_, ...), custom_call_target="tpu_custom_call", output_to_operand_aliasing={{3}: (8, {}), {4}: (9, {}), {5}: (10, {}), {6}: (11, {}), {... | custom-call | flops 4831838208 | bytes 12582912 | tf_op jit(solution)/shard_map/pallas_call | solution.py:440
  245.9 2.9 collective-permute-start.43
  253.4 1.6 collective-permute-start.55
  256.6 11.0 %shard_map.169 = (f32[2048,768]{1,0:T(8,128)}, f32[1,768]{1,0:T(1,128)}, bf16[8,48,768]{2,1,0:T(8,128)(2,1)}, bf16[16,48,384]{2,1,0:T(8,128)(2,1)}) custom-call(s32[1]{0:T(128)} %bitcast.refs_0_, bf16[2048,768]{1,0:T(8,128)(2,1)} %refs_1_.7, f32[1,768]{1,0:T(1,128)} %reshape.333.refs_2_, ...), custom_call_target="tpu_custom_call", output_to_operand_aliasing={{2}: (13, {}), {3}: (14, {})} | custom-call | flops 3623878656 | bytes 15728640 | tf_op jit(solution)/shard_map/pallas_call | solution.py:440
  270.0 1.9 add_convert_fusion.12
  271.9 1.5 collective-permute-start.39
  274.8 10.8 %shard_map.170 = (f32[2048,768]{1,0:T(8,128)}, f32[1,768]{1,0:T(1,128)}, bf16[4,48,768]{2,1,0:T(8,128)(2,1)}, bf16[8,48,384]{2,1,0:T(8,128)(2,1)}) custom-call(s32[1]{0:T(128)} %bitcast.refs_0_, bf16[2048,768]{1,0:T(8,128)(2,1)} %refs_1_.7, f32[1,768]{1,0:T(1,128)} %reshape.333.refs_2_, ...), custom_call_target="tpu_custom_call", output_to_operand_aliasing={{2}: (13, {}), {3}: (14, {}), {0}: (15, {})} | custom-call | flops 3623878656 | bytes 15728640 | tf_op jit(solution)/shard_map/pallas_call | solution.py:440
  286.3 2.9 collective-permute-start.51
  289.2 1.7 add_convert_fusion.9.refs_5_
  291.0 1.7 add_convert_fusion.20
  292.7 11.6 %shard_map.171 = (bf16[2048,768]{1,0:T(8,128)(2,1)}, bf16[4,48,384]{2,1,0:T(8,128)(2,1)}, bf16[48,1536]{1,0:T(8,128)(2,1)}, f32[72,384]{1,0:T(8,128)}) custom-call(s32[1]{0:T(128)} %bitcast.refs_0_, f32[2048,768]{1,0:T(8,128)} %get-tuple-element.74.refs_1_, ...), custom_call_target="tpu_custom_call", output_to_operand_aliasing={{1}: (6, {}), {2}: (7, {}), {3}: (8, {})} | custom-call | flops 3623878656 | bytes 18874368 | tf_op jit(solution)/shard_map/pallas_call | solution.py:440
  307.5 3.1 collective-permute-done.46
  312.8 1.8 collective-permute-start.58
  316.6 1.5 collective-permute-start.59
  318.1 2.4 collective-permute-start.49
  323.2 3.0 collective-permute-done.60
  (265 shorter events, 61.4 us)
Async XLA Ops:
  3.0 12.4 %collective-permute-start.10 = (bf16[24,768]{1,0:T(8,128)(2,1)S(1)}, bf16[24,768]{1,0:T(8,128)(2,1)S(1)}, u32[]{:S(2)}, u32[]{:S(2)}) collective-permute-start(bf16[24,768]{1,0:T(8,128)(2,1)S(1)} %get-tuple-element.185), channel_id=1, source_target_pairs={{0,1},{1,0},{2,3},{3,2},{4,5},{5,4},{6,7},{7,6},{8,9},{9,8},{10,11... | collective-permute-start | bytes 110600 | tf_op jit(solution)/shard_map/ppermute | solution.py:46
  3.8 13.4 %collective-permute-start.1 = (bf16[48,512]{1,0:T(8,128)(2,1)S(1)}, bf16[48,512]{1,0:T(8,128)(2,1)S(1)}, u32[]{:S(2)}, u32[]{:S(2)}) collective-permute-start(bf16[48,512]{1,0:T(8,128)(2,1)S(1)} %maximum_select_fusion.12), channel_id=1, source_target_pairs={{0,8},{1,9},{2,10},{3,11},{4,12},{5,13},{6,14},{7,15},{8,0},{9,1},... | collective-permute-start | bytes 147464 | tf_op jit(solution)/shard_map/ppermute | solution.py:46
  6.9 11.9 %collective-permute-start.2 = (bf16[48,512]{1,0:T(8,128)(2,1)S(1)}, bf16[48,512]{1,0:T(8,128)(2,1)S(1)}, u32[]{:S(2)}, u32[]{:S(2)}) collective-permute-start(bf16[48,512]{1,0:T(8,128)(2,1)S(1)} %maximum_select_fusion.12), channel_id=1, source_target_pairs={{0,16},{1,17},{2,18},{3,19},{4,20},{5,21},{6,22},{7,23},{8,24},{9,... | collective-permute-start | bytes 147464 | tf_op jit(solution)/shard_map/ppermute | solution.py:46
  9.5 13.5 %collective-permute-start.3 = (bf16[48,512]{1,0:T(8,128)(2,1)S(1)}, bf16[48,512]{1,0:T(8,128)(2,1)S(1)}, u32[]{:S(2)}, u32[]{:S(2)}) collective-permute-start(bf16[48,512]{1,0:T(8,128)(2,1)S(1)} %maximum_select_fusion.12), channel_id=1, source_target_pairs={{0,24},{1,25},{2,26},{3,27},{4,28},{5,29},{6,30},{7,31},{8,16},{9,... | collective-permute-start | bytes 147464 | tf_op jit(solution)/shard_map/ppermute | solution.py:46
  12.4 11.2 %collective-permute-start.18 = (bf16[24,1152]{1,0:T(8,128)(2,1)S(1)}, bf16[24,1152]{1,0:T(8,128)(2,1)S(1)}, u32[]{:S(2)}, u32[]{:S(2)}) collective-permute-start(bf16[24,1152]{1,0:T(8,128)(2,1)S(1)} %get-tuple-element.177), channel_id=1, source_target_pairs={{0,1},{1,0},{2,3},{3,2},{4,5},{5,4},{6,7},{7,6},{8,9},{9,8},{10,11... | collective-permute-start | bytes 165896 | tf_op jit(solution)/shard_map/ppermute | solution.py:46
  16.8 8.6 %collective-permute-start.19 = (bf16[24,384]{1,0:T(8,128)(2,1)S(1)}, bf16[24,384]{1,0:T(8,128)(2,1)S(1)}, u32[]{:S(2)}, u32[]{:S(2)}) collective-permute-start(bf16[24,384]{1,0:T(8,128)(2,1)S(1)} %get-tuple-element.197), channel_id=1, source_target_pairs={{0,1},{1,0},{2,3},{3,2},{4,5},{5,4},{6,7},{7,6},{8,9},{9,8},{10,11... | collective-permute-start | bytes 55304 | tf_op jit(solution)/shard_map/ppermute | solution.py:46
  17.2 12.6 %collective-permute-start.11 = (bf16[48,768]{1,0:T(8,128)(2,1)S(1)}, bf16[48,768]{1,0:T(8,128)(2,1)S(1)}, u32[]{:S(2)}, u32[]{:S(2)}) collective-permute-start(bf16[48,768]{1,0:T(8,128)(2,1)S(1)} %fusion.17), channel_id=1, source_target_pairs={{0,8},{1,9},{2,10},{3,11},{4,12},{5,13},{6,14},{7,15},{8,0},{9,1},... | collective-permute-start | bytes 221192 | tf_op jit(solution)/shard_map/ppermute | solution.py:46
  18.8 14.8 %collective-permute-start.12 = (bf16[48,768]{1,0:T(8,128)(2,1)S(1)}, bf16[48,768]{1,0:T(8,128)(2,1)S(1)}, u32[]{:S(2)}, u32[]{:S(2)}) collective-permute-start(bf16[48,768]{1,0:T(8,128)(2,1)S(1)} %fusion.17), channel_id=1, source_target_pairs={{0,16},{1,17},{2,18},{3,19},{4,20},{5,21},{6,22},{7,23},{8,24},{9,... | collective-permute-start | bytes 221192 | tf_op jit(solution)/shard_map/ppermute | solution.py:46
  22.9 10.7 %collective-permute-start.13 = (bf16[48,768]{1,0:T(8,128)(2,1)S(1)}, bf16[48,768]{1,0:T(8,128)(2,1)S(1)}, u32[]{:S(2)}, u32[]{:S(2)}) collective-permute-start(bf16[48,768]{1,0:T(8,128)(2,1)S(1)} %fusion.17), channel_id=1, source_target_pairs={{0,24},{1,25},{2,26},{3,27},{4,28},{5,29},{6,30},{7,31},{8,16},{9,... | collective-permute-start | bytes 221192 | tf_op jit(solution)/shard_map/ppermute | solution.py:46
  25.4 9.9 %collective-permute-start.4 = (bf16[4,48,512]{2,1,0:T(8,128)(2,1)S(1)}, bf16[4,48,512]{2,1,0:T(8,128)(2,1)S(1)}, u32[]{:S(2)}, u32[]{:S(2)}) collective-permute-start(bf16[4,48,512]{2,1,0:T(8,128)(2,1)S(1)} %pad_maximum_fusion.7), channel_id=1, source_target_pairs={{0,2},{1,3},{2,0},{3,1},{4,6},{5,7},{6,4},{7,5},{8,10},{9,11},{10,... | collective-permute-start | bytes 589832 | tf_op jit(solution)/shard_map/ppermute | solution.py:46
  29.2 41.9 %collective-permute-start.20 = (bf16[48,2688]{1,0:T(8,128)(2,1)}, bf16[48,2688]{1,0:T(8,128)(2,1)}, u32[]{:S(2)}, u32[]{:S(2)}) collective-permute-start(bf16[48,2688]{1,0:T(8,128)(2,1)} %broadcast_select_fusion), channel_id=1, source_target_pairs={{0,8},{1,9},{2,10},{3,11},{4,12},{5,13},{6,14},{7,15},{8,0},{9,1},... | collective-permute-start | bytes 774152 | tf_op jit(solution)/shard_map/ppermute | solution.py:46
  29.8 41.3 %collective-permute-start.21 = (bf16[48,2688]{1,0:T(8,128)(2,1)}, bf16[48,2688]{1,0:T(8,128)(2,1)}, u32[]{:S(2)}, u32[]{:S(2)}) collective-permute-start(bf16[48,2688]{1,0:T(8,128)(2,1)} %broadcast_select_fusion), channel_id=1, source_target_pairs={{0,16},{1,17},{2,18},{3,19},{4,20},{5,21},{6,22},{7,23},{8,24},{9,... | collective-permute-start | bytes 774152 | tf_op jit(solution)/shard_map/ppermute | solution.py:46
  33.7 10.0 %collective-permute-start.14 = (bf16[4,48,768]{2,1,0:T(8,128)(2,1)S(1)}, bf16[4,48,768]{2,1,0:T(8,128)(2,1)S(1)}, u32[]{:S(2)}, u32[]{:S(2)}) collective-permute-start(bf16[4,48,768]{2,1,0:T(8,128)(2,1)S(1)} %pad_maximum_fusion.5), channel_id=1, source_target_pairs={{0,4},{1,5},{2,6},{3,7},{4,0},{5,1},{6,2},{7,3},{8,12},{9,13},{10,... | collective-permute-start | bytes 884744 | tf_op jit(solution)/shard_map/ppermute | solution.py:46
  36.0 12.4 %collective-permute-start.5 = (bf16[8,48,512]{2,1,0:T(8,128)(2,1)S(1)}, bf16[8,48,512]{2,1,0:T(8,128)(2,1)S(1)}, u32[]{:S(2)}, u32[]{:S(2)}) collective-permute-start(bf16[8,48,512]{2,1,0:T(8,128)(2,1)S(1)} %get-tuple-element.166.refs_5_), channel_id=1, source_target_pairs={{0,4},{1,5},{2,6},{3,7},{4,0},{5,1},{6,2},{7,3},{8,12},{9,13},{10,... | collective-permute-start | bytes 1179656 | tf_op jit(solution)/shard_map/ppermute | solution.py:46
  36.5 14.5 %collective-permute-start.6 = (bf16[8,48,512]{2,1,0:T(8,128)(2,1)S(1)}, bf16[8,48,512]{2,1,0:T(8,128)(2,1)S(1)}, u32[]{:S(2)}, u32[]{:S(2)}) collective-permute-start(bf16[8,48,512]{2,1,0:T(8,128)(2,1)S(1)} %get-tuple-element.166.refs_5_), channel_id=1, source_target_pairs={{0,1},{1,0},{2,3},{3,2},{4,5},{5,4},{6,7},{7,6},{8,9},{9,8},{10,11... | collective-permute-start | bytes 1179656 | tf_op jit(solution)/shard_map/ppermute | solution.py:46
  43.7 9.9 %collective-permute-start.15 = (bf16[8,48,768]{2,1,0:T(8,128)(2,1)S(1)}, bf16[8,48,768]{2,1,0:T(8,128)(2,1)S(1)}, u32[]{:S(2)}, u32[]{:S(2)}) collective-permute-start(bf16[8,48,768]{2,1,0:T(8,128)(2,1)S(1)} %constant_dynamic-update-slice_fusion.11.refs_5_.refs_9_), channel_id=1, source_target_pairs={{0,2},{1,3},{2,0},{3,1},{4,6},{5,7},{6,4},{7,5},{8,10},{9,11},{10,... | collective-permute-start | bytes 1769480 | tf_op jit(solution)/shard_map/ppermute | solution.py:46
  51.0 20.2 %collective-permute-start.22 = (bf16[48,2688]{1,0:T(8,128)(2,1)}, bf16[48,2688]{1,0:T(8,128)(2,1)S(1)}, u32[]{:S(2)}, u32[]{:S(2)}) collective-permute-start(bf16[48,2688]{1,0:T(8,128)(2,1)} %broadcast_select_fusion), channel_id=1, source_target_pairs={{0,24},{1,25},{2,26},{3,27},{4,28},{5,29},{6,30},{7,31},{8,16},{9,... | collective-permute-start | bytes 774152 | tf_op jit(solution)/shard_map/ppermute | solution.py:46
  53.7 23.8 %collective-permute-start.16 = (bf16[8,48,768]{2,1,0:T(8,128)(2,1)S(1)}, bf16[8,48,768]{2,1,0:T(8,128)(2,1)S(1)}, u32[]{:S(2)}, u32[]{:S(2)}) collective-permute-start(bf16[8,48,768]{2,1,0:T(8,128)(2,1)S(1)} %constant_dynamic-update-slice_fusion.11.refs_5_.refs_9_), channel_id=1, source_target_pairs={{0,1},{1,0},{2,3},{3,2},{4,5},{5,4},{6,7},{7,6},{8,9},{9,8},{10,11... | collective-permute-start | bytes 1769480 | tf_op jit(solution)/shard_map/ppermute | solution.py:46
  53.7 23.8 %collective-permute-start.17 = (bf16[8,48,768]{2,1,0:T(8,128)(2,1)S(1)}, bf16[8,48,768]{2,1,0:T(8,128)(2,1)S(1)}, u32[]{:S(2)}, u32[]{:S(2)}) collective-permute-start(bf16[8,48,768]{2,1,0:T(8,128)(2,1)S(1)} %collective-permute-done.15.refs_6_.refs_10_), channel_id=1, source_target_pairs={{0,1},{1,0},{2,3},{3,2},{4,5},{5,4},{6,7},{7,6},{8,9},{9,8},{10,11... | collective-permute-start | bytes 1769480 | tf_op jit(solution)/shard_map/ppermute | solution.py:46
  73.3 19.4 %collective-permute-start.23 = (bf16[4,48,1152]{2,1,0:T(8,128)(2,1)S(1)}, bf16[4,48,1152]{2,1,0:T(8,128)(2,1)S(1)}, u32[]{:S(2)}, u32[]{:S(2)}) collective-permute-start(bf16[4,48,1152]{2,1,0:T(8,128)(2,1)S(1)} %get-tuple-element.142), channel_id=1, source_target_pairs={{0,2},{1,3},{2,0},{3,1},{4,6},{5,7},{6,4},{7,5},{8,10},{9,11},{10,... | collective-permute-start | bytes 1327112 | tf_op jit(solution)/shard_map/ppermute | solution.py:46
  76.0 18.3 %collective-permute-start.24 = (bf16[4,48,1536]{2,1,0:T(8,128)(2,1)}, bf16[4,48,1536]{2,1,0:T(8,128)(2,1)}, u32[]{:S(2)}, u32[]{:S(2)}) collective-permute-start(bf16[4,48,1536]{2,1,0:T(8,128)(2,1)} %get-tuple-element.144), channel_id=1, source_target_pairs={{0,4},{1,5},{2,6},{3,7},{4,0},{5,1},{6,2},{7,3},{8,12},{9,13},{10,... | collective-permute-start | bytes 1769480 | tf_op jit(solution)/shard_map/ppermute | solution.py:46
  92.8 21.1 %collective-permute-start.25 = (bf16[8,48,1152]{2,1,0:T(8,128)(2,1)S(1)}, bf16[8,48,1152]{2,1,0:T(8,128)(2,1)S(1)}, u32[]{:S(2)}, u32[]{:S(2)}) collective-permute-start(bf16[8,48,1152]{2,1,0:T(8,128)(2,1)S(1)} %pad_maximum_fusion.1), channel_id=1, source_target_pairs={{0,4},{1,5},{2,6},{3,7},{4,0},{5,1},{6,2},{7,3},{8,12},{9,13},{10,... | collective-permute-start | bytes 2654216 | tf_op jit(solution)/shard_map/ppermute | solution.py:46
  95.3 15.8 %collective-permute-start.26 = (bf16[8,48,384]{2,1,0:T(8,128)(2,1)S(1)}, bf16[8,48,384]{2,1,0:T(8,128)(2,1)S(1)}, u32[]{:S(2)}, u32[]{:S(2)}) collective-permute-start(bf16[8,48,384]{2,1,0:T(8,128)(2,1)S(1)} %pad_maximum_fusion.6), channel_id=1, source_target_pairs={{0,2},{1,3},{2,0},{3,1},{4,6},{5,7},{6,4},{7,5},{8,10},{9,11},{10,... | collective-permute-start | bytes 884744 | tf_op jit(solution)/shard_map/ppermute | solution.py:46
  178.7 20.9 %collective-permute-start.29 = (bf16[16,48,1152]{2,1,0:T(8,128)(2,1)}, bf16[16,48,1152]{2,1,0:T(8,128)(2,1)S(1)}, u32[]{:S(2)}, u32[]{:S(2)}) collective-permute-start(bf16[16,48,1152]{2,1,0:T(8,128)(2,1)} %get-tuple-element.84), channel_id=1, source_target_pairs={{0,1},{1,0},{2,3},{3,2},{4,5},{5,4},{6,7},{7,6},{8,9},{9,8},{10,11... | collective-permute-start | bytes 5308424 | tf_op jit(solution)/shard_map/ppermute | solution.py:46
  178.9 17.1 %collective-permute-start.31 = (bf16[8,144,384]{2,1,0:T(8,128)(2,1)}, bf16[8,144,384]{2,1,0:T(8,128)(2,1)S(1)}, u32[]{:S(2)}, u32[]{:S(2)}) collective-permute-start(bf16[8,144,384]{2,1,0:T(8,128)(2,1)} %get-tuple-element.88), channel_id=1, source_target_pairs={{0,1},{1,0},{2,3},{3,2},{4,5},{5,4},{6,7},{7,6},{8,9},{9,8},{10,11... | collective-permute-start | bytes 2654216 | tf_op jit(solution)/shard_map/ppermute | solution.py:46
  179.3 13.9 %collective-permute-start.30 = (bf16[16,48,384]{2,1,0:T(8,128)(2,1)}, bf16[16,48,384]{2,1,0:T(8,128)(2,1)}, u32[]{:S(2)}, u32[]{:S(2)}) collective-permute-start(bf16[16,48,384]{2,1,0:T(8,128)(2,1)} %get-tuple-element.86), channel_id=1, source_target_pairs={{0,1},{1,0},{2,3},{3,2},{4,5},{5,4},{6,7},{7,6},{8,9},{9,8},{10,11... | collective-permute-start | bytes 1769480 | tf_op jit(solution)/shard_map/ppermute | solution.py:46
  192.8 53.1 %collective-permute-start.36 = (bf16[16,48,384]{2,1,0:T(8,128)(2,1)}, bf16[16,48,384]{2,1,0:T(8,128)(2,1)S(1)}, u32[]{:S(2)}, u32[]{:S(2)}) collective-permute-start(bf16[16,48,384]{2,1,0:T(8,128)(2,1)} %get-tuple-element.100), channel_id=1, source_target_pairs={{0,1},{1,0},{2,3},{3,2},{4,5},{5,4},{6,7},{7,6},{8,9},{9,8},{10,11... | collective-permute-start | bytes 1769480 | tf_op jit(solution)/shard_map/ppermute | solution.py:46
  195.5 28.9 %collective-permute-start.34 = (bf16[8,48,384]{2,1,0:T(8,128)(2,1)}, bf16[8,48,384]{2,1,0:T(8,128)(2,1)S(1)}, u32[]{:S(2)}, u32[]{:S(2)}) collective-permute-start(bf16[8,48,384]{2,1,0:T(8,128)(2,1)} %get-tuple-element.139), channel_id=1, source_target_pairs={{0,4},{1,5},{2,6},{3,7},{4,0},{5,1},{6,2},{7,3},{8,12},{9,13},{10,... | collective-permute-start | bytes 884744 | tf_op jit(solution)/shard_map/ppermute | solution.py:46
  198.2 29.7 %collective-permute-start.32 = (bf16[4,144,384]{2,1,0:T(8,128)(2,1)S(1)}, bf16[4,144,384]{2,1,0:T(8,128)(2,1)}, u32[]{:S(2)}, u32[]{:S(2)}) collective-permute-start(bf16[4,144,384]{2,1,0:T(8,128)(2,1)S(1)} %get-tuple-element.130), channel_id=1, source_target_pairs={{0,4},{1,5},{2,6},{3,7},{4,0},{5,1},{6,2},{7,3},{8,12},{9,13},{10,... | collective-permute-start | bytes 1327112 | tf_op jit(solution)/shard_map/ppermute | solution.py:46
  201.1 30.1 %collective-permute-start.33 = (bf16[8,48,1152]{2,1,0:T(8,128)(2,1)S(1)}, bf16[8,48,1152]{2,1,0:T(8,128)(2,1)S(1)}, u32[]{:S(2)}, u32[]{:S(2)}) collective-permute-start(bf16[8,48,1152]{2,1,0:T(8,128)(2,1)S(1)} %get-tuple-element.125), channel_id=1, source_target_pairs={{0,2},{1,3},{2,0},{3,1},{4,6},{5,7},{6,4},{7,5},{8,10},{9,11},{10,... | collective-permute-start | bytes 2654216 | tf_op jit(solution)/shard_map/ppermute | solution.py:46
  224.3 25.7 %collective-permute-start.35 = (bf16[16,48,384]{2,1,0:T(8,128)(2,1)}, bf16[16,48,384]{2,1,0:T(8,128)(2,1)S(1)}, u32[]{:S(2)}, u32[]{:S(2)}) collective-permute-start(bf16[16,48,384]{2,1,0:T(8,128)(2,1)} %get-tuple-element.98), channel_id=1, source_target_pairs={{0,1},{1,0},{2,3},{3,2},{4,5},{5,4},{6,7},{7,6},{8,9},{9,8},{10,11... | collective-permute-start | bytes 1769480 | tf_op jit(solution)/shard_map/ppermute | solution.py:46
  226.2 29.4 %collective-permute-start.42 = (bf16[4,48,384]{2,1,0:T(8,128)(2,1)}, bf16[4,48,384]{2,1,0:T(8,128)(2,1)S(1)}, u32[]{:S(2)}, u32[]{:S(2)}) collective-permute-start(bf16[4,48,384]{2,1,0:T(8,128)(2,1)} %get-tuple-element.153), channel_id=1, source_target_pairs={{0,2},{1,3},{2,0},{3,1},{4,6},{5,7},{6,4},{7,5},{8,10},{9,11},{10,... | collective-permute-start | bytes 442376 | tf_op jit(solution)/shard_map/ppermute | solution.py:46
  229.9 21.9 %collective-permute-start.45 = (bf16[144,384]{1,0:T(8,128)(2,1)}, bf16[144,384]{1,0:T(8,128)(2,1)}, u32[]{:S(2)}, u32[]{:S(2)}) collective-permute-start(bf16[144,384]{1,0:T(8,128)(2,1)} %get-tuple-element.159), channel_id=1, source_target_pairs={{0,24},{1,25},{2,26},{3,27},{4,28},{5,29},{6,30},{7,31},{8,16},{9,... | collective-permute-start | bytes 331784 | tf_op jit(solution)/shard_map/ppermute | solution.py:46
  231.1 20.7 %collective-permute-start.44 = (bf16[144,384]{1,0:T(8,128)(2,1)}, bf16[144,384]{1,0:T(8,128)(2,1)S(1)}, u32[]{:S(2)}, u32[]{:S(2)}) collective-permute-start(bf16[144,384]{1,0:T(8,128)(2,1)} %get-tuple-element.160), channel_id=1, source_target_pairs={{0,16},{1,17},{2,18},{3,19},{4,20},{5,21},{6,22},{7,23},{8,24},{9,... | collective-permute-start | bytes 331784 | tf_op jit(solution)/shard_map/ppermute | solution.py:46
  251.3 18.7 %collective-permute-start.37 = (bf16[8,48,768]{2,1,0:T(8,128)(2,1)S(1)}, bf16[8,48,768]{2,1,0:T(8,128)(2,1)S(1)}, u32[]{:S(2)}, u32[]{:S(2)}) collective-permute-start(bf16[8,48,768]{2,1,0:T(8,128)(2,1)S(1)} %pad_maximum_fusion.4), channel_id=1, source_target_pairs={{0,2},{1,3},{2,0},{3,1},{4,6},{5,7},{6,4},{7,5},{8,10},{9,11},{10,... | collective-permute-start | bytes 1769480 | tf_op jit(solution)/shard_map/ppermute | solution.py:46
  251.8 21.5 %collective-permute-start.38 = (bf16[16,48,384]{2,1,0:T(8,128)(2,1)}, bf16[16,48,384]{2,1,0:T(8,128)(2,1)S(1)}, u32[]{:S(2)}, u32[]{:S(2)}) collective-permute-start(bf16[16,48,384]{2,1,0:T(8,128)(2,1)} %get-tuple-element.104), channel_id=1, source_target_pairs={{0,1},{1,0},{2,3},{3,2},{4,5},{5,4},{6,7},{7,6},{8,9},{9,8},{10,11... | collective-permute-start | bytes 1769480 | tf_op jit(solution)/shard_map/ppermute | solution.py:46
  251.8 15.8 %collective-permute-start.41 = (bf16[4,48,1152]{2,1,0:T(8,128)(2,1)}, bf16[4,48,1152]{2,1,0:T(8,128)(2,1)S(1)}, u32[]{:S(2)}, u32[]{:S(2)}) collective-permute-start(bf16[4,48,1152]{2,1,0:T(8,128)(2,1)} %get-tuple-element.127), channel_id=1, source_target_pairs={{0,4},{1,5},{2,6},{3,7},{4,0},{5,1},{6,2},{7,3},{8,12},{9,13},{10,... | collective-permute-start | bytes 1327112 | tf_op jit(solution)/shard_map/ppermute | solution.py:46
  253.4 52.6 %collective-permute-start.55 = (bf16[72,384]{1,0:T(8,128)(2,1)S(1)}, bf16[72,384]{1,0:T(8,128)(2,1)S(1)}, u32[]{:S(2)}, u32[]{:S(2)}) collective-permute-start(bf16[72,384]{1,0:T(8,128)(2,1)S(1)} %select_convert_fusion), channel_id=1, source_target_pairs={{0,2},{1,3},{2,0},{3,1},{4,6},{5,7},{6,4},{7,5},{8,10},{9,11},{10,... | collective-permute-start | bytes 165896 | tf_op jit(solution)/shard_map/ppermute | solution.py:46
  268.4 35.9 %collective-permute-start.53 = (bf16[48,1536]{1,0:T(8,128)(2,1)S(1)}, bf16[48,1536]{1,0:T(8,128)(2,1)S(1)}, u32[]{:S(2)}, u32[]{:S(2)}) collective-permute-start(bf16[48,1536]{1,0:T(8,128)(2,1)S(1)} %get-tuple-element.149), channel_id=1, source_target_pairs={{0,24},{1,25},{2,26},{3,27},{4,28},{5,29},{6,30},{7,31},{8,16},{9,... | collective-permute-start | bytes 442376 | tf_op jit(solution)/shard_map/ppermute | solution.py:46
  269.7 34.7 %collective-permute-start.52 = (bf16[48,1536]{1,0:T(8,128)(2,1)S(1)}, bf16[48,1536]{1,0:T(8,128)(2,1)S(1)}, u32[]{:S(2)}, u32[]{:S(2)}) collective-permute-start(bf16[48,1536]{1,0:T(8,128)(2,1)S(1)} %get-tuple-element.150), channel_id=1, source_target_pairs={{0,16},{1,17},{2,18},{3,19},{4,20},{5,21},{6,22},{7,23},{8,24},{9,... | collective-permute-start | bytes 442376 | tf_op jit(solution)/shard_map/ppermute | solution.py:46
  271.9 14.5 %collective-permute-start.39 = (bf16[4,48,768]{2,1,0:T(8,128)(2,1)S(1)}, bf16[4,48,768]{2,1,0:T(8,128)(2,1)S(1)}, u32[]{:S(2)}, u32[]{:S(2)}) collective-permute-start(bf16[4,48,768]{2,1,0:T(8,128)(2,1)S(1)} %get-tuple-element.134), channel_id=1, source_target_pairs={{0,4},{1,5},{2,6},{3,7},{4,0},{5,1},{6,2},{7,3},{8,12},{9,13},{10,... | collective-permute-start | bytes 884744 | tf_op jit(solution)/shard_map/ppermute | solution.py:46
  274.2 16.8 %collective-permute-start.40 = (bf16[8,48,384]{2,1,0:T(8,128)(2,1)S(1)}, bf16[8,48,384]{2,1,0:T(8,128)(2,1)S(1)}, u32[]{:S(2)}, u32[]{:S(2)}) collective-permute-start(bf16[8,48,384]{2,1,0:T(8,128)(2,1)S(1)} %get-tuple-element.131), channel_id=1, source_target_pairs={{0,4},{1,5},{2,6},{3,7},{4,0},{5,1},{6,2},{7,3},{8,12},{9,13},{10,... | collective-permute-start | bytes 884744 | tf_op jit(solution)/shard_map/ppermute | solution.py:46
  286.3 18.0 %collective-permute-start.51 = (bf16[48,1536]{1,0:T(8,128)(2,1)S(1)}, bf16[48,1536]{1,0:T(8,128)(2,1)S(1)}, u32[]{:S(2)}, u32[]{:S(2)}) collective-permute-start(bf16[48,1536]{1,0:T(8,128)(2,1)S(1)} %get-tuple-element.147), channel_id=1, source_target_pairs={{0,8},{1,9},{2,10},{3,11},{4,12},{5,13},{6,14},{7,15},{8,0},{9,1},... | collective-permute-start | bytes 442376 | tf_op jit(solution)/shard_map/ppermute | solution.py:46
  291.0 21.8 %collective-permute-start.57 = (f32[768]{0:T(1024)S(1)}, f32[768]{0:T(1024)S(1)}, u32[]{:S(2)}, u32[]{:S(2)}) collective-permute-start(f32[768]{0:T(1024)S(1)} %get-tuple-element.119), channel_id=1, source_target_pairs={{0,16},{1,17},{2,18},{3,19},{4,20},{5,21},{6,22},{7,23},{8,24},{9,... | collective-permute-start | bytes 9224 | tf_op jit(solution)/shard_map/ppermute | solution.py:46
  306.0 16.6 %collective-permute-start.54 = (f32[24,1536]{1,0:T(8,128)S(1)}, f32[24,1536]{1,0:T(8,128)S(1)}, u32[]{:S(2)}, u32[]{:S(2)}) collective-permute-start(f32[24,1536]{1,0:T(8,128)S(1)} %get-tuple-element.162), channel_id=1, source_target_pairs={{0,1},{1,0},{2,3},{3,2},{4,5},{5,4},{6,7},{7,6},{8,9},{9,8},{10,11... | collective-permute-start | bytes 442376 | tf_op jit(solution)/shard_map/ppermute | solution.py:46
  306.9 7.7 %collective-permute-start.56 = (f32[36,384]{1,0:T(8,128)S(1)}, f32[36,384]{1,0:T(8,128)S(1)}, u32[]{:S(2)}, u32[]{:S(2)}) collective-permute-start(f32[36,384]{1,0:T(8,128)S(1)} %get-tuple-element.168), channel_id=1, source_target_pairs={{0,1},{1,0},{2,3},{3,2},{4,5},{5,4},{6,7},{7,6},{8,9},{9,8},{10,11... | collective-permute-start | bytes 165896 | tf_op jit(solution)/shard_map/ppermute | solution.py:46
  318.1 10.3 %collective-permute-start.49 = (bf16[48,1152]{1,0:T(8,128)(2,1)S(1)}, bf16[48,1152]{1,0:T(8,128)(2,1)S(1)}, u32[]{:S(2)}, u32[]{:S(2)}) collective-permute-start(bf16[48,1152]{1,0:T(8,128)(2,1)S(1)} %get-tuple-element.156), channel_id=1, source_target_pairs={{0,24},{1,25},{2,26},{3,27},{4,28},{5,29},{6,30},{7,31},{8,16},{9,... | collective-permute-start | bytes 331784 | tf_op jit(solution)/shard_map/ppermute | solution.py:46
  320.5 7.8 %collective-permute-start.48 = (bf16[48,1152]{1,0:T(8,128)(2,1)S(1)}, bf16[48,1152]{1,0:T(8,128)(2,1)S(1)}, u32[]{:S(2)}, u32[]{:S(2)}) collective-permute-start(bf16[48,1152]{1,0:T(8,128)(2,1)S(1)} %get-tuple-element.157), channel_id=1, source_target_pairs={{0,16},{1,17},{2,18},{3,19},{4,20},{5,21},{6,22},{7,23},{8,24},{9,... | collective-permute-start | bytes 331784 | tf_op jit(solution)/shard_map/ppermute | solution.py:46
  (39 other events, 250.2 us)
